TPU v7x, 256 devices: a whole 4x4x8 slice. The times are simulated.
256 devices in a mesh: tok: 64 (over x_lo, z, y), head: 4 (over x_hi, core).
Axes of the slice: x: 4 (x_hi: 2, x_lo: 2; x = x_hi * 2 + x_lo), y: 4, z: 8, core: 2. Of those that a mesh axis runs over, the one named last changes fastest.
Arguments:
- queries: bfloat16 [16384, 24, 128], P('tok', 'head'), may hold values from -4.5 to 4.5
- keys: bfloat16 [16384, 24, 128], P('tok', 'head'), may hold values from -4.5 to 4.5
- values: bfloat16 [16384, 24, 128], P('tok', 'head'), may hold values from -5 to 5
- grad_out: bfloat16 [16384, 3072], P('tok', 'head'), may hold values from -6 to 6
- w_out: bfloat16 [3072, 3072], P('head'), may hold values from -0.109375 to 0.109375
- crit: int32 [64, 40], P('tok'), may hold values from -1 to 1023, as said below
Outputs:
- grad_q: bfloat16 [16384, 24, 128], P('tok', 'head')
- grad_k: bfloat16 [16384, 24, 128], P('tok', 'head')
- grad_v: bfloat16 [16384, 24, 128], P('tok', 'head')
Inputs may be any that keep to these rules, and one draw needn't show every extreme that they name: `crit`: row b lists distinct key tiles, -1 marking unused entries, which come last; no listed tile lies in query block b - 1, b or b + 1 (not counted round); at most 1 tiles of one row lie in one query block, and some row has 1 tiles in one block; row 0 lists a tile of block 63 and row 63 a tile of block 0; some row has no unused entry, and every row uses half of its entries or more.
All inputs are finite; a program needn't handle non-finite values.
Results may differ from a plain program's by a relative error of at most 0.022.
Values may be sent and summed in bfloat16 or wider, within the bound.
No kernel may reach another device: no remote copies, remote signals or barrier semaphores. Data moves between devices by JAX's collectives and lax.ppermute only.
A program may use at most 128 MiB of HBM per device.

v0:
```python
import jax
import jax.numpy as jnp
from jax import lax
from jax.sharding import PartitionSpec as P

KT = 16


def padded(cells, sides, width):
    for axis, dim in sides:
        count = lax.axis_size(axis)
        ends = count - 1
        head = lax.slice_in_dim(cells, 0, width, axis=dim)
        tail = lax.slice_in_dim(cells, cells.shape[dim] - width, cells.shape[dim], axis=dim)
        cells = jnp.concatenate(
            [
                lax.ppermute(tail, axis, [(i, (i + 1) % count) for i in range(ends)]),
                cells,
                lax.ppermute(head, axis, [((i + 1) % count, i) for i in range(ends)]),
            ],
            axis=dim,
        )
    return cells


def shifted(value, axis, steps):
    count = lax.axis_size(axis)
    leading, last = (max(0, -steps), min(count, count - steps))
    return lax.ppermute(value, axis, [(source, source + steps) for source in range(leading, last)])


def shards(queries, keys, values, grad_out, w_out, crit):
    tok_rows, heads_here, head_dim = queries.shape
    width_here = heads_here * head_dim
    count = lax.axis_size("tok")
    place = lax.axis_index("tok")
    tiles_here = tok_rows // KT
    ncrit = crit.shape[1]
    capacity = (ncrit + count - 4) // (count - 3)
    slots = count * capacity
    row_len = KT * width_here
    d_attn = lax.dot_general(
        lax.all_gather(grad_out, "head", axis=1, tiled=True),
        w_out,
        (((1,), (1,)), ((), ())),
        preferred_element_type=jnp.float32,
    )
    d_attn = d_attn.astype(jnp.bfloat16).reshape(tok_rows, heads_here, head_dim)
    tiles = crit[0]
    used = tiles >= 0
    owner = jnp.where(used, tiles // tiles_here, -1)
    local_tile = jnp.where(used, tiles % tiles_here, 0)
    order = jnp.arange(ncrit)
    earlier = (owner[:, None] == owner[None, :]) & (order[:, None] > order[None, :]) & used[None, :]
    slot = jnp.sum(earlier.astype(jnp.int32), axis=1)
    position = jnp.where(used, owner * capacity + slot, 0)
    slot_ids = jnp.arange(slots)
    chosen = used[:, None] & (position[:, None] == slot_ids[None, :])
    request = jnp.sum(jnp.where(chosen, local_tile[:, None] + 1, 0), axis=0) - 1
    has_left = place > 0
    has_right = place < count - 1
    asked = lax.all_to_all(
        request.reshape(count, capacity), "tok", split_axis=0, concat_axis=0, tiled=True
    ).reshape(slots)
    pair = jnp.stack([keys, values])
    pair_tiles = pair.reshape(2, tiles_here, KT, heads_here, head_dim)
    served = jnp.take(pair_tiles, jnp.clip(asked, 0, tiles_here - 1), axis=1)
    served = jnp.where((asked >= 0)[None, :, None, None, None], served, jnp.zeros((), jnp.bfloat16))
    fetched = lax.all_to_all(
        served.reshape(2, count, capacity, KT, heads_here, head_dim),
        "tok",
        split_axis=1,
        concat_axis=1,
        tiled=True,
    )
    fetched = fetched.reshape(2, slots, KT, heads_here, head_dim)
    far_pair = jnp.take(fetched, position, axis=1).reshape(2, ncrit * KT, heads_here, head_dim)
    window = padded(pair, (("tok", 1),), KT)
    key_pair = jnp.concatenate([window, far_pair], axis=1)
    valid = jnp.concatenate(
        [
            jnp.broadcast_to(has_left, (KT,)),
            jnp.ones((tok_rows,), bool),
            jnp.broadcast_to(has_right, (KT,)),
            jnp.repeat(used, KT),
        ]
    )
    scale = head_dim ** (-0.5)
    key_all = key_pair[0]
    value_all = key_pair[1]
    scores = (
        jnp.einsum("qhd,khd->hqk", queries, key_all, preferred_element_type=jnp.float32) * scale
    )
    scores = jnp.where(valid[None, None, :], scores, -1e30)
    top = jnp.max(scores, axis=-1, keepdims=True)
    probs = jnp.exp(scores - top)
    probs = probs / jnp.sum(probs, axis=-1, keepdims=True)
    probs_b = probs.astype(jnp.bfloat16)
    dprob = jnp.einsum("qhd,khd->hqk", d_attn, value_all, preferred_element_type=jnp.float32)
    delta = jnp.sum(probs * dprob, axis=-1, keepdims=True)
    dscore = (probs * (dprob - delta) * scale).astype(jnp.bfloat16)
    grad_q = jnp.einsum("hqk,khd->qhd", dscore, key_all, preferred_element_type=jnp.float32).astype(
        jnp.bfloat16
    )
    part_k = jnp.einsum("hqk,qhd->khd", dscore, queries, preferred_element_type=jnp.float32)
    part_v = jnp.einsum("hqk,qhd->khd", probs_b, d_attn, preferred_element_type=jnp.float32)
    grads = jnp.stack([part_k, part_v]) * valid.astype(jnp.float32)[None, :, None, None]
    left_part = grads[:, :KT]
    own_part = grads[:, KT : KT + tok_rows]
    right_part = grads[:, KT + tok_rows : 2 * KT + tok_rows]
    far_part = grads[:, 2 * KT + tok_rows :].reshape(2, ncrit, row_len)
    slotted = jnp.einsum(
        "cs,ecr->esr", chosen.astype(jnp.float32), far_part, precision=lax.Precision.HIGHEST
    )
    returned = lax.all_to_all(
        slotted.reshape(2, count, capacity, row_len).astype(jnp.bfloat16),
        "tok",
        split_axis=1,
        concat_axis=1,
        tiled=True,
    ).astype(jnp.float32)
    returned = returned.reshape(2, slots, row_len)
    owned = (asked[None, :] == jnp.arange(tiles_here)[:, None]).astype(jnp.float32)
    added = jnp.einsum("ts,esr->etr", owned, returned, precision=lax.Precision.HIGHEST)
    total = own_part + added.reshape(2, tok_rows, heads_here, head_dim)
    from_next = shifted(left_part.astype(jnp.bfloat16), "tok", -1).astype(left_part.dtype)
    from_prev = shifted(right_part.astype(jnp.bfloat16), "tok", 1).astype(right_part.dtype)
    total = total + jnp.pad(from_next, ((0, 0), (tok_rows - KT, 0), (0, 0), (0, 0)))
    total = total + jnp.pad(from_prev, ((0, 0), (0, tok_rows - KT), (0, 0), (0, 0)))
    return (grad_q, total[0].astype(jnp.bfloat16), total[1].astype(jnp.bfloat16))


def solution(mesh):
    return jax.shard_map(
        shards,
        mesh=mesh,
        in_specs=(
            P("tok", "head", None),
            P("tok", "head", None),
            P("tok", "head", None),
            P("tok", "head"),
            P("head", None),
            P("tok", None),
        ),
        out_specs=(P("tok", "head", None), P("tok", "head", None), P("tok", "head", None)),
        check_vma=False,
    )
```

profile of v0, /device:TPU:32, one launch (start us, length us, event | category | flops | bytes accessed | tf_op | source)
XLA Modules:
  0.0 267.8 jit_solution(12728092891525378253)
XLA Ops:
  7.2 0.0 copy-start
  7.2 0.7 compare_bitcast_fusion
  7.9 0.7 fusion.55
  8.6 0.7 fusion.60
  9.2 0.2 convert_reduce_fusion
  9.4 0.5 copy-done.10
  9.9 1.2 compare_and_fusion.1
  11.1 0.1 select_reduce_fusion
  11.2 0.7 copy.65
  11.9 12.7 %all-to-all-start = ((s32[64,1,1]{2,1,0:T(1,128)}), s32[64,1,1]{2,1,0:T(1,128)S(1)}, u32[]{:S(2)}, u32[]{:S(2)}) async-start(s32[64,1,1]{2,1,0:T(1,128)} %copy.65), calls=%async_computation | async-start | bytes 65536 | tf_op jit(solution)/shard_map/all_to_all | solution.py:62
  24.6 1.2 pad_maximum_fusion.1
  25.8 0.1 copy.81
  26.0 8.3 %all-to-all-done = s32[64,1,1]{2,1,0:T(1,128)S(1)} async-done(((s32[64,1,1]{2,1,0:T(1,128)}), s32[64,1,1]{2,1,0:T(1,128)S(1)}, u32[]{:S(2)}, u32[]{:S(2)}) %all-to-all-start) | async-done | bytes 288 | tf_op jit(solution)/shard_map/all_to_all | solution.py:62
  34.2 2.4 fusion.68
  36.6 2.6 gather_fusion
  39.2 4.0 %fusion.11 = bf16[2,64,1,16,6,128]{5,3,4,0,2,1:T(8,128)(2,1)} fusion(bf16[64,2,16,6,128]{4,2,3,1,0:T(8,128)(2,1)} %gather_fusion, pred[64]{0:T(512)(128)(4,1)S(1)} %get-tuple-element.39, pred[64]{0:T(512)(128)(4,1)S(1)} %get-tuple-element.38), kind=kLoop, calls=%fused_computation.18 | loop fusion | flops 3145728 | bytes 6291584 | tf_op jit(solution)/shard_map/jit(_where)/select_n | solution.py:68
  43.2 5.5 %all-to-all-start.1 = ((bf16[2,64,1,16,6,128]{5,3,4,0,2,1:T(8,128)(2,1)}), bf16[2,64,1,16,6,128]{5,3,4,0,2,1:T(8,128)(2,1)S(1)}, u32[]{:S(2)}, u32[]{:S(2)}) async-start(bf16[2,64,1,16,6,128]{5,3,4,0,2,1:T(8,128)(2,1)} %fusion.11), calls=%async_computation.1 | async-start | bytes 6291456 | tf_op jit(solution)/shard_map/all_to_all | solution.py:69
  48.7 0.0 all-gather.2.cloned.1.call-start
  48.8 0.7 all-gather.2.cloned.1.call-update
  49.5 1.4 pad_maximum_fusion.3
  50.9 3.4 %collective-permute-start = (bf16[2,16,6,128]{3,1,2,0:T(8,128)(2,1)}, bf16[2,16,6,128]{3,1,2,0:T(8,128)(2,1)}, u32[]{:S(2)}, u32[]{:S(2)}) collective-permute-start(bf16[2,16,6,128]{3,1,2,0:T(8,128)(2,1)} %get-tuple-element.34), channel_id=1, source_target_pairs={{0,4},{4,8},{8,12},{12,16},{16,20},{20,24},{24,28},{28,32},{32,36}... | collective-permute-start | bytes 147464 | tf_op jit(solution)/shard_map/ppermute | solution.py:17
  54.3 4.6 %collective-permute-start.1 = (bf16[2,16,6,128]{3,1,2,0:T(8,128)(2,1)}, bf16[2,16,6,128]{3,1,2,0:T(8,128)(2,1)}, u32[]{:S(2)}, u32[]{:S(2)}) collective-permute-start(bf16[2,16,6,128]{3,1,2,0:T(8,128)(2,1)} %get-tuple-element.35), channel_id=1, source_target_pairs={{4,0},{8,4},{12,8},{16,12},{20,16},{24,20},{28,24},{32,28},{36,32}... | collective-permute-start | bytes 147464 | tf_op jit(solution)/shard_map/ppermute | solution.py:19
  58.9 0.7 broadcast_in_dim.92
  59.6 0.7 broadcast_in_dim.93
  60.3 0.1 broadcast_in_dim.105
  60.4 0.7 reshape.285
  61.0 0.7 fusion.58
  61.8 1.3 fusion.67
  63.1 26.0 %all-gather.2.cloned.1.call-done = bf16[256,3072]{1,0:T(8,128)(2,1)} async-done(((bf16[256,768]{1,0:T(8,128)(2,1)}), bf16[256,3072]{1,0:T(8,128)(2,1)}) %all-gather.2.cloned.1.call-update) | async-done | bytes 1572880 | tf_op jit(solution)/shard_map/all_gather | solution.py:43
  89.1 5.0 %convolution_convert_fusion.1 = bf16[256,768]{1,0:T(8,128)(2,1)} fusion(bf16[256,3072]{1,0:T(8,128)(2,1)} %all-gather.2.cloned.1.call-done, bf16[768,3072]{1,0:T(8,128)(2,1)} %param.10), kind=kOutput, calls=%fused_computation.44 | convolution fusion | flops 1208156160 | bytes 6684672 | tf_op jit(solution)/shard_map/dot_general | solution.py:42
  94.0 1.9 copy.71
  96.0 24.4 %all-to-all-done.1 = bf16[2,64,1,16,6,128]{5,3,4,0,2,1:T(8,128)(2,1)S(1)} async-done(((bf16[2,64,1,16,6,128]{5,3,4,0,2,1:T(8,128)(2,1)}), bf16[2,64,1,16,6,128]{5,3,4,0,2,1:T(8,128)(2,1)S(1)}, u32[]{:S(2)}, u32[]{:S(2)}) %all-to-all-start.1) | async-done | bytes 3145760 | tf_op jit(solution)/shard_map/all_to_all | solution.py:69
  120.4 2.2 copy.88
  122.6 2.8 %gather_fusion.1 = bf16[40,2,16,6,128]{4,2,3,1,0:T(8,128)(2,1)S(1)} fusion(bf16[2,64,16,6,128]{4,2,3,1,0:T(8,128)(2,1)} %bitcast.131, s32[1024]{0:T(1024)S(1)} %pad_clamp_fusion), kind=kCustom, calls=%fused_computation.1 | custom fusion | bytes 3932320 | tf_op jit(solution)/shard_map/jit(_take)/gather | solution.py:77
  125.4 0.0 copy-start.5
  125.4 0.5 copy.70
  125.9 0.4 bitcast_select_fusion.1
  126.4 0.0 copy-done.4
  126.4 0.1 copy-done.5
  126.5 1.1 pad_maximum_fusion
  127.6 3.4 %fusion.36 = f32[6,256,928]{1,2,0:T(8,128)} fusion(bf16[256,6,128]{0,2,1:T(8,128)(2,1)S(1)} %bitcast.138, bf16[2,928,6,128]{3,1,2,0:T(8,128)(2,1)S(1)} %pad_maximum_fusion), kind=kOutput, calls=%fused_computation.41 | convolution fusion | flops 364904448 | bytes 7520256 | tf_op jit(solution)/shard_map/qhd,khd->hqk/dot_general | solution.py:99
  131.0 0.9 fusion.37
  132.0 1.9 fusion.71
  133.9 2.4 copy-done.12
  136.3 0.9 fusion.27
  137.2 10.8 %fusion.30 = f32[1,928,6,128]{3,1,2,0:T(8,128)} fusion(bf16[256,6,128]{2,0,1:T(8,128)(2,1)S(1)} %copy-done, f32[6,256,928]{1,2,0:T(8,128)} %fusion.36, f32[6,256,928]{1,2,0:T(8,128)} %copy-done.12, f32[6,256]{1,0:T(8,128)S(1)} %get-tuple-element.43), kind=kOutput, calls=%fused_computation.35 | convolution fusion | flops 374884768 | bytes 14653440 | tf_op jit(solution)/shard_map/hqk,qhd->khd/dot_general | solution.py:105
  148.0 4.3 %fusion.69 = (bf16[2,928,6,128]{3,1,2,0:T(8,128)(2,1)}, f32[2,928,6,128]{3,1,2,0:T(8,128)S(1)}) fusion(f32[928]{0:T(1024)S(1)} %get-tuple-element.36, f32[1,928,6,128]{3,1,2,0:T(8,128)S(1)} %fusion.27, f32[1,928,6,128]{3,1,2,0:T(8,128)} %fusion.30), kind=kLoop, calls=%fused_computation.113 | loop fusion | flops 4276224 | bytes 14257792 | tf_op jit(solution)/shard_map/convert.7
  152.3 0.3 slice.51
  152.6 2.2 copy-done.2
  154.8 4.7 %copy.74 = f32[2,640,6,128]{3,2,1,0:T(8,128)} copy(f32[2,640,6,128]{3,1,2,0:T(8,128)S(1)} %slice.51) | data formatting | bytes 7864320 | tf_op jit(solution)/shard_map/slice | solution.py:111
  159.5 5.6 %reshape.287 = f32[2,40,12288]{2,1,0:T(8,128)} reshape(f32[2,640,6,128]{3,2,1,0:T(8,128)} %copy.74) | data formatting | bytes 7864320 | tf_op jit(solution)/shard_map/reshape | solution.py:111
  165.1 5.0 %fusion.2 = bf16[2,64,1,12288]{3,1,0,2:T(8,128)(2,1)S(1)} fusion(f32[2,40,12288]{2,1,0:T(8,128)} %reshape.287, s32[40]{0:T(128)S(1)} %get-tuple-element.29, pred[40]{0:T(512)(128)(4,1)S(1)} %get-tuple-element.40), kind=kOutput, calls=%fused_computation.5 | convolution fusion | flops 756552704 | bytes 7078088 | tf_op jit(solution)/shard_map/cs,ecr->esr/dot_general | solution.py:112
  170.1 4.9 %copy.75 = bf16[2,64,1,12288]{3,0,2,1:T(2,128)(2,1)} copy(bf16[2,64,1,12288]{3,1,0,2:T(8,128)(2,1)S(1)} %fusion.2) | data formatting | bytes 6291456 | tf_op jit(solution)/shard_map/convert_element_type | solution.py:116
  175.0 7.0 %all-to-all-start.2 = ((bf16[2,64,1,12288]{3,0,2,1:T(2,128)(2,1)}), bf16[2,64,1,12288]{3,0,2,1:T(2,128)(2,1)S(1)}, u32[]{:S(2)}, u32[]{:S(2)}) async-start(bf16[2,64,1,12288]{3,0,2,1:T(2,128)(2,1)} %copy.75), calls=%async_computation.2 | async-start | bytes 6291456 | tf_op jit(solution)/shard_map/all_to_all | solution.py:115
  182.0 10.0 %fusion.41 = bf16[256,6,128]{0,2,1:T(8,128)(2,1)S(1)} fusion(f32[6,256,928]{1,2,0:T(8,128)} %fusion.36, bf16[2,928,6,128]{3,1,2,0:T(8,128)(2,1)} %copy-done.3, f32[6,256,928]{1,2,0:T(8,128)} %copy-done.12, f32[6,256]{1,0:T(8,128)S(1)} %copy-done.14), kind=kOutput, calls=%fused_computation.46 | convolution fusion | flops 375081376 | bytes 24641536 | tf_op jit(solution)/shard_map/hqk,khd->qhd/dot_general | solution.py:102
  192.0 0.9 copy.78
  192.9 1.5 fusion.70
  194.4 4.6 %collective-permute-start.2 = (bf16[2,16,6,128]{3,1,2,0:T(8,128)(2,1)}, bf16[2,16,6,128]{3,1,2,0:T(8,128)(2,1)}, u32[]{:S(2)}, u32[]{:S(2)}) collective-permute-start(bf16[2,16,6,128]{3,1,2,0:T(8,128)(2,1)} %get-tuple-element.30), channel_id=1, source_target_pairs={{4,0},{8,4},{12,8},{16,12},{20,16},{24,20},{28,24},{32,28},{36,32}... | collective-permute-start | bytes 147464 | tf_op jit(solution)/shard_map/ppermute | solution.py:29
  198.9 1.9 collective-permute-start.3
  200.9 52.2 %all-to-all-done.2 = bf16[2,64,1,12288]{3,0,2,1:T(2,128)(2,1)S(1)} async-done(((bf16[2,64,1,12288]{3,0,2,1:T(2,128)(2,1)}), bf16[2,64,1,12288]{3,0,2,1:T(2,128)(2,1)S(1)}, u32[]{:S(2)}, u32[]{:S(2)}) %all-to-all-start.2) | async-done | bytes 3145760 | tf_op jit(solution)/shard_map/all_to_all | solution.py:115
  253.0 3.0 %convolution_bitcast_fusion = f32[2,16,12288]{2,1,0:T(8,128)} fusion(bf16[2,64,1,12288]{3,0,2,1:T(2,128)(2,1)S(1)} %all-to-all-done.2, s32[64]{0:T(128)S(1)} %copy-done.9), kind=kOutput, calls=%fused_computation.6 | convolution fusion | flops 50332672 | bytes 4718848 | tf_op jit(solution)/shard_map/ts,esr->etr/dot_general | solution.py:124
  256.0 2.2 reshape.289
  258.2 1.8 fusion.35
  260.0 0.9 slice_bitcast_fusion.9
  (35 shorter events, 0.1 us)
Async XLA Ops:
  7.2 123.9 %copy-start = (bf16[256,6,128]{2,0,1:T(8,128)(2,1)S(1)}, bf16[256,6,128]{2,0,1:T(8,128)(2,1)}, u32[]{:S(2)}) copy-start(bf16[256,6,128]{2,0,1:T(8,128)(2,1)} %param.6) | copy-start | bytes 1179652
  9.4 0.5 copy-start.10
  11.9 22.3 %all-to-all-start = ((s32[64,1,1]{2,1,0:T(1,128)}), s32[64,1,1]{2,1,0:T(1,128)S(1)}, u32[]{:S(2)}, u32[]{:S(2)}) async-start(s32[64,1,1]{2,1,0:T(1,128)} %copy.65), calls=%async_computation | async-start | bytes 65536 | tf_op jit(solution)/shard_map/all_to_all | solution.py:62
  36.6 2.6 copy-start.8
  43.2 77.2 %all-to-all-start.1 = ((bf16[2,64,1,16,6,128]{5,3,4,0,2,1:T(8,128)(2,1)}), bf16[2,64,1,16,6,128]{5,3,4,0,2,1:T(8,128)(2,1)S(1)}, u32[]{:S(2)}, u32[]{:S(2)}) async-start(bf16[2,64,1,16,6,128]{5,3,4,0,2,1:T(8,128)(2,1)} %fusion.11), calls=%async_computation.1 | async-start | bytes 6291456 | tf_op jit(solution)/shard_map/all_to_all | solution.py:69
  48.7 40.3 %all-gather.2.cloned.1.call-start = ((), (), s32[]{:S(2)}) async-start(), calls=%async_computation.3 | async-start | bytes 1966080 | tf_op jit(solution)/shard_map/all_gather | solution.py:43
  50.9 75.4 %collective-permute-start = (bf16[2,16,6,128]{3,1,2,0:T(8,128)(2,1)}, bf16[2,16,6,128]{3,1,2,0:T(8,128)(2,1)}, u32[]{:S(2)}, u32[]{:S(2)}) collective-permute-start(bf16[2,16,6,128]{3,1,2,0:T(8,128)(2,1)} %get-tuple-element.34), channel_id=1, source_target_pairs={{0,4},{4,8},{8,12},{12,16},{16,20},{20,24},{24,28},{28,32},{32,36}... | collective-permute-start | bytes 147464 | tf_op jit(solution)/shard_map/ppermute | solution.py:17
  54.3 72.1 %collective-permute-start.1 = (bf16[2,16,6,128]{3,1,2,0:T(8,128)(2,1)}, bf16[2,16,6,128]{3,1,2,0:T(8,128)(2,1)}, u32[]{:S(2)}, u32[]{:S(2)}) collective-permute-start(bf16[2,16,6,128]{3,1,2,0:T(8,128)(2,1)} %get-tuple-element.35), channel_id=1, source_target_pairs={{4,0},{8,4},{12,8},{16,12},{20,16},{24,20},{28,24},{32,28},{36,32}... | collective-permute-start | bytes 147464 | tf_op jit(solution)/shard_map/ppermute | solution.py:19
  122.6 3.3 %copy-start.7 = (pred[640]{0:T(1024)(128)(4,1)S(1)}, pred[640]{0:T(1024)(128)(4,1)}, u32[]{:S(2)}) copy-start(pred[640]{0:T(1024)(128)(4,1)} %broadcast_in_dim.93) | copy-start | bytes 1924
  125.4 1.0 copy-start.4
  125.4 1.1 copy-start.5
  125.9 1.7 copy-start.6
  127.6 4.4 %copy-start.3 = (bf16[2,928,6,128]{3,1,2,0:T(8,128)(2,1)}, bf16[2,928,6,128]{3,1,2,0:T(8,128)(2,1)S(1)}, u32[]{:S(2)}) copy-start(bf16[2,928,6,128]{3,1,2,0:T(8,128)(2,1)S(1)} %pad_maximum_fusion) | copy-start | bytes 8552452
  131.0 0.9 copy-start.11
  133.9 2.4 copy-start.12
  133.9 3.3 %copy-start.13 = (f32[6,256]{1,0:T(8,128)}, f32[6,256]{1,0:T(8,128)S(1)}, u32[]{:S(2)}) copy-start(f32[6,256]{1,0:T(8,128)S(1)} %get-tuple-element.43) | copy-start | bytes 18436
  152.3 2.5 copy-start.2
  175.0 7.0 %copy-start.14 = (f32[6,256]{1,0:T(8,128)S(1)}, f32[6,256]{1,0:T(8,128)}, u32[]{:S(2)}) copy-start(f32[6,256]{1,0:T(8,128)} %copy-done.13) | copy-start | bytes 18436
  175.0 78.0 %all-to-all-start.2 = ((bf16[2,64,1,12288]{3,0,2,1:T(2,128)(2,1)}), bf16[2,64,1,12288]{3,0,2,1:T(2,128)(2,1)S(1)}, u32[]{:S(2)}, u32[]{:S(2)}) async-start(bf16[2,64,1,12288]{3,0,2,1:T(2,128)(2,1)} %copy.75), calls=%async_computation.2 | async-start | bytes 6291456 | tf_op jit(solution)/shard_map/all_to_all | solution.py:115
  182.0 71.0 %copy-start.9 = (s32[64]{0:T(128)S(1)}, s32[64]{0:T(128)}, u32[]{:S(2)}) copy-start(s32[64]{0:T(128)} %copy-done.8) | copy-start | bytes 772
  194.4 63.8 %collective-permute-start.2 = (bf16[2,16,6,128]{3,1,2,0:T(8,128)(2,1)}, bf16[2,16,6,128]{3,1,2,0:T(8,128)(2,1)}, u32[]{:S(2)}, u32[]{:S(2)}) collective-permute-start(bf16[2,16,6,128]{3,1,2,0:T(8,128)(2,1)} %get-tuple-element.30), channel_id=1, source_target_pairs={{4,0},{8,4},{12,8},{16,12},{20,16},{24,20},{28,24},{32,28},{36,32}... | collective-permute-start | bytes 147464 | tf_op jit(solution)/shard_map/ppermute | solution.py:29
  198.9 59.3 %collective-permute-start.3 = (bf16[2,16,6,128]{3,1,2,0:T(8,128)(2,1)}, bf16[2,16,6,128]{3,1,2,0:T(8,128)(2,1)}, u32[]{:S(2)}, u32[]{:S(2)}) collective-permute-start(bf16[2,16,6,128]{3,1,2,0:T(8,128)(2,1)} %get-tuple-element.31), channel_id=1, source_target_pairs={{0,4},{4,8},{8,12},{12,16},{16,20},{20,24},{24,28},{28,32},{32,36}... | collective-permute-start | bytes 147464 | tf_op jit(solution)/shard_map/ppermute | solution.py:29
  256.0 4.9 %copy-start.1 = (bf16[256,6,128]{2,0,1:T(8,128)(2,1)S(1)}, bf16[256,6,128]{2,0,1:T(8,128)(2,1)}, u32[]{:S(2)}) copy-start(bf16[256,6,128]{2,0,1:T(8,128)(2,1)} %param.6) | copy-start | bytes 1179652
Sparse Core Ops, SparseCore 0:
  51.4 37.6 all-gather.1
where the time goes:
time: 270 us; the launch traced here: 268 us
  waiting for transfers between devices  112 us (41%)
  starting transfers between devices  39.7 us (15%)
  local copies, waits for them, and re-layouts  39.3 us (15%)
  matrix products  38.9 us (14%)
  other arithmetic  24 us (9%)
  between operations  14.4 us (5%)
    all_to_all x1, waiting for transfers between devices, shards(): lax.all_to_all(slotted.reshape(2, count, capacity, row_len).astype(jnp.bf...  52.2 us
    all_gather x1, waiting for transfers between devices, shards(): lax.all_gather(grad_out, 'head', axis=1, tiled=True)  26 us
    all_to_all x1, waiting for transfers between devices, shards(): lax.all_to_all(served.reshape(2, count, capacity, KT, heads_here, head_di...  24.4 us
    all_to_all x1, starting transfers between devices, shards(): lax.all_to_all(request.reshape(count, capacity), 'tok', split_axis=0, con...  12.7 us
    dot_general x1, matrix products, shards(): jnp.einsum('hqk,qhd->khd', dscore, queries, preferred_element_type=jnp.fl...  10.8 us
    dot_general x1, matrix products, shards(): jnp.einsum('hqk,khd->qhd', dscore, key_all, preferred_element_type=jnp.fl...  9.97 us
    all_to_all x1, waiting for transfers between devices, shards(): lax.all_to_all(request.reshape(count, capacity), 'tok', split_axis=0, con...  8.25 us
    all_to_all x1, starting transfers between devices, shards(): lax.all_to_all(slotted.reshape(2, count, capacity, row_len).astype(jnp.bf...  6.97 us
  transfers between devices with their start and end apart: 8, of which 4 were waited for; matrix products, arithmetic and copies ran while one was open for 14% of the time, Pallas kernels for 0%

commit v1 on v0

v1 whole, which is shorter than its diff:
```python
import functools
import math

import jax
import jax.numpy as jnp
from jax import lax
from jax.experimental import pallas as pl
from jax.experimental.pallas import tpu as pltpu
from jax.sharding import Mesh
from jax.sharding import PartitionSpec as P

KT = 16
HD = 128
TOK = ("x_lo", "z", "y")
PLANE = ("x_lo", "y")
HEAD = ("x_hi", "core")
VMEM_LIMIT = 48 * 1024 * 1024
PARTS = ((0, 3, False), (3, 6, False))


def serve_kernel(asked_ref, pair_ref, out_ref):
    step = pl.program_id(0)
    block, sources = out_ref.shape[0], pair_ref.shape[0]
    for i in range(block):
        tile = jnp.maximum(asked_ref[step * block + i], 0)
        rows = pl.ds(pl.multiple_of(tile * KT, KT), KT)
        for kind in range(2):
            out_ref[i, kind] = pair_ref[i % sources, kind, rows, :]


def serve(asked, pair, block):
    count = asked.shape[0]
    width = pair.shape[-1]
    return pl.pallas_call(
        serve_kernel,
        out_shape=jax.ShapeDtypeStruct((count, 2, KT, width), pair.dtype),
        grid_spec=pltpu.PrefetchScalarGridSpec(
            num_scalar_prefetch=1,
            grid=(count // block,),
            in_specs=[pl.BlockSpec(pair.shape, lambda i, a: (0, 0, 0, 0))],
            out_specs=pl.BlockSpec((block, 2, KT, width), lambda i, a: (i, 0, 0, 0)),
        ),
        compiler_params=pltpu.CompilerParams(vmem_limit_bytes=VMEM_LIMIT),
    )(asked, pair)


def attend_kernel(
    tiles, src_ref, dst_ref, num_ref, q_ref, do_ref, kv_ref, far_ref, dq_ref, own_ref, out_ref, k_all, v_all
):
    rows = q_ref.shape[0]
    total = rows + tiles * KT
    scale = HD**-0.5
    k_all[:rows] = kv_ref[0]
    v_all[:rows] = kv_ref[1]
    for j in range(tiles):
        slot = src_ref[j]
        at = rows + j * KT
        k_all[at : at + KT] = far_ref[slot, 0]
        v_all[at : at + KT] = far_ref[slot, 1]
    q = q_ref[...]
    do = do_ref[...]
    scores = lax.dot_general(
        k_all[...], q, (((1,), (1,)), ((), ())), preferred_element_type=jnp.float32
    )
    row = lax.broadcasted_iota(jnp.int32, (total, rows), 0)
    scores = jnp.where(row < rows + num_ref[0] * KT, scores, -1e30)
    top = jnp.max(scores, axis=0, keepdims=True)
    weight = jnp.exp2((scores - top) * (scale * math.log2(math.e)))
    probs = weight * (1.0 / jnp.sum(weight, axis=0, keepdims=True))
    dprob = lax.dot_general(
        v_all[...], do, (((1,), (1,)), ((), ())), preferred_element_type=jnp.float32
    )
    delta = jnp.sum(probs * dprob, axis=0, keepdims=True)
    dscore = (probs * (dprob - delta) * scale).astype(jnp.bfloat16)
    probs_b = probs.astype(jnp.bfloat16)
    dq_ref[...] = lax.dot_general(
        dscore, k_all[...], (((0,), (0,)), ((), ())), preferred_element_type=jnp.float32
    ).astype(jnp.bfloat16)
    for kind, (left, right) in enumerate(((dscore, q), (probs_b, do))):
        part = jnp.dot(left, right, preferred_element_type=jnp.float32)
        own_ref[kind] = part[:rows]
        far = part[rows:].astype(jnp.bfloat16)
        for j in range(tiles):
            out_ref[dst_ref[j], kind] = far[j * KT : (j + 1) * KT]


def attend(src, dst, num, q, do, kv, far, first, heads):
    rows = q.shape[0]
    tiles = src.shape[0]
    slots = far.shape[0]
    total = rows + tiles * KT
    whole = lambda h, *_: (0, first + h)
    return pl.pallas_call(
        functools.partial(attend_kernel, tiles),
        out_shape=(
            jax.ShapeDtypeStruct((rows, heads * HD), jnp.bfloat16),
            jax.ShapeDtypeStruct((2, rows, heads * HD), jnp.float32),
            jax.ShapeDtypeStruct((slots, 2, KT, heads * HD), jnp.bfloat16),
        ),
        grid_spec=pltpu.PrefetchScalarGridSpec(
            num_scalar_prefetch=3,
            grid=(heads,),
            in_specs=[
                pl.BlockSpec((rows, HD), whole),
                pl.BlockSpec((rows, HD), whole),
                pl.BlockSpec((2, rows, HD), lambda h, *_: (0, 0, first + h)),
                pl.BlockSpec((slots, 2, KT, HD), lambda h, *_: (0, 0, 0, h)),
            ],
            out_specs=(
                pl.BlockSpec((rows, HD), lambda h, *_: (0, h)),
                pl.BlockSpec((2, rows, HD), lambda h, *_: (0, 0, h)),
                pl.BlockSpec((slots, 2, KT, HD), lambda h, *_: (0, 0, 0, h)),
            ),
            scratch_shapes=[
                pltpu.VMEM((total, HD), jnp.bfloat16),
                pltpu.VMEM((total, HD), jnp.bfloat16),
            ],
        ),
        compiler_params=pltpu.CompilerParams(vmem_limit_bytes=VMEM_LIMIT),
    )(src, dst, num, q, do, kv, far)


def settle_kernel(asked_ref, own_ref, back_ref, out_ref, acc):
    rows = own_ref.shape[1]
    acc[:, :rows] = own_ref[...]
    for s in range(back_ref.shape[0]):
        asked = asked_ref[s]
        tile = jnp.where(asked >= 0, asked, rows // KT)
        at = pl.ds(pl.multiple_of(tile * KT, KT), KT)
        for kind in range(2):
            acc[kind, at] += back_ref[s, kind].astype(jnp.float32)
    out_ref[...] = acc[:, :rows].astype(jnp.bfloat16)


def settle(asked, own, back):
    _, rows, width = own.shape
    slots = back.shape[0]
    return pl.pallas_call(
        settle_kernel,
        out_shape=jax.ShapeDtypeStruct((2, rows, width), jnp.bfloat16),
        grid_spec=pltpu.PrefetchScalarGridSpec(
            num_scalar_prefetch=1,
            grid=(width // HD,),
            in_specs=[
                pl.BlockSpec((2, rows, HD), lambda h, *_: (0, 0, h)),
                pl.BlockSpec((slots, 2, KT, HD), lambda h, *_: (0, 0, 0, h)),
            ],
            out_specs=pl.BlockSpec((2, rows, HD), lambda h, *_: (0, 0, h)),
            scratch_shapes=[pltpu.VMEM((2, rows + KT, HD), jnp.float32)],
        ),
        compiler_params=pltpu.CompilerParams(vmem_limit_bytes=VMEM_LIMIT),
    )(asked, own, back)


def shards(queries, keys, values, grad_out, w_out, crit):
    rows, heads, _ = queries.shape
    tiles_here = rows // KT
    sizes = tuple(lax.axis_size(a) for a in TOK)
    nx, nz, ny = sizes
    count = nx * nz * ny
    place = lax.axis_index(TOK)
    z = lax.axis_index("z")
    entries = jnp.concatenate([crit[0], jnp.stack([place * tiles_here - 1, (place + 1) * tiles_here])])
    used = (entries >= 0) & (entries < count * tiles_here)
    owner = jnp.where(used, entries // tiles_here, place)
    blocks = jnp.arange(count)
    want = jnp.max(
        jnp.where(used[None, :] & (owner[None, :] == blocks[:, None]), entries[None, :] % tiles_here, -1), axis=1
    )
    told = jnp.broadcast_to(
        want.reshape(nx, 1, nz, ny).transpose(0, 1, 3, 2), (nx, nz, ny, nz)
    ).reshape(count, nz)
    heard = lax.all_to_all(told, TOK, 0, 0, tiled=True)
    asked = lax.dynamic_index_in_dim(heard, z, 1, keepdims=False)

    pair = jnp.stack([keys.reshape(rows, heads * HD), values.reshape(rows, heads * HD)])
    far = []
    for first, last, _ in PARTS:
        part = pair[:, :, first * HD : last * HD][None]
        far.append(lax.all_to_all(serve(asked, part, 8), TOK, 0, 0, tiled=True))

    d_attn = lax.dot_general(
        lax.all_gather(grad_out, HEAD, axis=1, tiled=True),
        w_out,
        (((1,), (1,)), ((), ())),
        preferred_element_type=jnp.float32,
    ).astype(jnp.bfloat16)
    flat_q = queries.reshape(rows, heads * HD)

    tiles = entries.shape[0]
    order = jnp.arange(tiles)
    rank = jnp.sum(used[None, :] & (order[None, :] < order[:, None]), axis=1)
    slot_of = jnp.max(
        jnp.where(used[None, :] & (rank[None, :] == order[:, None]), owner[None, :], -1), axis=1
    ).astype(jnp.int32)
    slot_of = jnp.where(slot_of >= 0, slot_of, place).astype(jnp.int32)
    number = jnp.sum(used.astype(jnp.int32)).reshape(1)

    grad_q, totals = [], []
    for (first, last, _), got in zip(PARTS, far):
        dq, own, out = attend(slot_of, slot_of, number, flat_q, d_attn, pair, got, first, last - first)
        back = lax.all_to_all(out, TOK, 0, 0, tiled=True)
        grad_q.append(dq)
        totals.append(settle(asked, own, back))
    grad_q = jnp.concatenate(grad_q, axis=1).reshape(rows, heads, HD)
    totals = jnp.concatenate(totals, axis=2).reshape(2, rows, heads, HD)
    return grad_q, totals[0], totals[1]


def solution(mesh):
    fine = Mesh(mesh.devices.reshape(2, 8, 4, 2, 2), TOK + HEAD)
    return jax.shard_map(
        shards,
        mesh=fine,
        in_specs=(
            P(TOK, HEAD, None),
            P(TOK, HEAD, None),
            P(TOK, HEAD, None),
            P(TOK, HEAD),
            P(HEAD, None),
            P(TOK, None),
        ),
        out_specs=(P(TOK, HEAD, None), P(TOK, HEAD, None), P(TOK, HEAD, None)),
        check_vma=False,
    )
```

time: 270 us -> 245 us (0.907)
  matrix products: 38.9 us -> 4.35 us
  waiting for transfers between devices: 112 us -> 144 us
  local copies, waits for them, and re-layouts: 39.3 us -> 12.7 us
  Pallas kernels: 0 us -> 25 us
  other arithmetic: 24 us -> 2.03 us
    dot_general x8 -> x1, matrix products: 38.9 us -> 4.35 us  [shards(): lax.dot_general(lax.all_gather(grad_out, HEAD, axis=1, tiled=True), w_out...]
    pallas_call x0 -> x6, Pallas kernels: none -> 25 us  [the longest x2 12.5 us: attend(): pl.pallas_call(functools.partial(attend_kernel, tiles), out_shape=(jax.Sh...]
    all_to_all x3 -> x5, waiting for transfers between devices: 84.8 us -> 109 us  [the longest x2 65.9 us: shards(): back = lax.all_to_all(out, TOK, 0, 0, tiled=True)]
    all_to_all x3 -> x5, starting transfers between devices: 25.2 us -> 41.1 us  [the longest x2 17 us: shards(): back = lax.all_to_all(out, TOK, 0, 0, tiled=True)]
    ppermute x4 -> x0, starting transfers between devices: 14.4 us -> none  [the longest x2 6.49 us: shifted(): lax.ppermute(value, axis, [(source, source + steps) for source in range(l...]
    all_gather x1, waiting for transfers between devices: 26 us -> 34.7 us  [shards(): lax.all_gather(grad_out, HEAD, axis=1, tiled=True)]
    reshape x3 -> x2, local copies, waits for them, and re-layouts: 8.47 us -> 0.25 us  [the longest x1 0.17 us: shards(): flat_q = queries.reshape(rows, heads * HD)]
    convert_element_type x3 -> x0, local copies, waits for them, and re-layouts: 7.75 us -> none  [the longest x1 4.91 us: shards(): slotted.reshape(2, count, capacity, row_len).astype(jnp.bfloat16)]
  transfers between devices with their start and end apart: 8 -> 6, of which waited for: 4 -> 5; matrix products, arithmetic and copies ran while one was open for 14% -> 3% of each run, Pallas kernels for 0% -> 8%
where the time goes in v1:
time: 245 us; the launch traced here: 244 us
  waiting for transfers between devices  144 us (59%)
  starting transfers between devices  41.1 us (17%)
  Pallas kernels  25 us (10%)
  between operations  14.3 us (6%)
  local copies, waits for them, and re-layouts  12.7 us (5%)
  matrix products  4.35 us (2%)
    all_to_all x2, waiting for transfers between devices, shards(): back = lax.all_to_all(out, TOK, 0, 0, tiled=True)  65.9 us
    all_to_all x2, waiting for transfers between devices, shards(): far.append(lax.all_to_all(serve(asked, part, 8), TOK, 0, 0, tiled=True))  35.5 us
    all_gather x1, waiting for transfers between devices, shards(): lax.all_gather(grad_out, HEAD, axis=1, tiled=True)  34.7 us
    all_to_all x2, starting transfers between devices, shards(): back = lax.all_to_all(out, TOK, 0, 0, tiled=True)  17 us
    all_to_all x1, starting transfers between devices, shards(): heard = lax.all_to_all(told, TOK, 0, 0, tiled=True)  12.7 us
    pallas_call x2, Pallas kernels, attend(): pl.pallas_call(functools.partial(attend_kernel, tiles), out_shape=(jax.Sh...  12.5 us
    all_to_all x2, starting transfers between devices, shards(): far.append(lax.all_to_all(serve(asked, part, 8), TOK, 0, 0, tiled=True))  11.4 us
    unnamed x26, local copies, waits for them, and re-layouts  9.52 us
  transfers between devices with their start and end apart: 6, of which 5 were waited for; matrix products, arithmetic and copies ran while one was open for 3% of the time, Pallas kernels for 8%

profile of v1, /device:TPU:32, one launch (start us, length us, event | category | flops | bytes accessed | tf_op | source)
XLA Modules:
  0.0 243.9 jit_solution(15147583041212530199)
XLA Ops:
  7.2 0.0 copy-start.8
  7.2 0.8 and_select_fusion
  8.0 0.6 convert_reduce_fusion.1
  8.6 0.1 select_reduce_fusion
  8.7 0.1 reshape.263
  8.8 0.1 copy.65
  8.9 0.6 broadcast_in_dim.59
  9.5 12.7 %all-to-all-start = ((s32[64,1,8]{2,1,0:T(1,128)}), s32[64,1,8]{2,1,0:T(1,128)S(1)}, u32[]{:S(2)}, u32[]{:S(2)}) async-start(s32[64,1,8]{2,1,0:T(1,128)} %bitcast.10), calls=%async_computation | async-start | bytes 65536 | tf_op jit(solution)/shard_map/all_to_all | solution.py:173
  22.2 1.2 copy.61
  23.4 0.2 copy.63
  23.6 0.0 copy-done.8
  23.6 0.2 copy.62
  23.8 0.2 copy.64
  23.9 0.1 fusion.2
  24.0 7.8 %all-to-all-done = s32[64,1,8]{2,1,0:T(1,128)S(1)} async-done(((s32[64,1,8]{2,1,0:T(1,128)}), s32[64,1,8]{2,1,0:T(1,128)S(1)}, u32[]{:S(2)}, u32[]{:S(2)}) %all-to-all-start) | async-done | bytes 2080 | tf_op jit(solution)/shard_map/all_to_all | solution.py:173
  31.8 1.3 dynamic-slice_reduce_fusion.asked_ref
  33.1 3.4 %shard_map.85 = bf16[64,2,16,384]{3,2,1,0:T(8,128)(2,1)} custom-call(s32[64]{0:T(128)S(1)} %dynamic-slice_reduce_fusion.asked_ref, bf16[1,2,256,384]{3,2,1,0:T(8,128)(2,1)S(1)} %get-tuple-element.34.pair_ref), custom_call_target="tpu_custom_call" | custom-call | tf_op jit(solution)/shard_map/pallas_call | solution.py:34
  36.6 5.5 %all-to-all-start.1 = ((bf16[64,2,16,384]{3,2,1,0:T(8,128)(2,1)}), bf16[64,2,16,384]{3,2,1,0:T(8,128)(2,1)S(1)}, u32[]{:S(2)}, u32[]{:S(2)}) async-start(bf16[64,2,16,384]{3,2,1,0:T(8,128)(2,1)} %shard_map.85), calls=%async_computation.1 | async-start | bytes 3145728 | tf_op jit(solution)/shard_map/all_to_all | solution.py:180
  42.0 3.5 %shard_map.87 = bf16[64,2,16,384]{3,2,1,0:T(8,128)(2,1)} custom-call(s32[64]{0:T(128)S(1)} %dynamic-slice_reduce_fusion.asked_ref, bf16[1,2,256,384]{3,2,1,0:T(8,128)(2,1)S(1)} %get-tuple-element.35.pair_ref), custom_call_target="tpu_custom_call" | custom-call | tf_op jit(solution)/shard_map/pallas_call | solution.py:34
  45.5 0.0 copy-start.9
  45.5 35.5 %all-to-all-done.1.far_ref = bf16[64,2,16,384]{3,2,1,0:T(8,128)(2,1)S(1)} async-done(((bf16[64,2,16,384]{3,2,1,0:T(8,128)(2,1)}), bf16[64,2,16,384]{3,2,1,0:T(8,128)(2,1)S(1)}, u32[]{:S(2)}, u32[]{:S(2)}) %all-to-all-start.1) | async-done | bytes 1572896 | tf_op jit(solution)/shard_map/all_to_all | solution.py:180
  81.0 0.0 copy-start
  81.0 1.1 copy-done
  82.1 5.9 %all-to-all-start.2 = ((bf16[64,2,16,384]{3,2,1,0:T(8,128)(2,1)}), bf16[64,2,16,384]{3,2,1,0:T(8,128)(2,1)S(1)}, u32[]{:S(2)}, u32[]{:S(2)}) async-start(bf16[64,2,16,384]{3,2,1,0:T(8,128)(2,1)} %shard_map.87), calls=%async_computation.2 | async-start | bytes 3145728 | tf_op jit(solution)/shard_map/all_to_all | solution.py:180
  88.0 0.0 all-gather.2.cloned.1.call-start
  88.1 0.7 all-gather.2.cloned.1.call-update
  88.8 0.0 copy-done.9
  88.8 0.2 copy.60
  89.0 0.2 copy.67.q_ref
  89.1 0.1 convert_reduce_fusion
  89.3 0.1 select_reduce_fusion.1
  89.4 0.1 pad_maximum_fusion.kv_ref
  89.5 34.7 %all-gather.2.cloned.1.call-done = bf16[256,3072]{1,0:T(8,128)(2,1)} async-done(((bf16[256,768]{1,0:T(8,128)(2,1)}), bf16[256,3072]{1,0:T(8,128)(2,1)}) %all-gather.2.cloned.1.call-update) | async-done | bytes 1572880 | tf_op jit(solution)/shard_map/all_gather | solution.py:183
  124.2 0.0 copy-start.1
  124.2 4.4 %convolution_convert_fusion.do_ref = bf16[256,768]{1,0:T(8,128)(2,1)S(1)} fusion(bf16[256,3072]{1,0:T(8,128)(2,1)} %all-gather.2.cloned.1.call-done, bf16[768,3072]{1,0:T(8,128)(2,1)} %param.10), kind=kOutput, calls=%fused_computation | convolution fusion | flops 1208156160 | bytes 6684672 | tf_op jit(solution)/shard_map/dot_general | solution.py:182
  128.5 0.0 copy-done.1
  128.5 6.2 %shard_map.86 = (bf16[256,384]{1,0:T(8,128)(2,1)S(1)}, f32[2,256,384]{2,1,0:T(8,128)S(1)}, bf16[64,2,16,384]{3,2,1,0:T(8,128)(2,1)S(1)}) custom-call(s32[42]{0:T(128)S(1)} %compare_select_fusion.src_ref.dst_ref, s32[42]{0:T(128)S(1)} %compare_select_fusion.src_ref.dst_ref, s32[1]{0:T(128)} %bitcast.3.num_ref, bf16[256,768]{1,0:T(8,128)(2,1)S(1)} %copy.67.q_ref, ...), custom_call_target="tpu_custom_call" | custom-call | tf_op jit(solution)/shard_map/pallas_call | solution.py:93
  134.8 0.0 copy-start.3
  134.8 1.1 copy-done.3
  135.9 0.0 copy-start.4
  135.9 0.9 copy-done.4
  136.8 0.0 all-to-all-done.2.far_ref
  136.8 10.5 %all-to-all-start.3 = ((bf16[64,2,16,384]{3,2,1,0:T(8,128)(2,1)}), bf16[64,2,16,384]{3,2,1,0:T(8,128)(2,1)}, u32[]{:S(2)}, u32[]{:S(2)}) async-start(bf16[64,2,16,384]{3,2,1,0:T(8,128)(2,1)} %copy-done.3), calls=%async_computation.3 | async-start | bytes 3145728 | tf_op jit(solution)/shard_map/all_to_all | solution.py:202
  147.3 6.2 %shard_map.88 = (bf16[256,384]{1,0:T(8,128)(2,1)S(1)}, f32[2,256,384]{2,1,0:T(8,128)S(1)}, bf16[64,2,16,384]{3,2,1,0:T(8,128)(2,1)S(1)}) custom-call(s32[42]{0:T(128)S(1)} %compare_select_fusion.src_ref.dst_ref, s32[42]{0:T(128)S(1)} %compare_select_fusion.src_ref.dst_ref, s32[1]{0:T(128)} %bitcast.3.num_ref, bf16[256,768]{1,0:T(8,128)(2,1)S(1)} %copy.67.q_ref, ...), custom_call_target="tpu_custom_call" | custom-call | tf_op jit(solution)/shard_map/pallas_call | solution.py:93
  153.6 0.0 copy-start.2
  153.6 1.1 copy-done.2
  154.7 0.0 copy-start.6
  154.7 0.9 copy-done.6
  155.6 31.5 %all-to-all-done.3.back_ref = bf16[64,2,16,384]{3,2,1,0:T(8,128)(2,1)} async-done(((bf16[64,2,16,384]{3,2,1,0:T(8,128)(2,1)}), bf16[64,2,16,384]{3,2,1,0:T(8,128)(2,1)}, u32[]{:S(2)}, u32[]{:S(2)}) %all-to-all-start.3) | async-done | bytes 1572896 | tf_op jit(solution)/shard_map/all_to_all | solution.py:202
  187.1 6.5 %all-to-all-start.4 = ((bf16[64,2,16,384]{3,2,1,0:T(8,128)(2,1)}), bf16[64,2,16,384]{3,2,1,0:T(8,128)(2,1)S(1)}, u32[]{:S(2)}, u32[]{:S(2)}) async-start(bf16[64,2,16,384]{3,2,1,0:T(8,128)(2,1)} %copy-done.2), calls=%async_computation.4 | async-start | bytes 3145728 | tf_op jit(solution)/shard_map/all_to_all | solution.py:202
  193.6 0.0 copy-start.5
  193.6 0.2 copy.69
  193.8 0.9 copy.72
  194.7 0.0 copy-start.7
  194.7 0.0 copy-done.5
  194.7 3.5 %shard_map.89 = bf16[2,256,384]{2,1,0:T(8,128)(2,1)S(1)} custom-call(s32[64]{0:T(128)S(1)} %dynamic-slice_reduce_fusion.asked_ref, f32[2,256,384]{2,1,0:T(8,128)S(1)} %copy-done.5, bf16[64,2,16,384]{3,2,1,0:T(8,128)(2,1)} %all-to-all-done.3.back_ref), custom_call_target="tpu_custom_call" | custom-call | tf_op jit(solution)/shard_map/pallas_call | solution.py:138
  198.2 34.4 %all-to-all-done.4.back_ref = bf16[64,2,16,384]{3,2,1,0:T(8,128)(2,1)S(1)} async-done(((bf16[64,2,16,384]{3,2,1,0:T(8,128)(2,1)}), bf16[64,2,16,384]{3,2,1,0:T(8,128)(2,1)S(1)}, u32[]{:S(2)}, u32[]{:S(2)}) %all-to-all-start.4) | async-done | bytes 1572896 | tf_op jit(solution)/shard_map/all_to_all | solution.py:202
  232.7 0.0 copy-done.7
  232.7 2.1 shard_map.90
  234.8 0.1 pad_maximum_fusion.1
  234.9 0.2 copy.71
  235.1 0.9 copy.74
  236.0 0.2 copy.70
  236.1 0.9 copy.73
  (3 shorter events, 0.0 us)
Async XLA Ops:
  7.2 16.4 %copy-start.8 = (bf16[256,6,128]{2,0,1:T(8,128)(2,1)S(1)}, bf16[256,6,128]{2,0,1:T(8,128)(2,1)}, u32[]{:S(2)}) copy-start(bf16[256,6,128]{2,0,1:T(8,128)(2,1)} %param.8) | copy-start | bytes 1179652
  9.5 22.3 %all-to-all-start = ((s32[64,1,8]{2,1,0:T(1,128)}), s32[64,1,8]{2,1,0:T(1,128)S(1)}, u32[]{:S(2)}, u32[]{:S(2)}) async-start(s32[64,1,8]{2,1,0:T(1,128)} %bitcast.10), calls=%async_computation | async-start | bytes 65536 | tf_op jit(solution)/shard_map/all_to_all | solution.py:173
  36.6 44.4 %all-to-all-start.1 = ((bf16[64,2,16,384]{3,2,1,0:T(8,128)(2,1)}), bf16[64,2,16,384]{3,2,1,0:T(8,128)(2,1)S(1)}, u32[]{:S(2)}, u32[]{:S(2)}) async-start(bf16[64,2,16,384]{3,2,1,0:T(8,128)(2,1)} %shard_map.85), calls=%async_computation.1 | async-start | bytes 3145728 | tf_op jit(solution)/shard_map/all_to_all | solution.py:180
  45.5 43.3 %copy-start.9 = (bf16[256,6,128]{2,0,1:T(8,128)(2,1)S(1)}, bf16[256,6,128]{2,0,1:T(8,128)(2,1)}, u32[]{:S(2)}) copy-start(bf16[256,6,128]{2,0,1:T(8,128)(2,1)} %param.6) | copy-start | bytes 1179652
  81.0 1.1 copy-start
  82.1 54.7 %all-to-all-start.2 = ((bf16[64,2,16,384]{3,2,1,0:T(8,128)(2,1)}), bf16[64,2,16,384]{3,2,1,0:T(8,128)(2,1)S(1)}, u32[]{:S(2)}, u32[]{:S(2)}) async-start(bf16[64,2,16,384]{3,2,1,0:T(8,128)(2,1)} %shard_map.87), calls=%async_computation.2 | async-start | bytes 3145728 | tf_op jit(solution)/shard_map/all_to_all | solution.py:180
  88.0 36.1 %all-gather.2.cloned.1.call-start = ((), (), s32[]{:S(2)}) async-start(), calls=%async_computation.5 | async-start | bytes 1966080 | tf_op jit(solution)/shard_map/all_gather | solution.py:183
  124.2 4.4 %copy-start.1 = (bf16[64,2,16,384]{3,2,1,0:T(8,128)(2,1)S(1)}, bf16[64,2,16,384]{3,2,1,0:T(8,128)(2,1)}, u32[]{:S(2)}) copy-start(bf16[64,2,16,384]{3,2,1,0:T(8,128)(2,1)} %copy-done) | copy-start | bytes 4718596
  134.8 1.1 copy-start.3
  135.9 0.9 copy-start.4
  136.8 50.3 %all-to-all-start.3 = ((bf16[64,2,16,384]{3,2,1,0:T(8,128)(2,1)}), bf16[64,2,16,384]{3,2,1,0:T(8,128)(2,1)}, u32[]{:S(2)}, u32[]{:S(2)}) async-start(bf16[64,2,16,384]{3,2,1,0:T(8,128)(2,1)} %copy-done.3), calls=%async_computation.3 | async-start | bytes 3145728 | tf_op jit(solution)/shard_map/all_to_all | solution.py:202
  153.6 1.2 copy-start.2
  154.7 0.9 copy-start.6
  187.1 45.6 %all-to-all-start.4 = ((bf16[64,2,16,384]{3,2,1,0:T(8,128)(2,1)}), bf16[64,2,16,384]{3,2,1,0:T(8,128)(2,1)S(1)}, u32[]{:S(2)}, u32[]{:S(2)}) async-start(bf16[64,2,16,384]{3,2,1,0:T(8,128)(2,1)} %copy-done.2), calls=%async_computation.4 | async-start | bytes 3145728 | tf_op jit(solution)/shard_map/all_to_all | solution.py:202
  193.6 1.1 copy-start.5
  194.7 37.9 %copy-start.7 = (f32[2,256,384]{2,1,0:T(8,128)S(1)}, f32[2,256,384]{2,1,0:T(8,128)}, u32[]{:S(2)}) copy-start(f32[2,256,384]{2,1,0:T(8,128)} %copy-done.6) | copy-start | bytes 2359300
Sparse Core Ops, SparseCore 0:
  90.7 33.4 all-gather.1

commit v2 on v1

--- a/solution.py
+++ b/solution.py
@@ -152,6 +152,58 @@
     )(asked, own, back)
 
 
+def project_kernel(me_ref, own_ref, flip_ref, both_ref, w_ref, out_ref, acc):
+    step = pl.program_id(0)
+
+    def add(rows):
+        part = lax.dot_general(rows, w_ref[...], (((1,), (1,)), ((), ())), preferred_element_type=jnp.float32)
+        acc[...] = jnp.where(step == 0, part, acc[...] + part)
+
+    @pl.when(step == 0)
+    def _():
+        add(own_ref[...])
+
+    @pl.when(step == 1)
+    def _():
+        add(flip_ref[...])
+
+    @pl.when(step == 2)
+    def _():
+        add(both_ref[0])
+
+    @pl.when(step == 3)
+    def _():
+        add(both_ref[1])
+        out_ref[...] = acc[...].astype(out_ref.dtype)
+
+
+def project(grad_out, w_out):
+    rows, width = grad_out.shape
+    out_width = w_out.shape[0]
+    swap = [(0, 1), (1, 0)]
+    flip = lax.ppermute(grad_out, HEAD[0], swap)
+    both = lax.ppermute(jnp.stack([grad_out, flip]), HEAD[1], swap)
+    me = (lax.axis_index(HEAD[0]) * 2 + lax.axis_index(HEAD[1])).astype(jnp.int32).reshape(1)
+    block = lambda i, m: (0, m[0] ^ (i // 2 + (i % 2) * 2))
+    return pl.pallas_call(
+        project_kernel,
+        out_shape=jax.ShapeDtypeStruct((rows, out_width), jnp.bfloat16),
+        grid_spec=pltpu.PrefetchScalarGridSpec(
+            num_scalar_prefetch=1,
+            grid=(4,),
+            in_specs=[
+                pl.BlockSpec((rows, width), lambda i, m: (0, 0)),
+                pl.BlockSpec((rows, width), lambda i, m: (0, 0)),
+                pl.BlockSpec((2, rows, width), lambda i, m: (0, 0, 0)),
+                pl.BlockSpec((out_width, width), block),
+            ],
+            out_specs=pl.BlockSpec((rows, out_width), lambda i, m: (0, 0)),
+            scratch_shapes=[pltpu.VMEM((rows, out_width), jnp.float32)],
+        ),
+        compiler_params=pltpu.CompilerParams(vmem_limit_bytes=VMEM_LIMIT),
+    )(me, grad_out, flip, both, w_out)
+
+
 def shards(queries, keys, values, grad_out, w_out, crit):
     rows, heads, _ = queries.shape
     tiles_here = rows // KT
@@ -179,12 +231,7 @@
         part = pair[:, :, first * HD : last * HD][None]
         far.append(lax.all_to_all(serve(asked, part, 8), TOK, 0, 0, tiled=True))
 
-    d_attn = lax.dot_general(
-        lax.all_gather(grad_out, HEAD, axis=1, tiled=True),
-        w_out,
-        (((1,), (1,)), ((), ())),
-        preferred_element_type=jnp.float32,
-    ).astype(jnp.bfloat16)
+    d_attn = project(grad_out, w_out)
     flat_q = queries.reshape(rows, heads * HD)
 
     tiles = entries.shape[0]

time: 245 us -> 221 us (0.902)
  waiting for transfers between devices: 144 us -> 129 us
  between operations: 14.3 us -> 0.93 us
  Pallas kernels: 25 us -> 29.5 us
  matrix products: 4.35 us -> 0 us
  starting transfers between devices: 41.1 us -> 44.6 us
    all_gather x1 -> x0, waiting for transfers between devices: 34.7 us -> none  [shards(): lax.all_gather(grad_out, HEAD, axis=1, tiled=True)]
    ppermute x0 -> x2, waiting for transfers between devices: none -> 17.3 us  [the longest x1 16.4 us: project(): flip = lax.ppermute(grad_out, HEAD[0], swap)]
    pallas_call x0 -> x1, Pallas kernels: none -> 4.61 us  [project(): pl.pallas_call(project_kernel, out_shape=jax.ShapeDtypeStruct((rows, out_...]
    dot_general x1 -> x0, matrix products: 4.35 us -> none  [shards(): lax.dot_general(lax.all_gather(grad_out, HEAD, axis=1, tiled=True), w_out...]
    ppermute x0 -> x2, starting transfers between devices: none -> 2.82 us  [the longest x1 2.82 us: project(): flip = lax.ppermute(grad_out, HEAD[0], swap)]
    all_to_all x2, waiting for transfers between devices: 35.5 us -> 38 us  [shards(): far.append(lax.all_to_all(serve(asked, part, 8), TOK, 0, 0, tiled=True))]
    unnamed x26 -> x34, local copies, waits for them, and re-layouts: 9.52 us -> 9.54 us
  transfers between devices with their start and end apart: 6 -> 7, of which waited for: 5 -> 7; matrix products, arithmetic and copies ran while one was open for 3% -> 3% of each run, Pallas kernels for 8% -> 11%
where the time goes in v2:
time: 221 us
  waiting for transfers between devices  129 us (58%)
  starting transfers between devices  44.6 us (20%)
  Pallas kernels  29.5 us (13%)
  local copies, waits for them, and re-layouts  12.7 us (6%)
  other arithmetic  4.06 us (2%)
    all_to_all x2, waiting for transfers between devices, shards(): back = lax.all_to_all(out, TOK, 0, 0, tiled=True)  65.7 us
    all_to_all x2, waiting for transfers between devices, shards(): far.append(lax.all_to_all(serve(asked, part, 8), TOK, 0, 0, tiled=True))  38 us
    all_to_all x2, starting transfers between devices, shards(): back = lax.all_to_all(out, TOK, 0, 0, tiled=True)  17.7 us
    ppermute x1, waiting for transfers between devices, project(): flip = lax.ppermute(grad_out, HEAD[0], swap)  16.4 us
    all_to_all x1, starting transfers between devices, shards(): heard = lax.all_to_all(told, TOK, 0, 0, tiled=True)  12.7 us
    pallas_call x2, Pallas kernels, attend(): pl.pallas_call(functools.partial(attend_kernel, tiles), out_shape=(jax.Sh...  12.5 us
    all_to_all x2, starting transfers between devices, shards(): far.append(lax.all_to_all(serve(asked, part, 8), TOK, 0, 0, tiled=True))  11.4 us
    unnamed x34, local copies, waits for them, and re-layouts  9.54 us
  transfers between devices with their start and end apart: 7, of which 7 were waited for; matrix products, arithmetic and copies ran while one was open for 3% of the time, Pallas kernels for 11%

profile of v2, /device:TPU:32, one launch (start us, length us, event | category | flops | bytes accessed | tf_op | source)
XLA Modules:
  0.0 220.5 jit_solution(5882325250369151310)
XLA Ops:
  0.6 0.0 copy-start.12
  0.7 0.8 and_select_fusion
  1.4 0.6 convert_reduce_fusion.1
  2.1 0.1 select_reduce_fusion
  2.2 0.1 reshape.267
  2.3 0.1 copy.65
  2.4 0.6 broadcast_in_dim.59
  3.0 12.7 %all-to-all-start = ((s32[64,1,8]{2,1,0:T(1,128)}), s32[64,1,8]{2,1,0:T(1,128)S(1)}, u32[]{:S(2)}, u32[]{:S(2)}) async-start(s32[64,1,8]{2,1,0:T(1,128)} %bitcast.13), calls=%async_computation | async-start | bytes 65536 | tf_op jit(solution)/shard_map/all_to_all | solution.py:225
  15.7 1.2 copy.61
  16.9 0.2 copy.63
  17.0 0.0 copy-done.12
  17.0 0.2 copy.62
  17.2 0.2 copy.64
  17.4 0.0 copy-start.11
  17.4 0.1 fusion.2
  17.5 7.7 %all-to-all-done = s32[64,1,8]{2,1,0:T(1,128)S(1)} async-done(((s32[64,1,8]{2,1,0:T(1,128)}), s32[64,1,8]{2,1,0:T(1,128)S(1)}, u32[]{:S(2)}, u32[]{:S(2)}) %all-to-all-start) | async-done | bytes 2080 | tf_op jit(solution)/shard_map/all_to_all | solution.py:225
  25.3 1.3 dynamic-slice_reduce_fusion.asked_ref
  26.6 3.4 %shard_map.86 = bf16[64,2,16,384]{3,2,1,0:T(8,128)(2,1)} custom-call(s32[64]{0:T(128)S(1)} %dynamic-slice_reduce_fusion.asked_ref, bf16[1,2,256,384]{3,2,1,0:T(8,128)(2,1)S(1)} %get-tuple-element.34.pair_ref), custom_call_target="tpu_custom_call" | custom-call | tf_op jit(solution)/shard_map/pallas_call | solution.py:34
  30.0 5.5 %all-to-all-start.1 = ((bf16[64,2,16,384]{3,2,1,0:T(8,128)(2,1)}), bf16[64,2,16,384]{3,2,1,0:T(8,128)(2,1)S(1)}, u32[]{:S(2)}, u32[]{:S(2)}) async-start(bf16[64,2,16,384]{3,2,1,0:T(8,128)(2,1)} %shard_map.86), calls=%async_computation.1 | async-start | bytes 3145728 | tf_op jit(solution)/shard_map/all_to_all | solution.py:232
  35.5 3.4 %shard_map.88 = bf16[64,2,16,384]{3,2,1,0:T(8,128)(2,1)} custom-call(s32[64]{0:T(128)S(1)} %dynamic-slice_reduce_fusion.asked_ref, bf16[1,2,256,384]{3,2,1,0:T(8,128)(2,1)S(1)} %get-tuple-element.35.pair_ref), custom_call_target="tpu_custom_call" | custom-call | tf_op jit(solution)/shard_map/pallas_call | solution.py:34
  39.0 35.5 %all-to-all-done.1.far_ref = bf16[64,2,16,384]{3,2,1,0:T(8,128)(2,1)S(1)} async-done(((bf16[64,2,16,384]{3,2,1,0:T(8,128)(2,1)}), bf16[64,2,16,384]{3,2,1,0:T(8,128)(2,1)S(1)}, u32[]{:S(2)}, u32[]{:S(2)}) %all-to-all-start.1) | async-done | bytes 1572896 | tf_op jit(solution)/shard_map/all_to_all | solution.py:232
  74.5 1.1 copy-done
  75.6 0.0 copy-done.11
  75.6 5.9 %all-to-all-start.2 = ((bf16[64,2,16,384]{3,2,1,0:T(8,128)(2,1)}), bf16[64,2,16,384]{3,2,1,0:T(8,128)(2,1)S(1)}, u32[]{:S(2)}, u32[]{:S(2)}) async-start(bf16[64,2,16,384]{3,2,1,0:T(8,128)(2,1)} %shard_map.88), calls=%async_computation.2 | async-start | bytes 3145728 | tf_op jit(solution)/shard_map/all_to_all | solution.py:232
  81.5 0.0 copy-done.4
  81.5 0.0 copy-start.13
  81.5 2.8 %collective-permute-start = (bf16[256,768]{1,0:T(8,128)(2,1)S(1)}, bf16[256,768]{1,0:T(8,128)(2,1)S(1)}, u32[]{:S(2)}, u32[]{:S(2)}) collective-permute-start(bf16[256,768]{1,0:T(8,128)(2,1)S(1)} %copy-done.4), channel_id=1, source_target_pairs={{0,2},{2,0},{1,3},{3,1},{4,6},{6,4},{5,7},{7,5},{8,10},{10,8},{9,1... | collective-permute-start | bytes 1179656 | tf_op jit(solution)/shard_map/ppermute | solution.py:184
  84.4 16.4 %collective-permute-done.flip_ref = bf16[256,768]{1,0:T(8,128)(2,1)S(1)} collective-permute-done((bf16[256,768]{1,0:T(8,128)(2,1)S(1)}, bf16[256,768]{1,0:T(8,128)(2,1)S(1)}, u32[]{:S(2)}, u32[]{:S(2)}) %collective-permute-start) | collective-permute-done | bytes 393248 | tf_op jit(solution)/shard_map/ppermute | solution.py:184
  100.7 1.0 pad_maximum_fusion.1
  101.8 0.0 collective-permute-start.1
  101.8 0.0 copy-done.13
  101.8 0.2 copy.60
  101.9 0.0 copy-done.5
  102.0 0.2 copy.67.q_ref
  102.1 0.0 copy-start.6
  102.2 0.1 convert_reduce_fusion
  102.3 0.1 select_reduce_fusion.1
  102.4 1.1 pad_maximum_fusion.kv_ref
  103.5 0.9 collective-permute-done.1.both_ref
  104.4 0.0 copy-done.6
  104.4 4.6 %shard_map.85.do_ref = bf16[256,768]{1,0:T(8,128)(2,1)S(1)} custom-call(s32[1]{0:T(128)} %bitcast.5.me_ref, bf16[256,768]{1,0:T(8,128)(2,1)S(1)} %copy-done.4, bf16[256,768]{1,0:T(8,128)(2,1)S(1)} %copy-done.6, bf16[2,256,768]{2,1,0:T(8,128)(2,1)} %collective-permute-done.1.both_ref, bf16[768,3072]{1,0:T(8,128)(2,1)} %w_ref.1), custom_call_target="tpu_custom_call" | custom-call | tf_op jit(solution)/shard_map/pallas_call | solution.py:188
  109.0 0.0 copy-done.1
  109.0 6.2 %shard_map.87 = (bf16[256,384]{1,0:T(8,128)(2,1)S(1)}, f32[2,256,384]{2,1,0:T(8,128)S(1)}, bf16[64,2,16,384]{3,2,1,0:T(8,128)(2,1)S(1)}) custom-call(s32[42]{0:T(128)S(1)} %compare_select_fusion.src_ref.dst_ref, s32[42]{0:T(128)S(1)} %compare_select_fusion.src_ref.dst_ref, s32[1]{0:T(128)} %bitcast.3.num_ref, bf16[256,768]{1,0:T(8,128)(2,1)S(1)} %copy.67.q_ref, ...), custom_call_target="tpu_custom_call" | custom-call | tf_op jit(solution)/shard_map/pallas_call | solution.py:93
  115.3 0.0 copy-start.3
  115.3 1.1 copy-done.3
  116.4 0.9 copy-done.7
  117.3 2.5 %all-to-all-done.2.far_ref = bf16[64,2,16,384]{3,2,1,0:T(8,128)(2,1)S(1)} async-done(((bf16[64,2,16,384]{3,2,1,0:T(8,128)(2,1)}), bf16[64,2,16,384]{3,2,1,0:T(8,128)(2,1)S(1)}, u32[]{:S(2)}, u32[]{:S(2)}) %all-to-all-start.2) | async-done | bytes 1572896 | tf_op jit(solution)/shard_map/all_to_all | solution.py:232
  119.8 11.2 %all-to-all-start.3 = ((bf16[64,2,16,384]{3,2,1,0:T(8,128)(2,1)}), bf16[64,2,16,384]{3,2,1,0:T(8,128)(2,1)}, u32[]{:S(2)}, u32[]{:S(2)}) async-start(bf16[64,2,16,384]{3,2,1,0:T(8,128)(2,1)} %copy-done.3), calls=%async_computation.3 | async-start | bytes 3145728 | tf_op jit(solution)/shard_map/all_to_all | solution.py:249
  131.0 6.2 %shard_map.89 = (bf16[256,384]{1,0:T(8,128)(2,1)S(1)}, f32[2,256,384]{2,1,0:T(8,128)S(1)}, bf16[64,2,16,384]{3,2,1,0:T(8,128)(2,1)S(1)}) custom-call(s32[42]{0:T(128)S(1)} %compare_select_fusion.src_ref.dst_ref, s32[42]{0:T(128)S(1)} %compare_select_fusion.src_ref.dst_ref, s32[1]{0:T(128)} %bitcast.3.num_ref, bf16[256,768]{1,0:T(8,128)(2,1)S(1)} %copy.67.q_ref, ...), custom_call_target="tpu_custom_call" | custom-call | tf_op jit(solution)/shard_map/pallas_call | solution.py:93
  137.3 1.1 copy-done.2
  138.4 0.9 copy-done.9
  139.3 31.4 %all-to-all-done.3.back_ref = bf16[64,2,16,384]{3,2,1,0:T(8,128)(2,1)} async-done(((bf16[64,2,16,384]{3,2,1,0:T(8,128)(2,1)}), bf16[64,2,16,384]{3,2,1,0:T(8,128)(2,1)}, u32[]{:S(2)}, u32[]{:S(2)}) %all-to-all-start.3) | async-done | bytes 1572896 | tf_op jit(solution)/shard_map/all_to_all | solution.py:249
  170.7 6.5 %all-to-all-start.4 = ((bf16[64,2,16,384]{3,2,1,0:T(8,128)(2,1)}), bf16[64,2,16,384]{3,2,1,0:T(8,128)(2,1)S(1)}, u32[]{:S(2)}, u32[]{:S(2)}) async-start(bf16[64,2,16,384]{3,2,1,0:T(8,128)(2,1)} %copy-done.2), calls=%async_computation.4 | async-start | bytes 3145728 | tf_op jit(solution)/shard_map/all_to_all | solution.py:249
  177.2 0.2 copy.69
  177.4 0.9 copy.72
  178.3 3.5 %shard_map.90 = bf16[2,256,384]{2,1,0:T(8,128)(2,1)S(1)} custom-call(s32[64]{0:T(128)S(1)} %dynamic-slice_reduce_fusion.asked_ref, f32[2,256,384]{2,1,0:T(8,128)S(1)} %copy-done.8, bf16[64,2,16,384]{3,2,1,0:T(8,128)(2,1)} %all-to-all-done.3.back_ref), custom_call_target="tpu_custom_call" | custom-call | tf_op jit(solution)/shard_map/pallas_call | solution.py:138
  181.8 34.3 %all-to-all-done.4.back_ref = bf16[64,2,16,384]{3,2,1,0:T(8,128)(2,1)S(1)} async-done(((bf16[64,2,16,384]{3,2,1,0:T(8,128)(2,1)}), bf16[64,2,16,384]{3,2,1,0:T(8,128)(2,1)S(1)}, u32[]{:S(2)}, u32[]{:S(2)}) %all-to-all-start.4) | async-done | bytes 1572896 | tf_op jit(solution)/shard_map/all_to_all | solution.py:249
  216.1 0.0 copy-done.10
  216.1 2.1 shard_map.91
  218.2 0.1 pad_maximum_fusion.2
  218.3 0.2 copy.71
  218.5 0.9 copy.74
  219.4 0.2 copy.70
  219.6 0.9 copy.73
  (13 shorter events, 0.1 us)
Async XLA Ops:
  0.6 16.4 %copy-start.12 = (bf16[256,6,128]{2,0,1:T(8,128)(2,1)S(1)}, bf16[256,6,128]{2,0,1:T(8,128)(2,1)}, u32[]{:S(2)}) copy-start(bf16[256,6,128]{2,0,1:T(8,128)(2,1)} %param.8) | copy-start | bytes 1179652
  3.0 22.3 %all-to-all-start = ((s32[64,1,8]{2,1,0:T(1,128)}), s32[64,1,8]{2,1,0:T(1,128)S(1)}, u32[]{:S(2)}, u32[]{:S(2)}) async-start(s32[64,1,8]{2,1,0:T(1,128)} %bitcast.13), calls=%async_computation | async-start | bytes 65536 | tf_op jit(solution)/shard_map/all_to_all | solution.py:225
  17.4 58.2 %copy-start.11 = (bf16[1,256,768]{2,1,0:T(8,128)(2,1)}, bf16[1,256,768]{2,1,0:T(8,128)(2,1)S(1)}, u32[]{:S(2)}) copy-start(bf16[1,256,768]{2,1,0:T(8,128)(2,1)S(1)} %copy.64) | copy-start | bytes 1179652
  30.0 44.4 %all-to-all-start.1 = ((bf16[64,2,16,384]{3,2,1,0:T(8,128)(2,1)}), bf16[64,2,16,384]{3,2,1,0:T(8,128)(2,1)S(1)}, u32[]{:S(2)}, u32[]{:S(2)}) async-start(bf16[64,2,16,384]{3,2,1,0:T(8,128)(2,1)} %shard_map.86), calls=%async_computation.1 | async-start | bytes 3145728 | tf_op jit(solution)/shard_map/all_to_all | solution.py:232
  39.0 42.6 %copy-start.4 = (bf16[256,768]{1,0:T(8,128)(2,1)S(1)}, bf16[256,768]{1,0:T(8,128)(2,1)}, u32[]{:S(2)}) copy-start(bf16[256,768]{1,0:T(8,128)(2,1)} %own_ref.1) | copy-start | bytes 1179652
  74.5 1.1 copy-start
  75.6 44.2 %all-to-all-start.2 = ((bf16[64,2,16,384]{3,2,1,0:T(8,128)(2,1)}), bf16[64,2,16,384]{3,2,1,0:T(8,128)(2,1)S(1)}, u32[]{:S(2)}, u32[]{:S(2)}) async-start(bf16[64,2,16,384]{3,2,1,0:T(8,128)(2,1)} %shard_map.88), calls=%async_computation.2 | async-start | bytes 3145728 | tf_op jit(solution)/shard_map/all_to_all | solution.py:232
  81.5 20.2 %copy-start.13 = (bf16[256,6,128]{2,0,1:T(8,128)(2,1)S(1)}, bf16[256,6,128]{2,0,1:T(8,128)(2,1)}, u32[]{:S(2)}) copy-start(bf16[256,6,128]{2,0,1:T(8,128)(2,1)} %param.6) | copy-start | bytes 1179652
  81.5 19.2 %collective-permute-start = (bf16[256,768]{1,0:T(8,128)(2,1)S(1)}, bf16[256,768]{1,0:T(8,128)(2,1)S(1)}, u32[]{:S(2)}, u32[]{:S(2)}) collective-permute-start(bf16[256,768]{1,0:T(8,128)(2,1)S(1)} %copy-done.4), channel_id=1, source_target_pairs={{0,2},{2,0},{1,3},{3,1},{4,6},{6,4},{5,7},{7,5},{8,10},{10,8},{9,1... | collective-permute-start | bytes 1179656 | tf_op jit(solution)/shard_map/ppermute | solution.py:184
  100.7 1.2 copy-start.5
  101.8 2.6 %collective-permute-start.1 = (bf16[2,256,768]{2,1,0:T(8,128)(2,1)}, bf16[2,256,768]{2,1,0:T(8,128)(2,1)}, u32[]{:S(2)}, u32[]{:S(2)}) collective-permute-start(bf16[2,256,768]{2,1,0:T(8,128)(2,1)} %pad_maximum_fusion.1), channel_id=1, source_target_pairs={{0,1},{1,0},{2,3},{3,2},{4,5},{5,4},{6,7},{7,6},{8,9},{9,8},{10,11... | collective-permute-start | bytes 2359304 | tf_op jit(solution)/shard_map/ppermute | solution.py:185
  102.1 2.2 %copy-start.6 = (bf16[256,768]{1,0:T(8,128)(2,1)S(1)}, bf16[256,768]{1,0:T(8,128)(2,1)}, u32[]{:S(2)}) copy-start(bf16[256,768]{1,0:T(8,128)(2,1)} %copy-done.5) | copy-start | bytes 1179652
  104.4 4.6 %copy-start.1 = (bf16[64,2,16,384]{3,2,1,0:T(8,128)(2,1)S(1)}, bf16[64,2,16,384]{3,2,1,0:T(8,128)(2,1)}, u32[]{:S(2)}) copy-start(bf16[64,2,16,384]{3,2,1,0:T(8,128)(2,1)} %copy-done) | copy-start | bytes 4718596
  115.3 1.1 copy-start.3
  116.4 0.9 copy-start.7
  119.8 50.9 %all-to-all-start.3 = ((bf16[64,2,16,384]{3,2,1,0:T(8,128)(2,1)}), bf16[64,2,16,384]{3,2,1,0:T(8,128)(2,1)}, u32[]{:S(2)}, u32[]{:S(2)}) async-start(bf16[64,2,16,384]{3,2,1,0:T(8,128)(2,1)} %copy-done.3), calls=%async_computation.3 | async-start | bytes 3145728 | tf_op jit(solution)/shard_map/all_to_all | solution.py:249
  137.3 1.2 copy-start.2
  138.4 0.9 copy-start.9
  170.7 45.4 %all-to-all-start.4 = ((bf16[64,2,16,384]{3,2,1,0:T(8,128)(2,1)}), bf16[64,2,16,384]{3,2,1,0:T(8,128)(2,1)S(1)}, u32[]{:S(2)}, u32[]{:S(2)}) async-start(bf16[64,2,16,384]{3,2,1,0:T(8,128)(2,1)} %copy-done.2), calls=%async_computation.4 | async-start | bytes 3145728 | tf_op jit(solution)/shard_map/all_to_all | solution.py:249
  177.2 1.1 copy-start.8
  178.3 37.8 %copy-start.10 = (f32[2,256,384]{2,1,0:T(8,128)S(1)}, f32[2,256,384]{2,1,0:T(8,128)}, u32[]{:S(2)}) copy-start(f32[2,256,384]{2,1,0:T(8,128)} %copy-done.9) | copy-start | bytes 2359300

commit v3 on v2

v3 whole, which is shorter than its diff:
```python
import functools
import math

import jax
import jax.numpy as jnp
from jax import lax
from jax.experimental import pallas as pl
from jax.experimental.pallas import tpu as pltpu
from jax.sharding import Mesh
from jax.sharding import PartitionSpec as P

KT = 16
HD = 128
TOK = ("x_lo", "z", "y")
PLANE = ("x_lo", "y")
HEAD = ("x_hi", "core")
VMEM_LIMIT = 48 * 1024 * 1024
RING = 3
STEPS = (0, -1, 1, -2, 2, -3, 3, 4)
PARAMS = pltpu.CompilerParams(vmem_limit_bytes=VMEM_LIMIT)
VMEM = pl.BlockSpec(memory_space=pltpu.VMEM)
SMEM = pl.BlockSpec(memory_space=pltpu.SMEM)


def tile_rows(tile):
    return pl.ds(pl.multiple_of(tile * KT, KT), KT)


def serve_all_kernel(first, asked_ref, k_ref, v_ref, out_ref):
    block, heads = out_ref.shape[:2]
    for i in range(block):
        rows = tile_rows(jnp.maximum(asked_ref[pl.program_id(0) * block + i], 0))
        for h in range(heads):
            out_ref[i, h, 0] = k_ref[first + h, rows, :]
            out_ref[i, h, 1] = v_ref[first + h, rows, :]


def serve_all(asked, keys, values, first, block=16):
    count, heads = asked.shape[0], keys.shape[0] - first
    whole = pl.BlockSpec(keys.shape, lambda i, a: (0, 0, 0))
    return pl.pallas_call(
        functools.partial(serve_all_kernel, first),
        out_shape=jax.ShapeDtypeStruct((count, heads, 2, KT, HD), keys.dtype),
        grid_spec=pltpu.PrefetchScalarGridSpec(
            num_scalar_prefetch=1,
            grid=(count // block,),
            in_specs=[whole, whole],
            out_specs=pl.BlockSpec((block, heads, 2, KT, HD), lambda i, a: (i, 0, 0, 0, 0)),
        ),
        compiler_params=PARAMS,
    )(asked, keys, values)


def serve_plane_kernel(sizes, wanted_ref, pos_ref, *refs):
    nx, nz, ny = sizes
    held, outs = refs[: len(STEPS) + 1], refs[len(STEPS) + 1 :]
    heads = outs[0].shape[1]
    for r in range(nx * ny):
        mate = lax.rem(pos_ref[0] + r // ny, nx) * ny + lax.rem(pos_ref[2] + r % ny, ny)
        for s, step in enumerate(STEPS):
            tile = wanted_ref[mate * nz + lax.rem(pos_ref[1] + step + nz, nz)]
            rows = tile_rows(jnp.maximum(tile, 0))
            for h in range(heads):
                for kind in range(2):
                    if s < len(STEPS) - 1:
                        outs[r][s, h, kind] = held[s][kind, h, rows, :]
                    else:
                        outs[r][s, h, kind] = held[s + kind][h, rows, :]


def serve_plane(sizes, wanted, pos, held):
    mates = sizes[0] * sizes[2]
    heads = held[0].shape[1]
    return pl.pallas_call(
        functools.partial(serve_plane_kernel, sizes),
        out_shape=[jax.ShapeDtypeStruct((len(STEPS), heads, 2, KT, HD), held[0].dtype)] * mates,
        in_specs=[SMEM] * 2 + [VMEM] * len(held),
        out_specs=[VMEM] * mates,
        compiler_params=PARAMS,
    )(wanted, pos, *held)


def attend_kernel(tiles, parts, src_ref, dst_ref, num_ref, q_ref, do_ref, k_ref, v_ref, *refs):
    fars, (dq_ref, own_ref, out_ref, k_all, v_all) = refs[:parts], refs[-5 - (parts > 1) :][:5]
    rows = q_ref.shape[1]
    total = rows + tiles * KT
    scale = HD**-0.5
    if parts > 1:
        far_ref = refs[-1]
        each = fars[0].shape[0]
        for i in range(parts):
            far_ref[i * each : (i + 1) * each] = fars[i][:, 0]
        load = lambda slot, kind: far_ref[slot, kind]
    else:
        load = lambda slot, kind: fars[0][slot, 0, kind]
    k_all[:rows] = k_ref[0]
    v_all[:rows] = v_ref[0]
    for j in range(tiles):
        slot = src_ref[j]
        at = rows + j * KT
        k_all[at : at + KT] = load(slot, 0)
        v_all[at : at + KT] = load(slot, 1)
    q = q_ref[0]
    do = do_ref[...]
    scores = lax.dot_general(
        k_all[...], q, (((1,), (1,)), ((), ())), preferred_element_type=jnp.float32
    )
    row = lax.broadcasted_iota(jnp.int32, (total, rows), 0)
    scores = jnp.where(row < rows + num_ref[0] * KT, scores, -1e30)
    top = jnp.max(scores, axis=0, keepdims=True)
    weight = jnp.exp2((scores - top) * (scale * math.log2(math.e)))
    probs = weight * (1.0 / jnp.sum(weight, axis=0, keepdims=True))
    dprob = lax.dot_general(
        v_all[...], do, (((1,), (1,)), ((), ())), preferred_element_type=jnp.float32
    )
    delta = jnp.sum(probs * dprob, axis=0, keepdims=True)
    dscore = (probs * (dprob - delta) * scale).astype(jnp.bfloat16)
    probs_b = probs.astype(jnp.bfloat16)
    dq_ref[0] = lax.dot_general(
        dscore, k_all[...], (((0,), (0,)), ((), ())), preferred_element_type=jnp.float32
    ).astype(jnp.bfloat16)
    for kind, (left, right) in enumerate(((dscore, q), (probs_b, do))):
        part = jnp.dot(left, right, preferred_element_type=jnp.float32)
        own_ref[kind, 0] = part[:rows]
        far = part[rows:].astype(jnp.bfloat16)
        for j in range(tiles):
            out_ref[dst_ref[j], 0, kind] = far[j * KT : (j + 1) * KT]


def attend(src, dst, num, q, do, keys, values, fars, first, earlier=()):
    heads, rows, _ = q.shape
    tiles = src.shape[0]
    parts = len(fars)
    each, here = fars[0].shape[:2]
    slots = parts * each
    total = rows + tiles * KT
    own = pl.BlockSpec((1, rows, HD), lambda h, *_: (first + h, 0, 0))
    return pl.pallas_call(
        functools.partial(attend_kernel, tiles, parts),
        out_shape=(
            jax.ShapeDtypeStruct((heads, rows, HD), jnp.bfloat16),
            jax.ShapeDtypeStruct((2, heads, rows, HD), jnp.float32),
            jax.ShapeDtypeStruct((slots, heads, 2, KT, HD), jnp.bfloat16),
        ),
        grid_spec=pltpu.PrefetchScalarGridSpec(
            num_scalar_prefetch=3,
            grid=(here,),
            in_specs=[own, pl.BlockSpec((rows, HD), lambda h, *_: (0, first + h)), own, own]
            + [pl.BlockSpec((each, 1, 2, KT, HD), lambda h, *_: (0, h, 0, 0, 0))] * parts
            + [pl.BlockSpec(memory_space=pl.ANY)] * len(earlier),
            out_specs=(
                own,
                pl.BlockSpec((2, 1, rows, HD), lambda h, *_: (0, first + h, 0, 0)),
                pl.BlockSpec((slots, 1, 2, KT, HD), lambda h, *_: (0, first + h, 0, 0, 0)),
            ),
            scratch_shapes=[
                pltpu.VMEM((total, HD), jnp.bfloat16),
                pltpu.VMEM((total, HD), jnp.bfloat16),
            ]
            + ([pltpu.VMEM((slots, 2, KT, HD), jnp.bfloat16)] if parts > 1 else []),
        ),
        input_output_aliases={7 + parts + i: i for i in range(len(earlier))},
        compiler_params=PARAMS,
    )(src, dst, num, q, do, keys, values, *fars, *earlier)


def settle_kernel(asked_ref, own_ref, back_ref, dk_ref, dv_ref, *accs):
    slots, heads = back_ref.shape[:2]
    rows = own_ref.shape[2]
    for h in range(heads):
        for kind in range(2):
            accs[h * 2 + kind][:rows] = own_ref[kind, h]
    for s in range(slots):
        asked = asked_ref[s]
        at = tile_rows(jnp.where(asked >= 0, asked, rows // KT))
        for h in range(heads):
            for kind in range(2):
                accs[h * 2 + kind][at] += back_ref[s, h, kind].astype(jnp.float32)
    for h in range(heads):
        for kind, out in enumerate((dk_ref, dv_ref)):
            out[h] = accs[h * 2 + kind][:rows].astype(jnp.bfloat16)


def settle(asked, own, back, block=2):
    _, heads, rows, _ = own.shape
    slots = back.shape[0]
    out = pl.BlockSpec((block, rows, HD), lambda h, *_: (h, 0, 0))
    return pl.pallas_call(
        settle_kernel,
        out_shape=[jax.ShapeDtypeStruct((heads, rows, HD), jnp.bfloat16)] * 2,
        grid_spec=pltpu.PrefetchScalarGridSpec(
            num_scalar_prefetch=1,
            grid=(heads // block,),
            in_specs=[
                pl.BlockSpec((2, block, rows, HD), lambda h, *_: (0, h, 0, 0)),
                pl.BlockSpec((slots, block, 2, KT, HD), lambda h, *_: (0, h, 0, 0, 0)),
            ],
            out_specs=[out, out],
            scratch_shapes=[pltpu.VMEM((rows + KT, HD), jnp.float32)] * (2 * block),
        ),
        compiler_params=PARAMS,
    )(asked, own, back)


def project_kernel(me_ref, own_ref, flip_ref, both_ref, w_ref, out_ref, acc):
    step = pl.program_id(0)

    def add(rows):
        part = lax.dot_general(rows, w_ref[...], (((1,), (1,)), ((), ())), preferred_element_type=jnp.float32)
        acc[...] = jnp.where(step == 0, part, acc[...] + part)

    @pl.when(step == 0)
    def _():
        add(own_ref[...])

    @pl.when(step == 1)
    def _():
        add(flip_ref[...])

    @pl.when(step == 2)
    def _():
        add(both_ref[0])

    @pl.when(step == 3)
    def _():
        add(both_ref[1])
        out_ref[...] = acc[...].astype(out_ref.dtype)


def columns(grad_out):
    swap = [(0, 1), (1, 0)]
    flip = lax.ppermute(grad_out, HEAD[0], swap)
    return flip, lax.ppermute(jnp.stack([grad_out, flip]), HEAD[1], swap)


def project(grad_out, flip, both, w_out):
    rows, width = grad_out.shape
    out_width = w_out.shape[0]
    me = (lax.axis_index(HEAD[0]) * 2 + lax.axis_index(HEAD[1])).astype(jnp.int32).reshape(1)
    block = lambda i, m: (0, m[0] ^ (i // 2 + (i % 2) * 2))
    return pl.pallas_call(
        project_kernel,
        out_shape=jax.ShapeDtypeStruct((rows, out_width), jnp.bfloat16),
        grid_spec=pltpu.PrefetchScalarGridSpec(
            num_scalar_prefetch=1,
            grid=(4,),
            in_specs=[
                pl.BlockSpec((rows, width), lambda i, m: (0, 0)),
                pl.BlockSpec((rows, width), lambda i, m: (0, 0)),
                pl.BlockSpec((2, rows, width), lambda i, m: (0, 0, 0)),
                pl.BlockSpec((out_width, width), block),
            ],
            out_specs=pl.BlockSpec((rows, out_width), lambda i, m: (0, 0)),
            scratch_shapes=[pltpu.VMEM((rows, out_width), jnp.float32)],
        ),
        compiler_params=pltpu.CompilerParams(vmem_limit_bytes=VMEM_LIMIT),
    )(me, grad_out, flip, both, w_out)


def along_z(value, step):
    count = lax.axis_size("z")
    return lax.ppermute(value, "z", [(i, (i + step) % count) for i in range(count)])


def across_plane(value, dx, dy):
    nx, ny = lax.axis_size("x_lo"), lax.axis_size("y")
    pairs = [(x * ny + y, (x + dx) % nx * ny + (y + dy) % ny) for x in range(nx) for y in range(ny)]
    return lax.ppermute(value, PLANE, pairs)


def shards(queries, keys, values, grad_out, w_out, crit):
    queries, keys, values = (a.transpose(1, 0, 2) for a in (queries, keys, values))
    heads, rows, _ = queries.shape
    tiles_here = rows // KT
    sizes = tuple(lax.axis_size(a) for a in TOK)
    nx, nz, ny = sizes
    count = nx * nz * ny
    x, z, y = (lax.axis_index(a).astype(jnp.int32) for a in TOK)
    pos = jnp.stack([x, z, y])
    place = (x * nz + z) * ny + y

    entries = jnp.concatenate([crit[0], jnp.stack([place * tiles_here - 1, (place + 1) * tiles_here])])
    used = (entries >= 0) & (entries < count * tiles_here)
    owner = jnp.where(used, entries // tiles_here, place)
    blocks = jnp.arange(count)
    want = jnp.max(
        jnp.where(used[None, :] & (owner[None, :] == blocks[:, None]), entries[None, :] % tiles_here, -1), axis=1
    )
    wanted = lax.all_to_all(
        want.reshape(nx, nz, ny).transpose(0, 2, 1).reshape(nx * ny, nz), PLANE, 0, 0, tiled=True
    )
    asked = lax.all_to_all(wanted.T, "z", 0, 0, tiled=True)
    asked = asked.reshape(nz, nx, ny).transpose(1, 0, 2).reshape(count)
    wanted = wanted.reshape(nx * ny * nz)

    ring = jnp.stack([keys[:RING], values[:RING]])
    up, down = along_z(ring, 1), along_z(ring, -1)
    held = [ring, up, down]
    up, down, wanted = lax.optimization_barrier((up, down, wanted))
    up, down = along_z(up, 1), along_z(down, -1)
    held += [up, down]
    up, down, asked = lax.optimization_barrier((up, down, asked))
    up, down = along_z(up, 1), along_z(down, -1)
    held += [up, down]
    held += [along_z(up[0], 1), along_z(down[1], -1)]

    flip, both = columns(grad_out)

    tiles = entries.shape[0]
    order = jnp.arange(tiles)
    rank = jnp.sum(used[None, :] & (order[None, :] < order[:, None]), axis=1)
    slot = jnp.max(jnp.where(used[None, :] & (rank[None, :] == order[:, None]), owner[None, :], -1), axis=1)
    slot = jnp.where(slot >= 0, slot, place).astype(jnp.int32)
    number = jnp.sum(used.astype(jnp.int32)).reshape(1)
    dx, dz, dy = (x - slot // (nz * ny)) % nx, (slot // ny - z) % nz, (y - slot % ny) % ny
    rank_of = sum(jnp.where(dz == step % nz, s, 0) for s, step in enumerate(STEPS))
    plane_slot = ((dx * ny + dy) * len(STEPS) + rank_of).astype(jnp.int32)

    served = serve_all(asked, keys, values, RING)
    served, held, flip, both = lax.optimization_barrier((served, held, flip, both))
    far = lax.all_to_all(served, TOK, 0, 0, tiled=True)
    near = serve_plane(sizes, wanted, pos, held)
    near = [near[0]] + [across_plane(near[r], r // ny, r % ny) for r in range(1, nx * ny)]
    d_attn = project(grad_out, flip, both, w_out)

    done = attend(plane_slot, slot, number, queries, d_attn, keys, values, near, 0)
    grad_q, own, out = attend(slot, slot, number, queries, d_attn, keys, values, [far], RING, done)
    back = lax.all_to_all(out, TOK, 0, 0, tiled=True)
    grad_k, grad_v = settle(asked, own, back)
    return tuple(a.transpose(1, 0, 2) for a in (grad_q, grad_k, grad_v))


def solution(mesh):
    fine = Mesh(mesh.devices.reshape(2, 8, 4, 2, 2), TOK + HEAD)
    return jax.shard_map(
        shards,
        mesh=fine,
        in_specs=(
            P(TOK, HEAD, None),
            P(TOK, HEAD, None),
            P(TOK, HEAD, None),
            P(TOK, HEAD),
            P(HEAD, None),
            P(TOK, None),
        ),
        out_specs=(P(TOK, HEAD, None), P(TOK, HEAD, None), P(TOK, HEAD, None)),
        check_vma=False,
    )
```

time: 221 us -> 203 us (0.919)
  waiting for transfers between devices: 129 us -> 19.9 us
  blocking collectives: 0 us -> 99.6 us
  starting transfers between devices: 44.6 us -> 37.7 us
  Pallas kernels: 29.5 us -> 23.5 us
  local copies, waits for them, and re-layouts: 12.7 us -> 16.6 us
    all_to_all x5 -> x1, waiting for transfers between devices: 111 us -> 0.01 us  [shards(): far = lax.all_to_all(served, TOK, 0, 0, tiled=True)]
    all_to_all x0 -> x3, blocking collectives: none -> 99.6 us  [the longest x1 74.4 us: shards(): back = lax.all_to_all(out, TOK, 0, 0, tiled=True)]
    all_to_all x5 -> x1, starting transfers between devices: 41.8 us -> 7.88 us  [shards(): far = lax.all_to_all(served, TOK, 0, 0, tiled=True)]
    ppermute x2 -> x17, starting transfers between devices: 2.82 us -> 29.9 us  [the longest x7 16.2 us: across_plane(): return lax.ppermute(value, PLANE, pairs)]
    pallas_call x6 -> x5, Pallas kernels: 24.9 us -> 19.1 us  [the longest x2 12.9 us: attend(): pl.pallas_call(functools.partial(attend_kernel, tiles, parts), out_shape=...]
    unnamed x34 -> x50, local copies, waits for them, and re-layouts: 9.54 us -> 14.3 us
    ppermute x2 -> x17, waiting for transfers between devices: 17.3 us -> 19.9 us  [the longest x7 14 us: across_plane(): return lax.ppermute(value, PLANE, pairs)]
  transfers between devices with their start and end apart: 7 -> 18, of which waited for: 7 -> 7; matrix products, arithmetic and copies ran while one was open for 3% -> 2% of each run, Pallas kernels for 11% -> 7%
where the time goes in v3:
time: 203 us; the launch traced here: 202 us
  blocking collectives  99.6 us (49%)
  starting transfers between devices  37.7 us (19%)
  Pallas kernels  23.5 us (12%)
  waiting for transfers between devices  19.9 us (10%)
  local copies, waits for them, and re-layouts  16.6 us (8%)
  other arithmetic  3.59 us (2%)
    all_to_all x1, blocking collectives, shards(): back = lax.all_to_all(out, TOK, 0, 0, tiled=True)  74.4 us
    ppermute x7, starting transfers between devices, across_plane(): return lax.ppermute(value, PLANE, pairs)  16.2 us
    unnamed x50, local copies, waits for them, and re-layouts  14.3 us
    ppermute x7, waiting for transfers between devices, across_plane(): return lax.ppermute(value, PLANE, pairs)  14 us
    all_to_all x1, blocking collectives, shards(): asked = lax.all_to_all(wanted.T, 'z', 0, 0, tiled=True)  13.9 us
    pallas_call x2, Pallas kernels, attend(): pl.pallas_call(functools.partial(attend_kernel, tiles, parts), out_shape=...  12.9 us
    all_to_all x1, blocking collectives, shards(): lax.all_to_all(want.reshape(nx, nz, ny).transpose(0, 2, 1).reshape(nx * n...  11.4 us
    ppermute x8, starting transfers between devices, along_z(): lax.ppermute(value, 'z', [(i, (i + step) % count) for i in range(count)])  10.8 us
  transfers between devices with their start and end apart: 18, of which 7 were waited for; matrix products, arithmetic and copies ran while one was open for 2% of the time, Pallas kernels for 7%

profile of v3, /device:TPU:32, one launch (start us, length us, event | category | flops | bytes accessed | tf_op | source)
XLA Modules:
  0.0 201.7 jit_solution(9462893360339282642)
XLA Ops:
  0.7 1.1 slice_bitcast_fusion.2
  1.8 1.9 collective-permute-start.1
  3.7 0.2 collective-permute-start
  3.9 0.7 and_select_fusion.6
  4.7 0.6 convert_reduce_fusion.1
  5.3 0.1 select_reduce_fusion
  5.4 0.1 reshape.266
  5.5 0.1 copy.26
  5.6 11.4 %all_to_all.31 = s32[8,1,8]{2,1,0:T(1,128)S(1)} all-to-all(s32[8,1,8]{2,1,0:T(1,128)S(1)} %bitcast.51), channel_id=1, replica_groups=mesh['x_lo'=2,'z'=8,'y'=4,'x_hi'=2,'core'=2] {'x_lo','y'}, dimensions={0} | all-to-all | bytes 512 | tf_op jit(solution)/shard_map/all_to_all | solution.py:289
  16.9 0.5 broadcast.109
  17.4 0.7 reduce.3
  18.1 0.1 reshape.267.wanted_ref
  18.2 2.0 collective-permute-start.2
  20.2 0.7 copy-done.15
  20.9 2.0 %collective-permute-start.3 = (bf16[2,3,256,128]{3,2,1,0:T(8,128)(2,1)S(1)}, bf16[2,3,256,128]{3,2,1,0:T(8,128)(2,1)S(1)}, u32[]{:S(2)}, u32[]{:S(2)}) collective-permute-start(bf16[2,3,256,128]{3,2,1,0:T(8,128)(2,1)S(1)} %collective-permute-done.1.refs_2_), channel_id=1, source_target_pairs={{0,112},{16,0},{32,16},{48,32},{64,48},{80,64},{96,80},{112,96},{1... | collective-permute-start | bytes 1179656 | tf_op jit(solution)/shard_map/ppermute | solution.py:262
  23.0 0.7 copy-done.13
  23.7 2.7 %collective-permute-start.8 = (bf16[256,768]{1,0:T(8,128)(2,1)}, bf16[256,768]{1,0:T(8,128)(2,1)S(1)}, u32[]{:S(2)}, u32[]{:S(2)}) collective-permute-start(bf16[256,768]{1,0:T(8,128)(2,1)} %own_ref.1), channel_id=1, source_target_pairs={{0,2},{2,0},{1,3},{3,1},{4,6},{6,4},{5,7},{7,5},{8,10},{10,8},{9,1... | collective-permute-start | bytes 1179656 | tf_op jit(solution)/shard_map/ppermute | solution.py:232
  26.5 13.9 %all_to_all.32 = s32[8,1,8]{2,1,0:T(1,128)S(1)} all-to-all(s32[8,1,8]{2,1,0:T(1,128)S(1)} %copy.29), channel_id=1, replica_groups=mesh['x_lo'=2,'z'=8,'y'=4,'x_hi'=2,'core'=2] {'z'}, dimensions={0} | all-to-all | bytes 512 | tf_op jit(solution)/shard_map/all_to_all | solution.py:292
  40.5 0.1 copy.31
  40.6 0.1 reshape.269.asked_ref
  40.7 0.6 collective-permute-start.4
  41.3 1.5 collective-permute-start.5
  42.8 1.1 pad_maximum_fusion
  43.9 0.1 collective-permute-start.9
  44.0 4.9 %collective-permute-done.4.refs_5_ = bf16[2,3,256,128]{3,2,1,0:T(8,128)(2,1)S(1)} collective-permute-done((bf16[2,3,256,128]{3,2,1,0:T(8,128)(2,1)S(1)}, bf16[2,3,256,128]{3,2,1,0:T(8,128)(2,1)S(1)}, u32[]{:S(2)}, u32[]{:S(2)}) %collective-permute-start.4) | collective-permute-done | bytes 393248 | tf_op jit(solution)/shard_map/ppermute | solution.py:262
  48.9 1.6 collective-permute-start.6
  50.5 0.1 collective-permute-done.5.refs_6_
  50.6 1.0 collective-permute-start.7
  51.6 2.3 %shard_map.85 = bf16[64,3,2,16,128]{4,3,2,1,0:T(8,128)(2,1)} custom-call(s32[64]{0:T(128)S(1)} %reshape.269.asked_ref, bf16[6,256,128]{2,1,0:T(8,128)(2,1)S(1)} %bitcast.37, bf16[6,256,128]{2,1,0:T(8,128)(2,1)S(1)} %bitcast.41), custom_call_target="tpu_custom_call" | custom-call | tf_op jit(solution)/shard_map/pallas_call | solution.py:41
  53.9 0.9 copy-done.11
  54.8 0.3 collective-permute-done.6.refs_7_
  55.1 0.7 copy-done.21
  55.8 0.6 collective-permute-done.7.refs_8_
  56.4 0.7 copy-done.23
  57.1 7.9 %all-to-all-start.2 = ((bf16[64,3,2,16,128]{4,3,2,1,0:T(8,128)(2,1)}), bf16[64,3,2,16,128]{4,3,2,1,0:T(8,128)(2,1)S(1)}, u32[]{:S(2)}, u32[]{:S(2)}) async-start(bf16[64,3,2,16,128]{4,3,2,1,0:T(8,128)(2,1)} %shard_map.85), calls=%async_computation.2 | async-start | bytes 3145728 | tf_op jit(solution)/shard_map/all_to_all | solution.py:321
  64.9 0.1 pad_add_fusion.1.pos_ref
  65.0 1.0 copy-done.10
  66.0 1.0 copy-done.14
  67.0 1.0 copy-done.16
  68.0 1.0 copy-done.18
  69.0 1.0 copy-done.20
  70.0 0.9 copy-done.22
  70.9 0.9 copy-done.24
  71.9 0.8 shard_map.87
  72.7 1.5 collective-permute-start.10
  74.3 2.7 %collective-permute-start.11 = (bf16[8,3,2,16,128]{4,3,2,1,0:T(8,128)(2,1)S(1)}, bf16[8,3,2,16,128]{4,3,2,1,0:T(8,128)(2,1)S(1)}, u32[]{:S(2)}, u32[]{:S(2)}) collective-permute-start(bf16[8,3,2,16,128]{4,3,2,1,0:T(8,128)(2,1)S(1)} %get-tuple-element.57), channel_id=1, source_target_pairs={{0,8},{4,12},{8,0},{12,4},{128,136},{132,140},{136,128},{140,132},... | collective-permute-start | bytes 589832 | tf_op jit(solution)/shard_map/ppermute | solution.py:268
  76.9 0.1 convert_reduce_fusion
  77.0 0.1 select_reduce_fusion.1
  77.2 1.5 collective-permute-start.12
  78.7 1.6 collective-permute-start.13
  80.3 0.4 collective-permute-start.14
  80.7 5.5 %collective-permute-done.10.refs_1_ = bf16[8,3,2,16,128]{4,3,2,1,0:T(8,128)(2,1)S(1)} collective-permute-done((bf16[8,3,2,16,128]{4,3,2,1,0:T(8,128)(2,1)S(1)}, bf16[8,3,2,16,128]{4,3,2,1,0:T(8,128)(2,1)S(1)}, u32[]{:S(2)}, u32[]{:S(2)}) %collective-permute-start.10) | collective-permute-done | bytes 196640 | tf_op jit(solution)/shard_map/ppermute | solution.py:268
  86.3 8.4 %collective-permute-start.15 = (bf16[8,3,2,16,128]{4,3,2,1,0:T(8,128)(2,1)S(1)}, bf16[8,3,2,16,128]{4,3,2,1,0:T(8,128)(2,1)S(1)}, u32[]{:S(2)}, u32[]{:S(2)}) collective-permute-start(bf16[8,3,2,16,128]{4,3,2,1,0:T(8,128)(2,1)S(1)} %get-tuple-element.61), channel_id=1, source_target_pairs={{0,136},{4,140},{8,128},{12,132},{128,8},{132,12},{136,0},{140,4},... | collective-permute-start | bytes 589832 | tf_op jit(solution)/shard_map/ppermute | solution.py:268
  94.7 6.4 %collective-permute-done.11.refs_2_ = bf16[8,3,2,16,128]{4,3,2,1,0:T(8,128)(2,1)S(1)} collective-permute-done((bf16[8,3,2,16,128]{4,3,2,1,0:T(8,128)(2,1)S(1)}, bf16[8,3,2,16,128]{4,3,2,1,0:T(8,128)(2,1)S(1)}, u32[]{:S(2)}, u32[]{:S(2)}) %collective-permute-start.11) | collective-permute-done | bytes 196640 | tf_op jit(solution)/shard_map/ppermute | solution.py:268
  101.2 4.4 %shard_map.86.do_ref = bf16[256,768]{1,0:T(8,128)(2,1)S(1)} custom-call(s32[1]{0:T(128)} %bitcast.5.me_ref, bf16[256,768]{1,0:T(8,128)(2,1)S(1)} %copy-done.8, bf16[256,768]{1,0:T(8,128)(2,1)S(1)} %collective-permute-done.8.flip_ref, bf16[2,256,768]{2,1,0:T(8,128)(2,1)S(1)} %copy-done.12, bf16[768,3072]{1,0:T(8,128)(2,1)} %w_ref.1), custom_call_target="tpu_custom_call" | custom-call | tf_op jit(solution)/shard_map/pallas_call | solution.py:241
  105.6 2.1 %collective-permute-done.16.refs_7_ = bf16[8,3,2,16,128]{4,3,2,1,0:T(8,128)(2,1)S(1)} collective-permute-done((bf16[8,3,2,16,128]{4,3,2,1,0:T(8,128)(2,1)S(1)}, bf16[8,3,2,16,128]{4,3,2,1,0:T(8,128)(2,1)S(1)}, u32[]{:S(2)}, u32[]{:S(2)}) %collective-permute-start.16) | collective-permute-done | bytes 196640 | tf_op jit(solution)/shard_map/ppermute | solution.py:268
  107.7 6.5 %shard_map.88 = (bf16[6,256,128]{2,1,0:T(8,128)(2,1)}, f32[2,6,256,128]{3,2,1,0:T(8,128)S(1)}, bf16[64,6,2,16,128]{4,3,2,1,0:T(8,128)(2,1)}) custom-call(s32[42]{0:T(128)S(1)} %get-tuple-element.71.src_ref, s32[42]{0:T(128)S(1)} %get-tuple-element.72.dst_ref.src_ref, s32[1]{0:T(128)} %bitcast.3.num_ref, bf16[6,256,128]{2,1,0:T(8,128)(2,1)S(1)} %bitcast.44, ...), custom_call_target="tpu_custom_call" | custom-call | tf_op jit(solution)/shard_map/pallas_call | solution.py:138
  114.2 0.7 copy-done.4
  114.9 1.0 copy-done.3
  115.9 1.0 copy-done.5
  116.9 1.0 copy-done.7
  117.9 6.4 %shard_map.89 = (bf16[6,256,128]{2,1,0:T(8,128)(2,1)}, f32[2,6,256,128]{3,2,1,0:T(8,128)S(1)}, bf16[64,6,2,16,128]{4,3,2,1,0:T(8,128)(2,1)}) custom-call(s32[42]{0:T(128)S(1)} %get-tuple-element.72.dst_ref.src_ref, s32[42]{0:T(128)S(1)} %get-tuple-element.72.dst_ref.src_ref, ...), custom_call_target="tpu_custom_call", output_to_operand_aliasing={{0}: (8, {}), {1}: (9, {}), {2}: (10, {})} | custom-call | tf_op jit(solution)/shard_map/pallas_call | solution.py:138
  124.4 74.4 %all_to_all.33.back_ref = bf16[64,6,2,16,128]{4,3,2,1,0:T(8,128)(2,1)S(1)} all-to-all(bf16[64,6,2,16,128]{4,3,2,1,0:T(8,128)(2,1)} %get-tuple-element.68), channel_id=1, replica_groups=mesh['x_lo'=2,'z'=8,'y'=4,'x_hi'=2,'core'=2] {'x_lo','z','y'}, dimensions={0} | all-to-all | bytes 6291456 | tf_op jit(solution)/shard_map/all_to_all | solution.py:328
  198.7 3.0 %shard_map.90 = (bf16[6,256,128]{2,1,0:T(8,128)(2,1)}, bf16[6,256,128]{2,1,0:T(8,128)(2,1)}) custom-call(s32[64]{0:T(128)S(1)} %reshape.269.asked_ref, f32[2,6,256,128]{3,2,1,0:T(8,128)S(1)} %get-tuple-element.67.own_ref, bf16[64,6,2,16,128]{4,3,2,1,0:T(8,128)(2,1)S(1)} %all_to_all.33.back_ref), custom_call_target="tpu_custom_call" | custom-call | tf_op jit(solution)/shard_map/pallas_call | solution.py:188
  (53 shorter events, 0.3 us)
Async XLA Ops:
  0.6 51.0 %copy-start.1 = (bf16[256,6,128]{2,0,1:T(8,128)(2,1)S(1)}, bf16[256,6,128]{2,0,1:T(8,128)(2,1)}, u32[]{:S(2)}) copy-start(bf16[256,6,128]{2,0,1:T(8,128)(2,1)} %param.8) | copy-start | bytes 1179652
  0.6 51.0 %copy-start = (bf16[256,6,128]{2,0,1:T(8,128)(2,1)S(1)}, bf16[256,6,128]{2,0,1:T(8,128)(2,1)}, u32[]{:S(2)}) copy-start(bf16[256,6,128]{2,0,1:T(8,128)(2,1)} %param.7) | copy-start | bytes 1179652
  1.8 16.4 %collective-permute-start.1 = (bf16[2,3,256,128]{3,2,1,0:T(8,128)(2,1)S(1)}, bf16[2,3,256,128]{3,2,1,0:T(8,128)(2,1)S(1)}, u32[]{:S(2)}, u32[]{:S(2)}) collective-permute-start(bf16[2,3,256,128]{3,2,1,0:T(8,128)(2,1)S(1)} %pad_maximum_fusion.1.refs_0_), channel_id=1, source_target_pairs={{0,112},{16,0},{32,16},{48,32},{64,48},{80,64},{96,80},{112,96},{1... | collective-permute-start | bytes 1179656 | tf_op jit(solution)/shard_map/ppermute | solution.py:262
  3.7 14.5 %collective-permute-start = (bf16[2,3,256,128]{3,2,1,0:T(8,128)(2,1)S(1)}, bf16[2,3,256,128]{3,2,1,0:T(8,128)(2,1)S(1)}, u32[]{:S(2)}, u32[]{:S(2)}) collective-permute-start(bf16[2,3,256,128]{3,2,1,0:T(8,128)(2,1)S(1)} %pad_maximum_fusion.1.refs_0_), channel_id=1, source_target_pairs={{0,16},{16,32},{32,48},{48,64},{64,80},{80,96},{96,112},{112,0},{1... | collective-permute-start | bytes 1179656 | tf_op jit(solution)/shard_map/ppermute | solution.py:262
  18.2 22.5 %collective-permute-start.2 = (bf16[2,3,256,128]{3,2,1,0:T(8,128)(2,1)S(1)}, bf16[2,3,256,128]{3,2,1,0:T(8,128)(2,1)S(1)}, u32[]{:S(2)}, u32[]{:S(2)}) collective-permute-start(bf16[2,3,256,128]{3,2,1,0:T(8,128)(2,1)S(1)} %collective-permute-done.refs_1_), channel_id=1, source_target_pairs={{0,16},{16,32},{32,48},{48,64},{64,80},{80,96},{96,112},{112,0},{1... | collective-permute-start | bytes 1179656 | tf_op jit(solution)/shard_map/ppermute | solution.py:262
  20.2 0.7 copy-start.15
  20.9 19.7 %collective-permute-start.3 = (bf16[2,3,256,128]{3,2,1,0:T(8,128)(2,1)S(1)}, bf16[2,3,256,128]{3,2,1,0:T(8,128)(2,1)S(1)}, u32[]{:S(2)}, u32[]{:S(2)}) collective-permute-start(bf16[2,3,256,128]{3,2,1,0:T(8,128)(2,1)S(1)} %collective-permute-done.1.refs_2_), channel_id=1, source_target_pairs={{0,112},{16,0},{32,16},{48,32},{64,48},{80,64},{96,80},{112,96},{1... | collective-permute-start | bytes 1179656 | tf_op jit(solution)/shard_map/ppermute | solution.py:262
  23.0 0.7 copy-start.13
  23.7 19.1 %collective-permute-start.8 = (bf16[256,768]{1,0:T(8,128)(2,1)}, bf16[256,768]{1,0:T(8,128)(2,1)S(1)}, u32[]{:S(2)}, u32[]{:S(2)}) collective-permute-start(bf16[256,768]{1,0:T(8,128)(2,1)} %own_ref.1), channel_id=1, source_target_pairs={{0,2},{2,0},{1,3},{3,1},{4,6},{6,4},{5,7},{7,5},{8,10},{10,8},{9,1... | collective-permute-start | bytes 1179656 | tf_op jit(solution)/shard_map/ppermute | solution.py:232
  40.7 16.4 %copy-start.17 = (bf16[2,3,256,128]{3,2,1,0:T(8,128)(2,1)}, bf16[2,3,256,128]{3,2,1,0:T(8,128)(2,1)S(1)}, u32[]{:S(2)}) copy-start(bf16[2,3,256,128]{3,2,1,0:T(8,128)(2,1)S(1)} %collective-permute-done.2.refs_3_) | copy-start | bytes 1179652
  40.7 16.4 %copy-start.19 = (bf16[2,3,256,128]{3,2,1,0:T(8,128)(2,1)}, bf16[2,3,256,128]{3,2,1,0:T(8,128)(2,1)S(1)}, u32[]{:S(2)}) copy-start(bf16[2,3,256,128]{3,2,1,0:T(8,128)(2,1)S(1)} %collective-permute-done.3.refs_4_) | copy-start | bytes 1179652
  40.7 8.2 %collective-permute-start.4 = (bf16[2,3,256,128]{3,2,1,0:T(8,128)(2,1)S(1)}, bf16[2,3,256,128]{3,2,1,0:T(8,128)(2,1)S(1)}, u32[]{:S(2)}, u32[]{:S(2)}) collective-permute-start(bf16[2,3,256,128]{3,2,1,0:T(8,128)(2,1)S(1)} %collective-permute-done.2.refs_3_), channel_id=1, source_target_pairs={{0,16},{16,32},{32,48},{48,64},{64,80},{80,96},{96,112},{112,0},{1... | collective-permute-start | bytes 1179656 | tf_op jit(solution)/shard_map/ppermute | solution.py:262
  41.3 9.3 %collective-permute-start.5 = (bf16[2,3,256,128]{3,2,1,0:T(8,128)(2,1)S(1)}, bf16[2,3,256,128]{3,2,1,0:T(8,128)(2,1)S(1)}, u32[]{:S(2)}, u32[]{:S(2)}) collective-permute-start(bf16[2,3,256,128]{3,2,1,0:T(8,128)(2,1)S(1)} %collective-permute-done.3.refs_4_), channel_id=1, source_target_pairs={{0,112},{16,0},{32,16},{48,32},{64,48},{80,64},{96,80},{112,96},{1... | collective-permute-start | bytes 1179656 | tf_op jit(solution)/shard_map/ppermute | solution.py:262
  43.9 10.0 %collective-permute-start.9 = (bf16[2,256,768]{2,1,0:T(8,128)(2,1)S(1)}, bf16[2,256,768]{2,1,0:T(8,128)(2,1)S(1)}, u32[]{:S(2)}, u32[]{:S(2)}) collective-permute-start(bf16[2,256,768]{2,1,0:T(8,128)(2,1)S(1)} %pad_maximum_fusion), channel_id=1, source_target_pairs={{0,1},{1,0},{2,3},{3,2},{4,5},{5,4},{6,7},{7,6},{8,9},{9,8},{10,11... | collective-permute-start | bytes 2359304 | tf_op jit(solution)/shard_map/ppermute | solution.py:233
  48.9 6.2 %collective-permute-start.6 = (bf16[3,256,128]{2,1,0:T(8,128)(2,1)S(1)}, bf16[3,256,128]{2,1,0:T(8,128)(2,1)S(1)}, u32[]{:S(2)}, u32[]{:S(2)}) collective-permute-start(bf16[3,256,128]{2,1,0:T(8,128)(2,1)S(1)} %slice_bitcast_fusion.1), channel_id=1, source_target_pairs={{0,16},{16,32},{32,48},{48,64},{64,80},{80,96},{96,112},{112,0},{1... | collective-permute-start | bytes 589832 | tf_op jit(solution)/shard_map/ppermute | solution.py:262
  50.6 6.4 %copy-start.9 = (bf16[2,3,256,128]{3,2,1,0:T(8,128)(2,1)}, bf16[2,3,256,128]{3,2,1,0:T(8,128)(2,1)S(1)}, u32[]{:S(2)}) copy-start(bf16[2,3,256,128]{3,2,1,0:T(8,128)(2,1)S(1)} %collective-permute-done.5.refs_6_) | copy-start | bytes 1179652
  50.6 5.7 %collective-permute-start.7 = (bf16[3,256,128]{2,1,0:T(8,128)(2,1)S(1)}, bf16[3,256,128]{2,1,0:T(8,128)(2,1)S(1)}, u32[]{:S(2)}, u32[]{:S(2)}) collective-permute-start(bf16[3,256,128]{2,1,0:T(8,128)(2,1)S(1)} %slice_bitcast_fusion), channel_id=1, source_target_pairs={{0,112},{16,0},{32,16},{48,32},{64,48},{80,64},{96,80},{112,96},{1... | collective-permute-start | bytes 589832 | tf_op jit(solution)/shard_map/ppermute | solution.py:262
  53.9 47.2 %copy-start.8 = (bf16[256,768]{1,0:T(8,128)(2,1)S(1)}, bf16[256,768]{1,0:T(8,128)(2,1)}, u32[]{:S(2)}) copy-start(bf16[256,768]{1,0:T(8,128)(2,1)} %own_ref.1) | copy-start | bytes 1179652
  53.9 0.9 copy-start.11
  55.1 0.7 copy-start.21
  56.4 0.7 copy-start.23
  57.1 57.9 %all-to-all-start.2 = ((bf16[64,3,2,16,128]{4,3,2,1,0:T(8,128)(2,1)}), bf16[64,3,2,16,128]{4,3,2,1,0:T(8,128)(2,1)S(1)}, u32[]{:S(2)}, u32[]{:S(2)}) async-start(bf16[64,3,2,16,128]{4,3,2,1,0:T(8,128)(2,1)} %shard_map.85), calls=%async_computation.2 | async-start | bytes 3145728 | tf_op jit(solution)/shard_map/all_to_all | solution.py:321
  65.0 1.0 copy-start.10
  66.0 1.0 copy-start.14
  67.0 1.0 copy-start.16
  68.0 1.0 copy-start.18
  69.0 1.0 copy-start.20
  70.0 0.9 copy-start.22
  70.9 0.9 copy-start.24
  71.9 29.3 %copy-start.12 = (bf16[2,256,768]{2,1,0:T(8,128)(2,1)S(1)}, bf16[2,256,768]{2,1,0:T(8,128)(2,1)}, u32[]{:S(2)}) copy-start(bf16[2,256,768]{2,1,0:T(8,128)(2,1)} %copy-done.11) | copy-start | bytes 2359300
  72.7 13.6 %collective-permute-start.10 = (bf16[8,3,2,16,128]{4,3,2,1,0:T(8,128)(2,1)S(1)}, bf16[8,3,2,16,128]{4,3,2,1,0:T(8,128)(2,1)S(1)}, u32[]{:S(2)}, u32[]{:S(2)}) collective-permute-start(bf16[8,3,2,16,128]{4,3,2,1,0:T(8,128)(2,1)S(1)} %get-tuple-element.56), channel_id=1, source_target_pairs={{0,4},{4,8},{8,12},{12,0},{128,132},{132,136},{136,140},{140,128},... | collective-permute-start | bytes 589832 | tf_op jit(solution)/shard_map/ppermute | solution.py:268
  74.3 26.9 %collective-permute-start.11 = (bf16[8,3,2,16,128]{4,3,2,1,0:T(8,128)(2,1)S(1)}, bf16[8,3,2,16,128]{4,3,2,1,0:T(8,128)(2,1)S(1)}, u32[]{:S(2)}, u32[]{:S(2)}) collective-permute-start(bf16[8,3,2,16,128]{4,3,2,1,0:T(8,128)(2,1)S(1)} %get-tuple-element.57), channel_id=1, source_target_pairs={{0,8},{4,12},{8,0},{12,4},{128,136},{132,140},{136,128},{140,132},... | collective-permute-start | bytes 589832 | tf_op jit(solution)/shard_map/ppermute | solution.py:268
  77.2 28.4 %collective-permute-start.12 = (bf16[8,3,2,16,128]{4,3,2,1,0:T(8,128)(2,1)S(1)}, bf16[8,3,2,16,128]{4,3,2,1,0:T(8,128)(2,1)S(1)}, u32[]{:S(2)}, u32[]{:S(2)}) collective-permute-start(bf16[8,3,2,16,128]{4,3,2,1,0:T(8,128)(2,1)S(1)} %get-tuple-element.58), channel_id=1, source_target_pairs={{0,12},{4,0},{8,4},{12,8},{128,140},{132,128},{136,132},{140,136},... | collective-permute-start | bytes 589832 | tf_op jit(solution)/shard_map/ppermute | solution.py:268
  78.7 26.9 %collective-permute-start.13 = (bf16[8,3,2,16,128]{4,3,2,1,0:T(8,128)(2,1)S(1)}, bf16[8,3,2,16,128]{4,3,2,1,0:T(8,128)(2,1)S(1)}, u32[]{:S(2)}, u32[]{:S(2)}) collective-permute-start(bf16[8,3,2,16,128]{4,3,2,1,0:T(8,128)(2,1)S(1)} %get-tuple-element.59), channel_id=1, source_target_pairs={{0,128},{4,132},{8,136},{12,140},{128,0},{132,4},{136,8},{140,12},... | collective-permute-start | bytes 589832 | tf_op jit(solution)/shard_map/ppermute | solution.py:268
  80.3 25.3 %collective-permute-start.14 = (bf16[8,3,2,16,128]{4,3,2,1,0:T(8,128)(2,1)S(1)}, bf16[8,3,2,16,128]{4,3,2,1,0:T(8,128)(2,1)S(1)}, u32[]{:S(2)}, u32[]{:S(2)}) collective-permute-start(bf16[8,3,2,16,128]{4,3,2,1,0:T(8,128)(2,1)S(1)} %get-tuple-element.60), channel_id=1, source_target_pairs={{0,132},{4,136},{8,140},{12,128},{128,4},{132,8},{136,12},{140,0},... | collective-permute-start | bytes 589832 | tf_op jit(solution)/shard_map/ppermute | solution.py:268
  86.3 19.3 %collective-permute-start.15 = (bf16[8,3,2,16,128]{4,3,2,1,0:T(8,128)(2,1)S(1)}, bf16[8,3,2,16,128]{4,3,2,1,0:T(8,128)(2,1)S(1)}, u32[]{:S(2)}, u32[]{:S(2)}) collective-permute-start(bf16[8,3,2,16,128]{4,3,2,1,0:T(8,128)(2,1)S(1)} %get-tuple-element.61), channel_id=1, source_target_pairs={{0,136},{4,140},{8,128},{12,132},{128,8},{132,12},{136,0},{140,4},... | collective-permute-start | bytes 589832 | tf_op jit(solution)/shard_map/ppermute | solution.py:268
  101.1 6.6 %collective-permute-start.16 = (bf16[8,3,2,16,128]{4,3,2,1,0:T(8,128)(2,1)S(1)}, bf16[8,3,2,16,128]{4,3,2,1,0:T(8,128)(2,1)S(1)}, u32[]{:S(2)}, u32[]{:S(2)}) collective-permute-start(bf16[8,3,2,16,128]{4,3,2,1,0:T(8,128)(2,1)S(1)} %get-tuple-element.62), channel_id=1, source_target_pairs={{0,140},{4,128},{8,132},{12,136},{128,12},{132,0},{136,4},{140,8},... | collective-permute-start | bytes 589832 | tf_op jit(solution)/shard_map/ppermute | solution.py:268
  101.2 6.5 %copy-start.2 = (bf16[256,6,128]{2,0,1:T(8,128)(2,1)S(1)}, bf16[256,6,128]{2,0,1:T(8,128)(2,1)}, u32[]{:S(2)}) copy-start(bf16[256,6,128]{2,0,1:T(8,128)(2,1)} %param.8) | copy-start | bytes 1179652
  101.2 6.5 %copy-start.6 = (bf16[256,6,128]{2,0,1:T(8,128)(2,1)S(1)}, bf16[256,6,128]{2,0,1:T(8,128)(2,1)}, u32[]{:S(2)}) copy-start(bf16[256,6,128]{2,0,1:T(8,128)(2,1)} %param.6) | copy-start | bytes 1179652
  114.2 0.7 copy-start.4
  114.9 1.0 copy-start.3
  115.9 1.0 copy-start.5
  116.9 1.0 copy-start.7

commit v4 on v3

--- a/solution.py
+++ b/solution.py
@@ -14,12 +14,12 @@
 TOK = ("x_lo", "z", "y")
 PLANE = ("x_lo", "y")
 HEAD = ("x_hi", "core")
-VMEM_LIMIT = 48 * 1024 * 1024
+MIB = 1024 * 1024
 RING = 3
 STEPS = (0, -1, 1, -2, 2, -3, 3, 4)
-PARAMS = pltpu.CompilerParams(vmem_limit_bytes=VMEM_LIMIT)
-VMEM = pl.BlockSpec(memory_space=pltpu.VMEM)
-SMEM = pl.BlockSpec(memory_space=pltpu.SMEM)
+GROUP = 1
+SMALL = pltpu.CompilerParams(vmem_limit_bytes=16 * MIB)
+LARGE = pltpu.CompilerParams(vmem_limit_bytes=60 * MIB)
 
 
 def tile_rows(tile):
@@ -47,96 +47,98 @@
             in_specs=[whole, whole],
             out_specs=pl.BlockSpec((block, heads, 2, KT, HD), lambda i, a: (i, 0, 0, 0, 0)),
         ),
-        compiler_params=PARAMS,
+        compiler_params=SMALL,
     )(asked, keys, values)
 
 
 def serve_plane_kernel(sizes, wanted_ref, pos_ref, *refs):
     nx, nz, ny = sizes
-    held, outs = refs[: len(STEPS) + 1], refs[len(STEPS) + 1 :]
-    heads = outs[0].shape[1]
+    held, outs = refs[: -nx * ny], refs[-nx * ny :]
     for r in range(nx * ny):
         mate = lax.rem(pos_ref[0] + r // ny, nx) * ny + lax.rem(pos_ref[2] + r % ny, ny)
         for s, step in enumerate(STEPS):
             tile = wanted_ref[mate * nz + lax.rem(pos_ref[1] + step + nz, nz)]
             rows = tile_rows(jnp.maximum(tile, 0))
-            for h in range(heads):
-                for kind in range(2):
-                    if s < len(STEPS) - 1:
-                        outs[r][s, h, kind] = held[s][kind, h, rows, :]
-                    else:
-                        outs[r][s, h, kind] = held[s + kind][h, rows, :]
+            for kind in range(2):
+                if s < len(STEPS) - 1:
+                    outs[r][s, 0, kind] = held[s][kind, 0, rows, :]
+                else:
+                    outs[r][s, 0, kind] = held[s + kind][0, rows, :]
 
 
 def serve_plane(sizes, wanted, pos, held):
     mates = sizes[0] * sizes[2]
-    heads = held[0].shape[1]
+    _, heads, rows, _ = held[0].shape
+    pair = pl.BlockSpec((2, 1, rows, HD), lambda h, *_: (0, h, 0, 0))
+    one = pl.BlockSpec((1, rows, HD), lambda h, *_: (h, 0, 0))
     return pl.pallas_call(
         functools.partial(serve_plane_kernel, sizes),
         out_shape=[jax.ShapeDtypeStruct((len(STEPS), heads, 2, KT, HD), held[0].dtype)] * mates,
-        in_specs=[SMEM] * 2 + [VMEM] * len(held),
-        out_specs=[VMEM] * mates,
-        compiler_params=PARAMS,
+        grid_spec=pltpu.PrefetchScalarGridSpec(
+            num_scalar_prefetch=2,
+            grid=(heads,),
+            in_specs=[pair if h.ndim == 4 else one for h in held],
+            out_specs=[pl.BlockSpec((len(STEPS), 1, 2, KT, HD), lambda h, *_: (0, h, 0, 0, 0))] * mates,
+        ),
+        compiler_params=LARGE,
     )(wanted, pos, *held)
 
 
 def attend_kernel(tiles, parts, src_ref, dst_ref, num_ref, q_ref, do_ref, k_ref, v_ref, *refs):
-    fars, (dq_ref, own_ref, out_ref, k_all, v_all) = refs[:parts], refs[-5 - (parts > 1) :][:5]
+    fars, (dq_ref, own_ref, out_ref, k_all, v_all, staged) = refs[:parts], refs[-6:]
     rows = q_ref.shape[1]
     total = rows + tiles * KT
     scale = HD**-0.5
-    if parts > 1:
-        far_ref = refs[-1]
-        each = fars[0].shape[0]
-        for i in range(parts):
-            far_ref[i * each : (i + 1) * each] = fars[i][:, 0]
-        load = lambda slot, kind: far_ref[slot, kind]
-    else:
-        load = lambda slot, kind: fars[0][slot, 0, kind]
-    k_all[:rows] = k_ref[0]
-    v_all[:rows] = v_ref[0]
-    for j in range(tiles):
-        slot = src_ref[j]
-        at = rows + j * KT
-        k_all[at : at + KT] = load(slot, 0)
-        v_all[at : at + KT] = load(slot, 1)
-    q = q_ref[0]
-    do = do_ref[...]
-    scores = lax.dot_general(
-        k_all[...], q, (((1,), (1,)), ((), ())), preferred_element_type=jnp.float32
-    )
+    for h in range(GROUP):
+        k_all[h, :rows] = k_ref[h]
+        v_all[h, :rows] = v_ref[h]
+        start = 0
+        for far in fars:
+            staged[h, start : start + far.shape[0]] = far[:, h]
+            start += far.shape[0]
+        for j in range(tiles):
+            at = rows + j * KT
+            k_all[h, at : at + KT] = staged[h, src_ref[j], 0]
+            v_all[h, at : at + KT] = staged[h, src_ref[j], 1]
+
     row = lax.broadcasted_iota(jnp.int32, (total, rows), 0)
-    scores = jnp.where(row < rows + num_ref[0] * KT, scores, -1e30)
-    top = jnp.max(scores, axis=0, keepdims=True)
-    weight = jnp.exp2((scores - top) * (scale * math.log2(math.e)))
-    probs = weight * (1.0 / jnp.sum(weight, axis=0, keepdims=True))
-    dprob = lax.dot_general(
-        v_all[...], do, (((1,), (1,)), ((), ())), preferred_element_type=jnp.float32
-    )
-    delta = jnp.sum(probs * dprob, axis=0, keepdims=True)
-    dscore = (probs * (dprob - delta) * scale).astype(jnp.bfloat16)
-    probs_b = probs.astype(jnp.bfloat16)
-    dq_ref[0] = lax.dot_general(
-        dscore, k_all[...], (((0,), (0,)), ((), ())), preferred_element_type=jnp.float32
-    ).astype(jnp.bfloat16)
-    for kind, (left, right) in enumerate(((dscore, q), (probs_b, do))):
-        part = jnp.dot(left, right, preferred_element_type=jnp.float32)
-        own_ref[kind, 0] = part[:rows]
-        far = part[rows:].astype(jnp.bfloat16)
-        for j in range(tiles):
-            out_ref[dst_ref[j], 0, kind] = far[j * KT : (j + 1) * KT]
-
-
-def attend(src, dst, num, q, do, keys, values, fars, first, earlier=()):
+    inside = row < rows + num_ref[0] * KT
+    for h in range(GROUP):
+        q = q_ref[h]
+        do = do_ref[:, h * HD : (h + 1) * HD]
+        scores = lax.dot_general(
+            k_all[h], q, (((1,), (1,)), ((), ())), preferred_element_type=jnp.float32
+        )
+        scores = jnp.where(inside, scores, -1e30)
+        top = jnp.max(scores, axis=0, keepdims=True)
+        weight = jnp.exp2((scores - top) * (scale * math.log2(math.e)))
+        probs = weight * (1.0 / jnp.sum(weight, axis=0, keepdims=True))
+        dprob = lax.dot_general(
+            v_all[h], do, (((1,), (1,)), ((), ())), preferred_element_type=jnp.float32
+        )
+        delta = jnp.sum(probs * dprob, axis=0, keepdims=True)
+        dscore = (probs * (dprob - delta) * scale).astype(jnp.bfloat16)
+        probs_b = probs.astype(jnp.bfloat16)
+        dq_ref[h] = lax.dot_general(
+            k_all[h], dscore, (((0,), (0,)), ((), ())), preferred_element_type=jnp.float32
+        ).T.astype(jnp.bfloat16)
+        for kind, (left, right) in enumerate(((dscore, q), (probs_b, do))):
+            part = jnp.dot(left, right, preferred_element_type=jnp.float32)
+            own_ref[kind, h] = part[:rows]
+            far = part[rows:].astype(jnp.bfloat16)
+            for j in range(tiles):
+                out_ref[dst_ref[j], h, kind] = far[j * KT : (j + 1) * KT]
+
+
+def attend(src, dst, num, q, do, keys, values, fars, slots, first, earlier=()):
     heads, rows, _ = q.shape
     tiles = src.shape[0]
-    parts = len(fars)
-    each, here = fars[0].shape[:2]
-    slots = parts * each
+    held = sum(far.shape[0] for far in fars)
     total = rows + tiles * KT
-    own = pl.BlockSpec((1, rows, HD), lambda h, *_: (first + h, 0, 0))
-    return pl.pallas_call(
-        functools.partial(attend_kernel, tiles, parts),
+    start = first // GROUP
+    own = pl.BlockSpec((GROUP, rows, HD), lambda g, *_: (start + g, 0, 0))
+    return pl.pallas_call(
+        functools.partial(attend_kernel, tiles, len(fars)),
         out_shape=(
             jax.ShapeDtypeStruct((heads, rows, HD), jnp.bfloat16),
             jax.ShapeDtypeStruct((2, heads, rows, HD), jnp.float32),
@@ -144,23 +146,23 @@
         ),
         grid_spec=pltpu.PrefetchScalarGridSpec(
             num_scalar_prefetch=3,
-            grid=(here,),
-            in_specs=[own, pl.BlockSpec((rows, HD), lambda h, *_: (0, first + h)), own, own]
-            + [pl.BlockSpec((each, 1, 2, KT, HD), lambda h, *_: (0, h, 0, 0, 0))] * parts
+            grid=(fars[0].shape[1] // GROUP,),
+            in_specs=[own, pl.BlockSpec((rows, GROUP * HD), lambda g, *_: (0, start + g)), own, own]
+            + [pl.BlockSpec((far.shape[0], GROUP, 2, KT, HD), lambda g, *_: (0, g, 0, 0, 0)) for far in fars]
             + [pl.BlockSpec(memory_space=pl.ANY)] * len(earlier),
             out_specs=(
                 own,
-                pl.BlockSpec((2, 1, rows, HD), lambda h, *_: (0, first + h, 0, 0)),
-                pl.BlockSpec((slots, 1, 2, KT, HD), lambda h, *_: (0, first + h, 0, 0, 0)),
+                pl.BlockSpec((2, GROUP, rows, HD), lambda g, *_: (0, start + g, 0, 0)),
+                pl.BlockSpec((slots, GROUP, 2, KT, HD), lambda g, *_: (0, start + g, 0, 0, 0)),
             ),
             scratch_shapes=[
-                pltpu.VMEM((total, HD), jnp.bfloat16),
-                pltpu.VMEM((total, HD), jnp.bfloat16),
-            ]
-            + ([pltpu.VMEM((slots, 2, KT, HD), jnp.bfloat16)] if parts > 1 else []),
-        ),
-        input_output_aliases={7 + parts + i: i for i in range(len(earlier))},
-        compiler_params=PARAMS,
+                pltpu.VMEM((GROUP, total, HD), jnp.bfloat16),
+                pltpu.VMEM((GROUP, total, HD), jnp.bfloat16),
+                pltpu.VMEM((GROUP, held, 2, KT, HD), jnp.bfloat16),
+            ],
+        ),
+        input_output_aliases={7 + len(fars) + i: i for i in range(len(earlier))},
+        compiler_params=LARGE,
     )(src, dst, num, q, do, keys, values, *fars, *earlier)
 
 
@@ -198,7 +200,7 @@
             out_specs=[out, out],
             scratch_shapes=[pltpu.VMEM((rows + KT, HD), jnp.float32)] * (2 * block),
         ),
-        compiler_params=PARAMS,
+        compiler_params=SMALL,
     )(asked, own, back)
 
 
@@ -253,7 +255,7 @@
             out_specs=pl.BlockSpec((rows, out_width), lambda i, m: (0, 0)),
             scratch_shapes=[pltpu.VMEM((rows, out_width), jnp.float32)],
         ),
-        compiler_params=pltpu.CompilerParams(vmem_limit_bytes=VMEM_LIMIT),
+        compiler_params=LARGE,
     )(me, grad_out, flip, both, w_out)
 
 
@@ -319,12 +321,13 @@
     served = serve_all(asked, keys, values, RING)
     served, held, flip, both = lax.optimization_barrier((served, held, flip, both))
     far = lax.all_to_all(served, TOK, 0, 0, tiled=True)
+    d_attn = project(grad_out, flip, both, w_out)
+    held, d_attn = lax.optimization_barrier((held, d_attn))
     near = serve_plane(sizes, wanted, pos, held)
     near = [near[0]] + [across_plane(near[r], r // ny, r % ny) for r in range(1, nx * ny)]
-    d_attn = project(grad_out, flip, both, w_out)
-
-    done = attend(plane_slot, slot, number, queries, d_attn, keys, values, near, 0)
-    grad_q, own, out = attend(slot, slot, number, queries, d_attn, keys, values, [far], RING, done)
+
+    done = attend(slot, slot, number, queries, d_attn, keys, values, [far], count, RING)
+    grad_q, own, out = attend(plane_slot, slot, number, queries, d_attn, keys, values, near, count, 0, done)
     back = lax.all_to_all(out, TOK, 0, 0, tiled=True)
     grad_k, grad_v = settle(asked, own, back)
     return tuple(a.transpose(1, 0, 2) for a in (grad_q, grad_k, grad_v))

time: 203 us -> 194 us (0.956)
  local copies, waits for them, and re-layouts: 16.6 us -> 7.25 us
  Pallas kernels: 23.5 us -> 30.6 us
  waiting for transfers between devices: 19.9 us -> 15.4 us
  blocking collectives: 99.6 us -> 96.9 us
    unnamed x50 -> x42, local copies, waits for them, and re-layouts: 14.3 us -> 4.49 us
    ppermute x7, waiting for transfers between devices: 14 us -> 9.94 us  [across_plane(): return lax.ppermute(value, PLANE, pairs)]
    pallas_call x1, Pallas kernels: 0.85 us -> 4.78 us  [serve_plane(): pl.pallas_call(functools.partial(serve_plane_kernel, sizes), out_shape=[j...]
    all_to_all x1, blocking collectives: 74.4 us -> 71.8 us  [shards(): back = lax.all_to_all(out, TOK, 0, 0, tiled=True)]
    pallas_call x2, Pallas kernels: 12.9 us -> 15.1 us  [attend(): pl.pallas_call(functools.partial(attend_kernel, tiles, len(fars)), out_sh...]
  transfers between devices with their start and end apart: 18 -> 18, of which waited for: 7 -> 3; matrix products, arithmetic and copies ran while one was open for 2% -> 3% of each run, Pallas kernels for 7% -> 10%
where the time goes in v4:
time: 194 us
  blocking collectives  96.9 us (50%)
  starting transfers between devices  37.7 us (19%)
  Pallas kernels  30.6 us (16%)
  waiting for transfers between devices  15.4 us (8%)
  local copies, waits for them, and re-layouts  7.25 us (4%)
  other arithmetic  4.8 us (2%)
    all_to_all x1, blocking collectives, shards(): back = lax.all_to_all(out, TOK, 0, 0, tiled=True)  71.8 us
    ppermute x7, starting transfers between devices, across_plane(): return lax.ppermute(value, PLANE, pairs)  15.9 us
    pallas_call x2, Pallas kernels, attend(): pl.pallas_call(functools.partial(attend_kernel, tiles, len(fars)), out_sh...  15.1 us
    all_to_all x1, blocking collectives, shards(): asked = lax.all_to_all(wanted.T, 'z', 0, 0, tiled=True)  13.8 us
    all_to_all x1, blocking collectives, shards(): lax.all_to_all(want.reshape(nx, nz, ny).transpose(0, 2, 1).reshape(nx * n...  11.4 us
    ppermute x8, starting transfers between devices, along_z(): lax.ppermute(value, 'z', [(i, (i + step) % count) for i in range(count)])  11 us
    ppermute x7, waiting for transfers between devices, across_plane(): return lax.ppermute(value, PLANE, pairs)  9.94 us
    all_to_all x1, starting transfers between devices, shards(): far = lax.all_to_all(served, TOK, 0, 0, tiled=True)  7.92 us
  transfers between devices with their start and end apart: 18, of which 3 were waited for; matrix products, arithmetic and copies ran while one was open for 3% of the time, Pallas kernels for 10%

profile of v4, /device:TPU:32, one launch (start us, length us, event | category | flops | bytes accessed | tf_op | source)
XLA Modules:
  0.0 193.6 jit_solution(15419685293579626517)
XLA Ops:
  0.6 0.0 copy-start.2
  0.6 0.0 copy-start.1
  0.7 1.1 slice_bitcast_fusion.2
  1.8 0.0 copy-start.4
  1.8 1.9 collective-permute-start.1
  3.8 0.2 collective-permute-start
  3.9 0.7 and_select_fusion
  4.7 0.6 convert_reduce_fusion.1
  5.3 0.1 select_reduce_fusion
  5.4 0.1 reshape.265
  5.5 0.1 copy.26
  5.6 11.4 %all_to_all.31 = s32[8,1,8]{2,1,0:T(1,128)S(1)} all-to-all(s32[8,1,8]{2,1,0:T(1,128)S(1)} %bitcast.51), channel_id=1, replica_groups=mesh['x_lo'=2,'z'=8,'y'=4,'x_hi'=2,'core'=2] {'x_lo','y'}, dimensions={0} | all-to-all | bytes 512 | tf_op jit(solution)/shard_map/all_to_all | solution.py:291
  16.9 0.5 broadcast.109
  17.5 0.7 reduce.3
  18.1 0.6 reshape.266.wanted_ref
  18.7 0.0 collective-permute-done.1.refs_2_
  18.7 0.0 collective-permute-done.refs_1_
  18.8 2.0 %collective-permute-start.2 = (bf16[2,3,256,128]{3,2,1,0:T(8,128)(2,1)S(1)}, bf16[2,3,256,128]{3,2,1,0:T(8,128)(2,1)S(1)}, u32[]{:S(2)}, u32[]{:S(2)}) collective-permute-start(bf16[2,3,256,128]{3,2,1,0:T(8,128)(2,1)S(1)} %collective-permute-done.refs_1_), channel_id=1, source_target_pairs={{0,16},{16,32},{32,48},{48,64},{64,80},{80,96},{96,112},{112,0},{1... | collective-permute-start | bytes 1179656 | tf_op jit(solution)/shard_map/ppermute | solution.py:264
  20.8 2.1 %collective-permute-start.3 = (bf16[2,3,256,128]{3,2,1,0:T(8,128)(2,1)S(1)}, bf16[2,3,256,128]{3,2,1,0:T(8,128)(2,1)S(1)}, u32[]{:S(2)}, u32[]{:S(2)}) collective-permute-start(bf16[2,3,256,128]{3,2,1,0:T(8,128)(2,1)S(1)} %collective-permute-done.1.refs_2_), channel_id=1, source_target_pairs={{0,112},{16,0},{32,16},{48,32},{64,48},{80,64},{96,80},{112,96},{1... | collective-permute-start | bytes 1179656 | tf_op jit(solution)/shard_map/ppermute | solution.py:264
  22.9 2.7 %collective-permute-start.8 = (bf16[256,768]{1,0:T(8,128)(2,1)}, bf16[256,768]{1,0:T(8,128)(2,1)S(1)}, u32[]{:S(2)}, u32[]{:S(2)}) collective-permute-start(bf16[256,768]{1,0:T(8,128)(2,1)} %own_ref.1), channel_id=1, source_target_pairs={{0,2},{2,0},{1,3},{3,1},{4,6},{6,4},{5,7},{7,5},{8,10},{10,8},{9,1... | collective-permute-start | bytes 1179656 | tf_op jit(solution)/shard_map/ppermute | solution.py:234
  25.6 0.1 copy.29
  25.7 13.8 %all_to_all.32 = s32[8,1,8]{2,1,0:T(1,128)S(1)} all-to-all(s32[8,1,8]{2,1,0:T(1,128)S(1)} %copy.29), channel_id=1, replica_groups=mesh['x_lo'=2,'z'=8,'y'=4,'x_hi'=2,'core'=2] {'z'}, dimensions={0} | all-to-all | bytes 512 | tf_op jit(solution)/shard_map/all_to_all | solution.py:294
  39.5 0.1 copy.30
  39.5 0.1 copy.31
  39.6 0.1 reshape.268.asked_ref
  39.7 0.0 collective-permute-done.2.refs_3_
  39.8 0.6 collective-permute-start.4
  40.4 1.5 collective-permute-start.5
  41.9 0.0 collective-permute-done.8.flip_ref
  41.9 1.2 pad_maximum_fusion
  43.1 0.1 collective-permute-start.9
  43.2 4.6 %collective-permute-done.4.refs_5_ = bf16[2,3,256,128]{3,2,1,0:T(8,128)(2,1)S(1)} collective-permute-done((bf16[2,3,256,128]{3,2,1,0:T(8,128)(2,1)S(1)}, bf16[2,3,256,128]{3,2,1,0:T(8,128)(2,1)S(1)}, u32[]{:S(2)}, u32[]{:S(2)}) %collective-permute-start.4) | collective-permute-done | bytes 393248 | tf_op jit(solution)/shard_map/ppermute | solution.py:264
  47.8 1.6 collective-permute-start.6
  49.4 0.0 collective-permute-done.5.refs_6_
  49.4 0.8 copy-done.7
  50.2 1.1 collective-permute-start.7
  51.3 2.3 %shard_map.85 = bf16[64,3,2,16,128]{4,3,2,1,0:T(8,128)(2,1)} custom-call(s32[64]{0:T(128)S(1)} %reshape.268.asked_ref, bf16[6,256,128]{2,1,0:T(8,128)(2,1)S(1)} %bitcast.39, bf16[6,256,128]{2,1,0:T(8,128)(2,1)S(1)} %bitcast.43), custom_call_target="tpu_custom_call" | custom-call | tf_op jit(solution)/shard_map/pallas_call | solution.py:41
  53.7 0.9 copy-done.8
  54.6 0.7 copy-done.13
  55.3 0.8 collective-permute-done.7.refs_8_
  56.1 7.9 %all-to-all-start.2 = ((bf16[64,3,2,16,128]{4,3,2,1,0:T(8,128)(2,1)}), bf16[64,3,2,16,128]{4,3,2,1,0:T(8,128)(2,1)S(1)}, u32[]{:S(2)}, u32[]{:S(2)}) async-start(bf16[64,3,2,16,128]{4,3,2,1,0:T(8,128)(2,1)} %shard_map.85), calls=%async_computation.2 | async-start | bytes 3145728 | tf_op jit(solution)/shard_map/all_to_all | solution.py:323
  64.1 0.6 pad_add_fusion.1.pos_ref
  64.7 5.4 %shard_map.86.do_ref = bf16[256,768]{1,0:T(8,128)(2,1)} custom-call(s32[1]{0:T(128)} %bitcast.21.me_ref, bf16[256,768]{1,0:T(8,128)(2,1)} %own_ref.1, bf16[256,768]{1,0:T(8,128)(2,1)} %copy-done.5, bf16[2,256,768]{2,1,0:T(8,128)(2,1)} %copy-done.8, bf16[768,3072]{1,0:T(8,128)(2,1)} %w_ref.1), custom_call_target="tpu_custom_call" | custom-call | tf_op jit(solution)/shard_map/pallas_call | solution.py:243
  70.1 4.8 %shard_map.87 = (bf16[8,3,2,16,128]{4,3,2,1,0:T(8,128)(2,1)}, bf16[8,3,2,16,128]{4,3,2,1,0:T(8,128)(2,1)}, bf16[8,3,2,16,128]{4,3,2,1,0:T(8,128)(2,1)}, bf16[8,3...) custom-call(s32[64]{0:T(128)} %reshape.266.wanted_ref, ...), custom_call_target="tpu_custom_call" | custom-call | tf_op jit(solution)/shard_map/pallas_call | solution.py:74
  74.9 1.5 collective-permute-start.10
  76.4 2.7 %collective-permute-start.11 = (bf16[8,3,2,16,128]{4,3,2,1,0:T(8,128)(2,1)}, bf16[8,3,2,16,128]{4,3,2,1,0:T(8,128)(2,1)S(1)}, u32[]{:S(2)}, u32[]{:S(2)}) collective-permute-start(bf16[8,3,2,16,128]{4,3,2,1,0:T(8,128)(2,1)} %get-tuple-element.76), channel_id=1, source_target_pairs={{0,8},{4,12},{8,0},{12,4},{128,136},{132,140},{136,128},{140,132},... | collective-permute-start | bytes 589832 | tf_op jit(solution)/shard_map/ppermute | solution.py:270
  79.1 0.1 convert_reduce_fusion
  79.2 0.1 select_reduce_fusion.1
  79.4 1.5 collective-permute-start.12
  80.9 1.6 collective-permute-start.13
  82.5 0.4 collective-permute-start.14
  82.9 9.9 %collective-permute-done.10.refs_1_ = bf16[8,3,2,16,128]{4,3,2,1,0:T(8,128)(2,1)S(1)} collective-permute-done((bf16[8,3,2,16,128]{4,3,2,1,0:T(8,128)(2,1)}, bf16[8,3,2,16,128]{4,3,2,1,0:T(8,128)(2,1)S(1)}, u32[]{:S(2)}, u32[]{:S(2)}) %collective-permute-start.10) | collective-permute-done | bytes 196640 | tf_op jit(solution)/shard_map/ppermute | solution.py:270
  92.9 8.2 %collective-permute-start.15 = (bf16[8,3,2,16,128]{4,3,2,1,0:T(8,128)(2,1)}, bf16[8,3,2,16,128]{4,3,2,1,0:T(8,128)(2,1)S(1)}, u32[]{:S(2)}, u32[]{:S(2)}) collective-permute-start(bf16[8,3,2,16,128]{4,3,2,1,0:T(8,128)(2,1)} %get-tuple-element.80), channel_id=1, source_target_pairs={{0,136},{4,140},{8,128},{12,132},{128,8},{132,12},{136,0},{140,4},... | collective-permute-start | bytes 589832 | tf_op jit(solution)/shard_map/ppermute | solution.py:270
  101.0 0.6 fusion.12
  101.6 1.2 copy-done.3
  102.8 7.5 %shard_map.88 = (bf16[6,256,128]{2,1,0:T(8,128)(2,1)}, f32[2,6,256,128]{3,2,1,0:T(8,128)}, bf16[64,6,2,16,128]{4,3,2,1,0:T(8,128)(2,1)}) custom-call(s32[42]{0:T(128)} %get-tuple-element.94.src_ref.dst_ref, s32[42]{0:T(128)} %get-tuple-element.94.src_ref.dst_ref, s32[1]{0:T(128)} %bitcast.3.num_ref, bf16[6,256,128]{2,1,0:T(8,128)(2,1)} %bitcast.44, ...), custom_call_target="tpu_custom_call" | custom-call | tf_op jit(solution)/shard_map/pallas_call | solution.py:140
  110.5 0.6 copy-done.16
  111.0 0.1 copy-done.17
  111.1 0.1 copy-done.18
  111.2 0.1 copy-done.19
  111.2 0.1 copy-done.20
  111.3 7.5 %shard_map.89 = (bf16[6,256,128]{2,1,0:T(8,128)(2,1)}, f32[2,6,256,128]{3,2,1,0:T(8,128)}, bf16[64,6,2,16,128]{4,3,2,1,0:T(8,128)(2,1)}) custom-call(s32[42]{0:T(128)} %get-tuple-element.93.src_ref, s32[42]{0:T(128)} %get-tuple-element.94.src_ref.dst_ref, s32[1]{0:T(128)} %bitcast.3.num_ref, ...), custom_call_target="tpu_custom_call", output_to_operand_aliasing={{0}: (15, {}), {1}: (16, {}), {2}: (17, {})} | custom-call | tf_op jit(solution)/shard_map/pallas_call | solution.py:140
  118.8 71.8 %all_to_all.33.back_ref = bf16[64,6,2,16,128]{4,3,2,1,0:T(8,128)(2,1)S(1)} all-to-all(bf16[64,6,2,16,128]{4,3,2,1,0:T(8,128)(2,1)} %get-tuple-element.88), channel_id=1, replica_groups=mesh['x_lo'=2,'z'=8,'y'=4,'x_hi'=2,'core'=2] {'x_lo','z','y'}, dimensions={0} | all-to-all | bytes 6291456 | tf_op jit(solution)/shard_map/all_to_all | solution.py:331
  190.6 3.0 %shard_map.90 = (bf16[6,256,128]{2,1,0:T(8,128)(2,1)}, bf16[6,256,128]{2,1,0:T(8,128)(2,1)}) custom-call(s32[64]{0:T(128)S(1)} %reshape.268.asked_ref, f32[2,6,256,128]{3,2,1,0:T(8,128)S(1)} %copy-done, bf16[64,6,2,16,128]{4,3,2,1,0:T(8,128)(2,1)S(1)} %all_to_all.33.back_ref), custom_call_target="tpu_custom_call" | custom-call | tf_op jit(solution)/shard_map/pallas_call | solution.py:190
  (45 shorter events, 0.2 us)
Async XLA Ops:
  0.6 50.7 %copy-start.2 = (bf16[256,6,128]{2,0,1:T(8,128)(2,1)S(1)}, bf16[256,6,128]{2,0,1:T(8,128)(2,1)}, u32[]{:S(2)}) copy-start(bf16[256,6,128]{2,0,1:T(8,128)(2,1)} %param.8) | copy-start | bytes 1179652
  0.6 50.7 %copy-start.1 = (bf16[256,6,128]{2,0,1:T(8,128)(2,1)S(1)}, bf16[256,6,128]{2,0,1:T(8,128)(2,1)}, u32[]{:S(2)}) copy-start(bf16[256,6,128]{2,0,1:T(8,128)(2,1)} %param.7) | copy-start | bytes 1179652
  1.8 54.3 %copy-start.4 = (bf16[2,3,256,128]{3,2,1,0:T(8,128)(2,1)}, bf16[2,3,256,128]{3,2,1,0:T(8,128)(2,1)S(1)}, u32[]{:S(2)}) copy-start(bf16[2,3,256,128]{3,2,1,0:T(8,128)(2,1)S(1)} %pad_maximum_fusion.1.refs_0_) | copy-start | bytes 1179652
  1.8 16.9 %collective-permute-start.1 = (bf16[2,3,256,128]{3,2,1,0:T(8,128)(2,1)S(1)}, bf16[2,3,256,128]{3,2,1,0:T(8,128)(2,1)S(1)}, u32[]{:S(2)}, u32[]{:S(2)}) collective-permute-start(bf16[2,3,256,128]{3,2,1,0:T(8,128)(2,1)S(1)} %pad_maximum_fusion.1.refs_0_), channel_id=1, source_target_pairs={{0,112},{16,0},{32,16},{48,32},{64,48},{80,64},{96,80},{112,96},{1... | collective-permute-start | bytes 1179656 | tf_op jit(solution)/shard_map/ppermute | solution.py:264
  3.8 15.0 %collective-permute-start = (bf16[2,3,256,128]{3,2,1,0:T(8,128)(2,1)S(1)}, bf16[2,3,256,128]{3,2,1,0:T(8,128)(2,1)S(1)}, u32[]{:S(2)}, u32[]{:S(2)}) collective-permute-start(bf16[2,3,256,128]{3,2,1,0:T(8,128)(2,1)S(1)} %pad_maximum_fusion.1.refs_0_), channel_id=1, source_target_pairs={{0,16},{16,32},{32,48},{48,64},{64,80},{80,96},{96,112},{112,0},{1... | collective-permute-start | bytes 1179656 | tf_op jit(solution)/shard_map/ppermute | solution.py:264
  18.7 37.3 %copy-start.9 = (bf16[2,3,256,128]{3,2,1,0:T(8,128)(2,1)}, bf16[2,3,256,128]{3,2,1,0:T(8,128)(2,1)S(1)}, u32[]{:S(2)}) copy-start(bf16[2,3,256,128]{3,2,1,0:T(8,128)(2,1)S(1)} %collective-permute-done.1.refs_2_) | copy-start | bytes 1179652
  18.8 37.3 %copy-start.10 = (bf16[2,3,256,128]{3,2,1,0:T(8,128)(2,1)}, bf16[2,3,256,128]{3,2,1,0:T(8,128)(2,1)S(1)}, u32[]{:S(2)}) copy-start(bf16[2,3,256,128]{3,2,1,0:T(8,128)(2,1)S(1)} %collective-permute-done.refs_1_) | copy-start | bytes 1179652
  18.8 21.0 %collective-permute-start.2 = (bf16[2,3,256,128]{3,2,1,0:T(8,128)(2,1)S(1)}, bf16[2,3,256,128]{3,2,1,0:T(8,128)(2,1)S(1)}, u32[]{:S(2)}, u32[]{:S(2)}) collective-permute-start(bf16[2,3,256,128]{3,2,1,0:T(8,128)(2,1)S(1)} %collective-permute-done.refs_1_), channel_id=1, source_target_pairs={{0,16},{16,32},{32,48},{48,64},{64,80},{80,96},{96,112},{112,0},{1... | collective-permute-start | bytes 1179656 | tf_op jit(solution)/shard_map/ppermute | solution.py:264
  20.8 19.0 %collective-permute-start.3 = (bf16[2,3,256,128]{3,2,1,0:T(8,128)(2,1)S(1)}, bf16[2,3,256,128]{3,2,1,0:T(8,128)(2,1)S(1)}, u32[]{:S(2)}, u32[]{:S(2)}) collective-permute-start(bf16[2,3,256,128]{3,2,1,0:T(8,128)(2,1)S(1)} %collective-permute-done.1.refs_2_), channel_id=1, source_target_pairs={{0,112},{16,0},{32,16},{48,32},{64,48},{80,64},{96,80},{112,96},{1... | collective-permute-start | bytes 1179656 | tf_op jit(solution)/shard_map/ppermute | solution.py:264
  22.9 19.0 %collective-permute-start.8 = (bf16[256,768]{1,0:T(8,128)(2,1)}, bf16[256,768]{1,0:T(8,128)(2,1)S(1)}, u32[]{:S(2)}, u32[]{:S(2)}) collective-permute-start(bf16[256,768]{1,0:T(8,128)(2,1)} %own_ref.1), channel_id=1, source_target_pairs={{0,2},{2,0},{1,3},{3,1},{4,6},{6,4},{5,7},{7,5},{8,10},{10,8},{9,1... | collective-permute-start | bytes 1179656 | tf_op jit(solution)/shard_map/ppermute | solution.py:234
  39.7 16.3 %copy-start.11 = (bf16[2,3,256,128]{3,2,1,0:T(8,128)(2,1)}, bf16[2,3,256,128]{3,2,1,0:T(8,128)(2,1)S(1)}, u32[]{:S(2)}) copy-start(bf16[2,3,256,128]{3,2,1,0:T(8,128)(2,1)S(1)} %collective-permute-done.2.refs_3_) | copy-start | bytes 1179652
  39.8 16.3 %copy-start.12 = (bf16[2,3,256,128]{3,2,1,0:T(8,128)(2,1)}, bf16[2,3,256,128]{3,2,1,0:T(8,128)(2,1)S(1)}, u32[]{:S(2)}) copy-start(bf16[2,3,256,128]{3,2,1,0:T(8,128)(2,1)S(1)} %collective-permute-done.3.refs_4_) | copy-start | bytes 1179652
  39.8 8.1 %collective-permute-start.4 = (bf16[2,3,256,128]{3,2,1,0:T(8,128)(2,1)S(1)}, bf16[2,3,256,128]{3,2,1,0:T(8,128)(2,1)S(1)}, u32[]{:S(2)}, u32[]{:S(2)}) collective-permute-start(bf16[2,3,256,128]{3,2,1,0:T(8,128)(2,1)S(1)} %collective-permute-done.2.refs_3_), channel_id=1, source_target_pairs={{0,16},{16,32},{32,48},{48,64},{64,80},{80,96},{96,112},{112,0},{1... | collective-permute-start | bytes 1179656 | tf_op jit(solution)/shard_map/ppermute | solution.py:264
  40.4 9.0 %collective-permute-start.5 = (bf16[2,3,256,128]{3,2,1,0:T(8,128)(2,1)S(1)}, bf16[2,3,256,128]{3,2,1,0:T(8,128)(2,1)S(1)}, u32[]{:S(2)}, u32[]{:S(2)}) collective-permute-start(bf16[2,3,256,128]{3,2,1,0:T(8,128)(2,1)S(1)} %collective-permute-done.3.refs_4_), channel_id=1, source_target_pairs={{0,112},{16,0},{32,16},{48,32},{64,48},{80,64},{96,80},{112,96},{1... | collective-permute-start | bytes 1179656 | tf_op jit(solution)/shard_map/ppermute | solution.py:264
  41.9 14.2 %copy-start.5 = (bf16[256,768]{1,0:T(8,128)(2,1)}, bf16[256,768]{1,0:T(8,128)(2,1)S(1)}, u32[]{:S(2)}) copy-start(bf16[256,768]{1,0:T(8,128)(2,1)S(1)} %collective-permute-done.8.flip_ref) | copy-start | bytes 1179652
  43.1 10.6 %collective-permute-start.9 = (bf16[2,256,768]{2,1,0:T(8,128)(2,1)S(1)}, bf16[2,256,768]{2,1,0:T(8,128)(2,1)S(1)}, u32[]{:S(2)}, u32[]{:S(2)}) collective-permute-start(bf16[2,256,768]{2,1,0:T(8,128)(2,1)S(1)} %pad_maximum_fusion), channel_id=1, source_target_pairs={{0,1},{1,0},{2,3},{3,2},{4,5},{5,4},{6,7},{7,6},{8,9},{9,8},{10,11... | collective-permute-start | bytes 2359304 | tf_op jit(solution)/shard_map/ppermute | solution.py:235
  47.8 8.3 %copy-start.6 = (bf16[2,3,256,128]{3,2,1,0:T(8,128)(2,1)}, bf16[2,3,256,128]{3,2,1,0:T(8,128)(2,1)S(1)}, u32[]{:S(2)}) copy-start(bf16[2,3,256,128]{3,2,1,0:T(8,128)(2,1)S(1)} %collective-permute-done.4.refs_5_) | copy-start | bytes 1179652
  47.8 6.7 %collective-permute-start.6 = (bf16[3,256,128]{2,1,0:T(8,128)(2,1)S(1)}, bf16[3,256,128]{2,1,0:T(8,128)(2,1)S(1)}, u32[]{:S(2)}, u32[]{:S(2)}) collective-permute-start(bf16[3,256,128]{2,1,0:T(8,128)(2,1)S(1)} %slice_bitcast_fusion.1), channel_id=1, source_target_pairs={{0,16},{16,32},{32,48},{48,64},{64,80},{80,96},{96,112},{112,0},{1... | collective-permute-start | bytes 589832 | tf_op jit(solution)/shard_map/ppermute | solution.py:264
  49.4 0.8 copy-start.7
  50.2 5.9 %collective-permute-start.7 = (bf16[3,256,128]{2,1,0:T(8,128)(2,1)S(1)}, bf16[3,256,128]{2,1,0:T(8,128)(2,1)}, u32[]{:S(2)}, u32[]{:S(2)}) collective-permute-start(bf16[3,256,128]{2,1,0:T(8,128)(2,1)S(1)} %slice_bitcast_fusion), channel_id=1, source_target_pairs={{0,112},{16,0},{32,16},{48,32},{64,48},{80,64},{96,80},{112,96},{1... | collective-permute-start | bytes 589832 | tf_op jit(solution)/shard_map/ppermute | solution.py:264
  53.7 0.9 copy-start.8
  54.6 0.7 copy-start.13
  56.1 45.5 %all-to-all-start.2 = ((bf16[64,3,2,16,128]{4,3,2,1,0:T(8,128)(2,1)}), bf16[64,3,2,16,128]{4,3,2,1,0:T(8,128)(2,1)S(1)}, u32[]{:S(2)}, u32[]{:S(2)}) async-start(bf16[64,3,2,16,128]{4,3,2,1,0:T(8,128)(2,1)} %shard_map.85), calls=%async_computation.2 | async-start | bytes 3145728 | tf_op jit(solution)/shard_map/all_to_all | solution.py:323
  74.9 18.0 %collective-permute-start.10 = (bf16[8,3,2,16,128]{4,3,2,1,0:T(8,128)(2,1)}, bf16[8,3,2,16,128]{4,3,2,1,0:T(8,128)(2,1)S(1)}, u32[]{:S(2)}, u32[]{:S(2)}) collective-permute-start(bf16[8,3,2,16,128]{4,3,2,1,0:T(8,128)(2,1)} %get-tuple-element.75), channel_id=1, source_target_pairs={{0,4},{4,8},{8,12},{12,0},{128,132},{132,136},{136,140},{140,128},... | collective-permute-start | bytes 589832 | tf_op jit(solution)/shard_map/ppermute | solution.py:270
  76.4 24.6 %collective-permute-start.11 = (bf16[8,3,2,16,128]{4,3,2,1,0:T(8,128)(2,1)}, bf16[8,3,2,16,128]{4,3,2,1,0:T(8,128)(2,1)S(1)}, u32[]{:S(2)}, u32[]{:S(2)}) collective-permute-start(bf16[8,3,2,16,128]{4,3,2,1,0:T(8,128)(2,1)} %get-tuple-element.76), channel_id=1, source_target_pairs={{0,8},{4,12},{8,0},{12,4},{128,136},{132,140},{136,128},{140,132},... | collective-permute-start | bytes 589832 | tf_op jit(solution)/shard_map/ppermute | solution.py:270
  79.4 31.0 %collective-permute-start.12 = (bf16[8,3,2,16,128]{4,3,2,1,0:T(8,128)(2,1)}, bf16[8,3,2,16,128]{4,3,2,1,0:T(8,128)(2,1)S(1)}, u32[]{:S(2)}, u32[]{:S(2)}) collective-permute-start(bf16[8,3,2,16,128]{4,3,2,1,0:T(8,128)(2,1)} %get-tuple-element.77), channel_id=1, source_target_pairs={{0,12},{4,0},{8,4},{12,8},{128,140},{132,128},{136,132},{140,136},... | collective-permute-start | bytes 589832 | tf_op jit(solution)/shard_map/ppermute | solution.py:270
  80.9 29.5 %collective-permute-start.13 = (bf16[8,3,2,16,128]{4,3,2,1,0:T(8,128)(2,1)}, bf16[8,3,2,16,128]{4,3,2,1,0:T(8,128)(2,1)S(1)}, u32[]{:S(2)}, u32[]{:S(2)}) collective-permute-start(bf16[8,3,2,16,128]{4,3,2,1,0:T(8,128)(2,1)} %get-tuple-element.78), channel_id=1, source_target_pairs={{0,128},{4,132},{8,136},{12,140},{128,0},{132,4},{136,8},{140,12},... | collective-permute-start | bytes 589832 | tf_op jit(solution)/shard_map/ppermute | solution.py:270
  82.5 27.9 %collective-permute-start.14 = (bf16[8,3,2,16,128]{4,3,2,1,0:T(8,128)(2,1)}, bf16[8,3,2,16,128]{4,3,2,1,0:T(8,128)(2,1)S(1)}, u32[]{:S(2)}, u32[]{:S(2)}) collective-permute-start(bf16[8,3,2,16,128]{4,3,2,1,0:T(8,128)(2,1)} %get-tuple-element.79), channel_id=1, source_target_pairs={{0,132},{4,136},{8,140},{12,128},{128,4},{132,8},{136,12},{140,0},... | collective-permute-start | bytes 589832 | tf_op jit(solution)/shard_map/ppermute | solution.py:270
  92.9 17.6 %copy-start.14 = (bf16[8,3,2,16,128]{4,3,2,1,0:T(8,128)(2,1)}, bf16[8,3,2,16,128]{4,3,2,1,0:T(8,128)(2,1)S(1)}, u32[]{:S(2)}) copy-start(bf16[8,3,2,16,128]{4,3,2,1,0:T(8,128)(2,1)S(1)} %collective-permute-done.10.refs_1_) | copy-start | bytes 589828
  92.9 17.5 %collective-permute-start.15 = (bf16[8,3,2,16,128]{4,3,2,1,0:T(8,128)(2,1)}, bf16[8,3,2,16,128]{4,3,2,1,0:T(8,128)(2,1)S(1)}, u32[]{:S(2)}, u32[]{:S(2)}) collective-permute-start(bf16[8,3,2,16,128]{4,3,2,1,0:T(8,128)(2,1)} %get-tuple-element.80), channel_id=1, source_target_pairs={{0,136},{4,140},{8,128},{12,132},{128,8},{132,12},{136,0},{140,4},... | collective-permute-start | bytes 589832 | tf_op jit(solution)/shard_map/ppermute | solution.py:270
  101.0 9.4 %copy-start.15 = (bf16[8,3,2,16,128]{4,3,2,1,0:T(8,128)(2,1)}, bf16[8,3,2,16,128]{4,3,2,1,0:T(8,128)(2,1)S(1)}, u32[]{:S(2)}) copy-start(bf16[8,3,2,16,128]{4,3,2,1,0:T(8,128)(2,1)S(1)} %collective-permute-done.11.refs_2_) | copy-start | bytes 589828
  101.0 9.4 %collective-permute-start.16 = (bf16[8,3,2,16,128]{4,3,2,1,0:T(8,128)(2,1)}, bf16[8,3,2,16,128]{4,3,2,1,0:T(8,128)(2,1)S(1)}, u32[]{:S(2)}, u32[]{:S(2)}) collective-permute-start(bf16[8,3,2,16,128]{4,3,2,1,0:T(8,128)(2,1)} %get-tuple-element.81), channel_id=1, source_target_pairs={{0,140},{4,128},{8,132},{12,136},{128,12},{132,0},{136,4},{140,8},... | collective-permute-start | bytes 589832 | tf_op jit(solution)/shard_map/ppermute | solution.py:270
  101.6 1.2 copy-start.3
  110.4 0.7 copy-start.16
  110.4 0.7 copy-start.17
  110.4 0.8 copy-start.18
  110.4 0.8 copy-start.19
  110.4 0.9 copy-start.20
  118.8 71.8 %copy-start = (f32[2,6,256,128]{3,2,1,0:T(8,128)S(1)}, f32[2,6,256,128]{3,2,1,0:T(8,128)}, u32[]{:S(2)}) copy-start(f32[2,6,256,128]{3,2,1,0:T(8,128)} %get-tuple-element.87.own_ref) | copy-start | bytes 4718596

commit v5 on v4

--- a/solution.py
+++ b/solution.py
@@ -18,6 +18,7 @@
 RING = 3
 STEPS = (0, -1, 1, -2, 2, -3, 3, 4)
 GROUP = 1
+PIECE = 8
 SMALL = pltpu.CompilerParams(vmem_limit_bytes=16 * MIB)
 LARGE = pltpu.CompilerParams(vmem_limit_bytes=60 * MIB)
 
@@ -84,7 +85,7 @@
     )(wanted, pos, *held)
 
 
-def attend_kernel(tiles, parts, src_ref, dst_ref, num_ref, q_ref, do_ref, k_ref, v_ref, *refs):
+def attend_kernel(tiles, parts, list_ref, q_ref, do_ref, k_ref, v_ref, *refs):
     fars, (dq_ref, own_ref, out_ref, k_all, v_all, staged) = refs[:parts], refs[-6:]
     rows = q_ref.shape[1]
     total = rows + tiles * KT
@@ -98,11 +99,11 @@
             start += far.shape[0]
         for j in range(tiles):
             at = rows + j * KT
-            k_all[h, at : at + KT] = staged[h, src_ref[j], 0]
-            v_all[h, at : at + KT] = staged[h, src_ref[j], 1]
+            k_all[h, at : at + KT] = staged[h, list_ref[j], 0]
+            v_all[h, at : at + KT] = staged[h, list_ref[j], 1]
 
     row = lax.broadcasted_iota(jnp.int32, (total, rows), 0)
-    inside = row < rows + num_ref[0] * KT
+    inside = row < rows + list_ref[2 * tiles] * KT
     for h in range(GROUP):
         q = q_ref[h]
         do = do_ref[:, h * HD : (h + 1) * HD]
@@ -127,28 +128,29 @@
             own_ref[kind, h] = part[:rows]
             far = part[rows:].astype(jnp.bfloat16)
             for j in range(tiles):
-                out_ref[dst_ref[j], h, kind] = far[j * KT : (j + 1) * KT]
-
-
-def attend(src, dst, num, q, do, keys, values, fars, slots, first, earlier=()):
+                out_ref[list_ref[tiles + j], h, kind] = far[j * KT : (j + 1) * KT]
+
+
+def attend(listed, tiles, q, do, keys, values, fars, slots, first, earlier=()):
     heads, rows, _ = q.shape
-    tiles = src.shape[0]
     held = sum(far.shape[0] for far in fars)
+    piece = lambda i: pl.BlockSpec((PIECE, GROUP, 2, KT, HD), lambda g, *_: (i, g, 0, 0, 0))
+    pieces = [(far, piece(i)) for far in fars for i in range(far.shape[0] // PIECE)]
     total = rows + tiles * KT
     start = first // GROUP
     own = pl.BlockSpec((GROUP, rows, HD), lambda g, *_: (start + g, 0, 0))
     return pl.pallas_call(
-        functools.partial(attend_kernel, tiles, len(fars)),
+        functools.partial(attend_kernel, tiles, len(pieces)),
         out_shape=(
             jax.ShapeDtypeStruct((heads, rows, HD), jnp.bfloat16),
             jax.ShapeDtypeStruct((2, heads, rows, HD), jnp.float32),
             jax.ShapeDtypeStruct((slots, heads, 2, KT, HD), jnp.bfloat16),
         ),
         grid_spec=pltpu.PrefetchScalarGridSpec(
-            num_scalar_prefetch=3,
+            num_scalar_prefetch=1,
             grid=(fars[0].shape[1] // GROUP,),
             in_specs=[own, pl.BlockSpec((rows, GROUP * HD), lambda g, *_: (0, start + g)), own, own]
-            + [pl.BlockSpec((far.shape[0], GROUP, 2, KT, HD), lambda g, *_: (0, g, 0, 0, 0)) for far in fars]
+            + [spec for _, spec in pieces]
             + [pl.BlockSpec(memory_space=pl.ANY)] * len(earlier),
             out_specs=(
                 own,
@@ -161,9 +163,9 @@
                 pltpu.VMEM((GROUP, held, 2, KT, HD), jnp.bfloat16),
             ],
         ),
-        input_output_aliases={7 + len(fars) + i: i for i in range(len(earlier))},
+        input_output_aliases={5 + len(pieces) + i: i for i in range(len(earlier))},
         compiler_params=LARGE,
-    )(src, dst, num, q, do, keys, values, *fars, *earlier)
+    )(listed, q, do, keys, values, *[far for far, _ in pieces], *earlier)
 
 
 def settle_kernel(asked_ref, own_ref, back_ref, dk_ref, dv_ref, *accs):
@@ -322,12 +324,13 @@
     served, held, flip, both = lax.optimization_barrier((served, held, flip, both))
     far = lax.all_to_all(served, TOK, 0, 0, tiled=True)
     d_attn = project(grad_out, flip, both, w_out)
-    held, d_attn = lax.optimization_barrier((held, d_attn))
+    lists = [jnp.concatenate([src, slot, number]) for src in (slot, plane_slot)]
+    held, d_attn, lists = lax.optimization_barrier((held, d_attn, lists))
     near = serve_plane(sizes, wanted, pos, held)
     near = [near[0]] + [across_plane(near[r], r // ny, r % ny) for r in range(1, nx * ny)]
 
-    done = attend(slot, slot, number, queries, d_attn, keys, values, [far], count, RING)
-    grad_q, own, out = attend(plane_slot, slot, number, queries, d_attn, keys, values, near, count, 0, done)
+    done = attend(lists[0], tiles, queries, d_attn, keys, values, [far], count, RING)
+    grad_q, own, out = attend(lists[1], tiles, queries, d_attn, keys, values, near, count, 0, done)
     back = lax.all_to_all(out, TOK, 0, 0, tiled=True)
     grad_k, grad_v = settle(asked, own, back)
     return tuple(a.transpose(1, 0, 2) for a in (grad_q, grad_k, grad_v))

time: 194 us -> 195 us (level)
  starting transfers between devices: 37.7 us -> 33.4 us
  waiting for transfers between devices: 15.4 us -> 19.5 us
    ppermute x7, starting transfers between devices: 15.9 us -> 11.8 us  [across_plane(): return lax.ppermute(value, PLANE, pairs)]
    ppermute x7, waiting for transfers between devices: 9.94 us -> 13.5 us  [across_plane(): return lax.ppermute(value, PLANE, pairs)]
    unnamed x42 -> x38, local copies, waits for them, and re-layouts: 4.49 us -> 3.76 us
  transfers between devices with their start and end apart: 18 -> 18, of which waited for: 3 -> 5; matrix products, arithmetic and copies ran while one was open for 3% -> 4% of each run, Pallas kernels for 10% -> 10%
where the time goes in v5:
time: 195 us; the launch traced here: 194 us
  blocking collectives  98.5 us (51%)
  starting transfers between devices  33.4 us (17%)
  Pallas kernels  29.4 us (15%)
  waiting for transfers between devices  19.5 us (10%)
  local copies, waits for them, and re-layouts  6.5 us (3%)
  other arithmetic  5.54 us (3%)
    all_to_all x1, blocking collectives, shards(): back = lax.all_to_all(out, TOK, 0, 0, tiled=True)  73.3 us
    all_to_all x1, blocking collectives, shards(): asked = lax.all_to_all(wanted.T, 'z', 0, 0, tiled=True)  13.9 us
    pallas_call x2, Pallas kernels, attend(): pl.pallas_call(functools.partial(attend_kernel, tiles, len(pieces)), out_...  13.8 us
    ppermute x7, waiting for transfers between devices, across_plane(): return lax.ppermute(value, PLANE, pairs)  13.5 us
    ppermute x7, starting transfers between devices, across_plane(): return lax.ppermute(value, PLANE, pairs)  11.8 us
    all_to_all x1, blocking collectives, shards(): lax.all_to_all(want.reshape(nx, nz, ny).transpose(0, 2, 1).reshape(nx * n...  11.4 us
    ppermute x8, starting transfers between devices, along_z(): lax.ppermute(value, 'z', [(i, (i + step) % count) for i in range(count)])  10.8 us
    all_to_all x1, starting transfers between devices, shards(): far = lax.all_to_all(served, TOK, 0, 0, tiled=True)  7.9 us
  transfers between devices with their start and end apart: 18, of which 5 were waited for; matrix products, arithmetic and copies ran while one was open for 4% of the time, Pallas kernels for 10%

profile of v5, /device:TPU:32, one launch (start us, length us, event | category | flops | bytes accessed | tf_op | source)
XLA Modules:
  0.0 193.8 jit_solution(4961531455035374981)
XLA Ops:
  0.6 0.0 copy-start.2
  0.6 0.0 copy-start.1
  0.7 1.1 slice_bitcast_fusion.2
  1.8 0.0 copy-start.4
  1.8 1.9 collective-permute-start.1
  3.8 0.2 collective-permute-start
  3.9 1.4 convert_reduce_fusion.1
  5.4 0.1 select_reduce_fusion.1
  5.5 0.1 reshape.264
  5.5 0.1 copy.26
  5.6 11.4 %all_to_all.31 = s32[8,1,8]{2,1,0:T(1,128)S(1)} all-to-all(s32[8,1,8]{2,1,0:T(1,128)S(1)} %bitcast.51), channel_id=1, replica_groups=mesh['x_lo'=2,'z'=8,'y'=4,'x_hi'=2,'core'=2] {'x_lo','y'}, dimensions={0} | all-to-all | bytes 512 | tf_op jit(solution)/shard_map/all_to_all | solution.py:293
  17.0 0.5 broadcast.109
  17.5 0.7 reduce.3
  18.2 0.6 reshape.265.wanted_ref
  18.8 0.0 collective-permute-done.refs_1_
  18.8 2.0 %collective-permute-start.2 = (bf16[2,3,256,128]{3,2,1,0:T(8,128)(2,1)S(1)}, bf16[2,3,256,128]{3,2,1,0:T(8,128)(2,1)}, u32[]{:S(2)}, u32[]{:S(2)}) collective-permute-start(bf16[2,3,256,128]{3,2,1,0:T(8,128)(2,1)S(1)} %collective-permute-done.refs_1_), channel_id=1, source_target_pairs={{0,16},{16,32},{32,48},{48,64},{64,80},{80,96},{96,112},{112,0},{1... | collective-permute-start | bytes 1179656 | tf_op jit(solution)/shard_map/ppermute | solution.py:266
  20.8 2.1 %collective-permute-start.3 = (bf16[2,3,256,128]{3,2,1,0:T(8,128)(2,1)S(1)}, bf16[2,3,256,128]{3,2,1,0:T(8,128)(2,1)}, u32[]{:S(2)}, u32[]{:S(2)}) collective-permute-start(bf16[2,3,256,128]{3,2,1,0:T(8,128)(2,1)S(1)} %collective-permute-done.1.refs_2_), channel_id=1, source_target_pairs={{0,112},{16,0},{32,16},{48,32},{64,48},{80,64},{96,80},{112,96},{1... | collective-permute-start | bytes 1179656 | tf_op jit(solution)/shard_map/ppermute | solution.py:266
  22.9 2.7 %collective-permute-start.8 = (bf16[256,768]{1,0:T(8,128)(2,1)}, bf16[256,768]{1,0:T(8,128)(2,1)S(1)}, u32[]{:S(2)}, u32[]{:S(2)}) collective-permute-start(bf16[256,768]{1,0:T(8,128)(2,1)} %own_ref.1), channel_id=1, source_target_pairs={{0,2},{2,0},{1,3},{3,1},{4,6},{6,4},{5,7},{7,5},{8,10},{10,8},{9,1... | collective-permute-start | bytes 1179656 | tf_op jit(solution)/shard_map/ppermute | solution.py:236
  25.6 0.1 copy.29
  25.7 13.9 %all_to_all.32 = s32[8,1,8]{2,1,0:T(1,128)S(1)} all-to-all(s32[8,1,8]{2,1,0:T(1,128)S(1)} %copy.29), channel_id=1, replica_groups=mesh['x_lo'=2,'z'=8,'y'=4,'x_hi'=2,'core'=2] {'z'}, dimensions={0} | all-to-all | bytes 512 | tf_op jit(solution)/shard_map/all_to_all | solution.py:296
  39.6 0.1 copy.30
  39.6 0.1 copy.31
  39.7 0.1 reshape.267.asked_ref
  39.8 0.0 collective-permute-done.2.refs_3_
  39.8 0.0 collective-permute-done.3.refs_4_
  39.8 0.5 collective-permute-start.4
  40.4 1.6 collective-permute-start.5
  42.0 1.2 pad_maximum_fusion
  43.2 0.1 collective-permute-start.9
  43.3 5.1 %collective-permute-done.4.refs_5_ = bf16[2,3,256,128]{3,2,1,0:T(8,128)(2,1)S(1)} collective-permute-done((bf16[2,3,256,128]{3,2,1,0:T(8,128)(2,1)}, bf16[2,3,256,128]{3,2,1,0:T(8,128)(2,1)S(1)}, u32[]{:S(2)}, u32[]{:S(2)}) %collective-permute-start.4) | collective-permute-done | bytes 393248 | tf_op jit(solution)/shard_map/ppermute | solution.py:266
  48.4 1.5 collective-permute-start.6
  49.8 0.1 collective-permute-done.5.refs_6_
  49.9 1.0 collective-permute-start.7
  51.0 2.4 %shard_map.85 = bf16[64,3,2,16,128]{4,3,2,1,0:T(8,128)(2,1)} custom-call(s32[64]{0:T(128)S(1)} %reshape.267.asked_ref, bf16[6,256,128]{2,1,0:T(8,128)(2,1)S(1)} %bitcast.39, bf16[6,256,128]{2,1,0:T(8,128)(2,1)S(1)} %bitcast.43), custom_call_target="tpu_custom_call" | custom-call | tf_op jit(solution)/shard_map/pallas_call | solution.py:42
  53.4 0.9 copy-done.8
  54.3 0.2 collective-permute-done.6.refs_7_
  54.5 0.7 copy-done.11
  55.2 0.6 collective-permute-done.7.refs_8_
  55.8 7.9 %all-to-all-start.2 = ((bf16[64,3,2,16,128]{4,3,2,1,0:T(8,128)(2,1)}), bf16[64,3,2,16,128]{4,3,2,1,0:T(8,128)(2,1)S(1)}, u32[]{:S(2)}, u32[]{:S(2)}) async-start(bf16[64,3,2,16,128]{4,3,2,1,0:T(8,128)(2,1)} %shard_map.85), calls=%async_computation.2 | async-start | bytes 3145728 | tf_op jit(solution)/shard_map/all_to_all | solution.py:325
  63.7 0.6 pad_add_fusion.1.pos_ref
  64.4 0.1 convert_reduce_fusion
  64.5 0.1 select_reduce_fusion
  64.6 1.2 add_add_fusion.1
  65.9 5.4 %shard_map.86.do_ref = bf16[256,768]{1,0:T(8,128)(2,1)} custom-call(s32[1]{0:T(128)} %bitcast.19.me_ref, bf16[256,768]{1,0:T(8,128)(2,1)} %own_ref.1, bf16[256,768]{1,0:T(8,128)(2,1)} %copy-done.5, bf16[2,256,768]{2,1,0:T(8,128)(2,1)} %copy-done.8, bf16[768,3072]{1,0:T(8,128)(2,1)} %w_ref.1), custom_call_target="tpu_custom_call" | custom-call | tf_op jit(solution)/shard_map/pallas_call | solution.py:245
  71.3 4.8 %shard_map.87 = (bf16[8,3,2,16,128]{4,3,2,1,0:T(8,128)(2,1)}, bf16[8,3,2,16,128]{4,3,2,1,0:T(8,128)(2,1)}, bf16[8,3,2,16,128]{4,3,2,1,0:T(8,128)(2,1)}, bf16[8,3...) custom-call(s32[64]{0:T(128)} %reshape.265.wanted_ref, ...), custom_call_target="tpu_custom_call" | custom-call | tf_op jit(solution)/shard_map/pallas_call | solution.py:75
  76.1 1.5 collective-permute-start.10
  77.6 2.7 %collective-permute-start.11 = (bf16[8,3,2,16,128]{4,3,2,1,0:T(8,128)(2,1)}, bf16[8,3,2,16,128]{4,3,2,1,0:T(8,128)(2,1)S(1)}, u32[]{:S(2)}, u32[]{:S(2)}) collective-permute-start(bf16[8,3,2,16,128]{4,3,2,1,0:T(8,128)(2,1)} %get-tuple-element.79), channel_id=1, source_target_pairs={{0,8},{4,12},{8,0},{12,4},{128,136},{132,140},{136,128},{140,132},... | collective-permute-start | bytes 589832 | tf_op jit(solution)/shard_map/ppermute | solution.py:272
  80.3 1.5 collective-permute-start.12
  81.8 1.6 collective-permute-start.13
  83.4 0.4 collective-permute-start.14
  83.8 13.5 %collective-permute-done.10.refs_1_ = bf16[8,3,2,16,128]{4,3,2,1,0:T(8,128)(2,1)S(1)} collective-permute-done((bf16[8,3,2,16,128]{4,3,2,1,0:T(8,128)(2,1)}, bf16[8,3,2,16,128]{4,3,2,1,0:T(8,128)(2,1)S(1)}, u32[]{:S(2)}, u32[]{:S(2)}) %collective-permute-start.10) | collective-permute-done | bytes 196640 | tf_op jit(solution)/shard_map/ppermute | solution.py:272
  97.3 4.1 %collective-permute-start.15 = (bf16[8,3,2,16,128]{4,3,2,1,0:T(8,128)(2,1)}, bf16[8,3,2,16,128]{4,3,2,1,0:T(8,128)(2,1)S(1)}, u32[]{:S(2)}, u32[]{:S(2)}) collective-permute-start(bf16[8,3,2,16,128]{4,3,2,1,0:T(8,128)(2,1)} %get-tuple-element.83), channel_id=1, source_target_pairs={{0,136},{4,140},{8,128},{12,132},{128,8},{132,12},{136,0},{140,4},... | collective-permute-start | bytes 589832 | tf_op jit(solution)/shard_map/ppermute | solution.py:272
  101.4 0.0 collective-permute-done.11.refs_2_
  101.4 0.0 all-to-all-done.2.refs_0_.refs_1_.refs_2_.refs_3_.refs_4_.refs_5_.refs_6_.refs_7_
  101.4 1.2 copy-done.3
  102.7 6.9 %shard_map.88 = (bf16[6,256,128]{2,1,0:T(8,128)(2,1)}, f32[2,6,256,128]{3,2,1,0:T(8,128)}, bf16[64,6,2,16,128]{4,3,2,1,0:T(8,128)(2,1)}) custom-call(s32[85]{0:T(128)} %get-tuple-element.85.list_ref, bf16[6,256,128]{2,1,0:T(8,128)(2,1)} %bitcast.44, bf16[256,768]{1,0:T(8,128)(2,1)} %shard_map.86.do_ref, bf16[6,256,128]{2,1,0:T(8,128)(2,1)} %bitcast.37, ...), custom_call_target="tpu_custom_call" | custom-call | tf_op jit(solution)/shard_map/pallas_call | solution.py:142
  109.7 0.6 copy-done.14
  110.3 0.1 copy-done.15
  110.4 0.1 copy-done.16
  110.4 0.1 copy-done.17
  110.5 0.1 copy-done.18
  110.6 6.9 %shard_map.89 = (bf16[6,256,128]{2,1,0:T(8,128)(2,1)}, f32[2,6,256,128]{3,2,1,0:T(8,128)}, bf16[64,6,2,16,128]{4,3,2,1,0:T(8,128)(2,1)}) custom-call(s32[85]{0:T(128)} %get-tuple-element.65.list_ref, bf16[6,256,128]{2,1,0:T(8,128)(2,1)} %bitcast.45, ...), custom_call_target="tpu_custom_call", output_to_operand_aliasing={{0}: (13, {}), {1}: (14, {}), {2}: (15, {})} | custom-call | tf_op jit(solution)/shard_map/pallas_call | solution.py:142
  117.4 73.3 %all_to_all.33.back_ref = bf16[64,6,2,16,128]{4,3,2,1,0:T(8,128)(2,1)S(1)} all-to-all(bf16[64,6,2,16,128]{4,3,2,1,0:T(8,128)(2,1)} %get-tuple-element.92), channel_id=1, replica_groups=mesh['x_lo'=2,'z'=8,'y'=4,'x_hi'=2,'core'=2] {'x_lo','z','y'}, dimensions={0} | all-to-all | bytes 6291456 | tf_op jit(solution)/shard_map/all_to_all | solution.py:334
  190.8 3.0 %shard_map.90 = (bf16[6,256,128]{2,1,0:T(8,128)(2,1)}, bf16[6,256,128]{2,1,0:T(8,128)(2,1)}) custom-call(s32[64]{0:T(128)S(1)} %reshape.267.asked_ref, f32[2,6,256,128]{3,2,1,0:T(8,128)S(1)} %copy-done, bf16[64,6,2,16,128]{4,3,2,1,0:T(8,128)(2,1)S(1)} %all_to_all.33.back_ref), custom_call_target="tpu_custom_call" | custom-call | tf_op jit(solution)/shard_map/pallas_call | solution.py:192
  (42 shorter events, 0.2 us)
Async XLA Ops:
  0.6 50.4 %copy-start.2 = (bf16[256,6,128]{2,0,1:T(8,128)(2,1)S(1)}, bf16[256,6,128]{2,0,1:T(8,128)(2,1)}, u32[]{:S(2)}) copy-start(bf16[256,6,128]{2,0,1:T(8,128)(2,1)} %param.8) | copy-start | bytes 1179652
  0.6 50.4 %copy-start.1 = (bf16[256,6,128]{2,0,1:T(8,128)(2,1)S(1)}, bf16[256,6,128]{2,0,1:T(8,128)(2,1)}, u32[]{:S(2)}) copy-start(bf16[256,6,128]{2,0,1:T(8,128)(2,1)} %param.7) | copy-start | bytes 1179652
  1.8 54.0 %copy-start.4 = (bf16[2,3,256,128]{3,2,1,0:T(8,128)(2,1)}, bf16[2,3,256,128]{3,2,1,0:T(8,128)(2,1)S(1)}, u32[]{:S(2)}) copy-start(bf16[2,3,256,128]{3,2,1,0:T(8,128)(2,1)S(1)} %pad_maximum_fusion.1.refs_0_) | copy-start | bytes 1179652
  1.8 16.9 %collective-permute-start.1 = (bf16[2,3,256,128]{3,2,1,0:T(8,128)(2,1)S(1)}, bf16[2,3,256,128]{3,2,1,0:T(8,128)(2,1)S(1)}, u32[]{:S(2)}, u32[]{:S(2)}) collective-permute-start(bf16[2,3,256,128]{3,2,1,0:T(8,128)(2,1)S(1)} %pad_maximum_fusion.1.refs_0_), channel_id=1, source_target_pairs={{0,112},{16,0},{32,16},{48,32},{64,48},{80,64},{96,80},{112,96},{1... | collective-permute-start | bytes 1179656 | tf_op jit(solution)/shard_map/ppermute | solution.py:266
  3.8 15.0 %collective-permute-start = (bf16[2,3,256,128]{3,2,1,0:T(8,128)(2,1)S(1)}, bf16[2,3,256,128]{3,2,1,0:T(8,128)(2,1)S(1)}, u32[]{:S(2)}, u32[]{:S(2)}) collective-permute-start(bf16[2,3,256,128]{3,2,1,0:T(8,128)(2,1)S(1)} %pad_maximum_fusion.1.refs_0_), channel_id=1, source_target_pairs={{0,16},{16,32},{32,48},{48,64},{64,80},{80,96},{96,112},{112,0},{1... | collective-permute-start | bytes 1179656 | tf_op jit(solution)/shard_map/ppermute | solution.py:266
  18.8 37.0 %copy-start.9 = (bf16[2,3,256,128]{3,2,1,0:T(8,128)(2,1)}, bf16[2,3,256,128]{3,2,1,0:T(8,128)(2,1)S(1)}, u32[]{:S(2)}) copy-start(bf16[2,3,256,128]{3,2,1,0:T(8,128)(2,1)S(1)} %collective-permute-done.1.refs_2_) | copy-start | bytes 1179652
  18.8 23.2 %copy-start.10 = (bf16[2,3,256,128]{3,2,1,0:T(8,128)(2,1)}, bf16[2,3,256,128]{3,2,1,0:T(8,128)(2,1)S(1)}, u32[]{:S(2)}) copy-start(bf16[2,3,256,128]{3,2,1,0:T(8,128)(2,1)S(1)} %collective-permute-done.refs_1_) | copy-start | bytes 1179652
  18.8 21.0 %collective-permute-start.2 = (bf16[2,3,256,128]{3,2,1,0:T(8,128)(2,1)S(1)}, bf16[2,3,256,128]{3,2,1,0:T(8,128)(2,1)}, u32[]{:S(2)}, u32[]{:S(2)}) collective-permute-start(bf16[2,3,256,128]{3,2,1,0:T(8,128)(2,1)S(1)} %collective-permute-done.refs_1_), channel_id=1, source_target_pairs={{0,16},{16,32},{32,48},{48,64},{64,80},{80,96},{96,112},{112,0},{1... | collective-permute-start | bytes 1179656 | tf_op jit(solution)/shard_map/ppermute | solution.py:266
  20.8 19.1 %collective-permute-start.3 = (bf16[2,3,256,128]{3,2,1,0:T(8,128)(2,1)S(1)}, bf16[2,3,256,128]{3,2,1,0:T(8,128)(2,1)}, u32[]{:S(2)}, u32[]{:S(2)}) collective-permute-start(bf16[2,3,256,128]{3,2,1,0:T(8,128)(2,1)S(1)} %collective-permute-done.1.refs_2_), channel_id=1, source_target_pairs={{0,112},{16,0},{32,16},{48,32},{64,48},{80,64},{96,80},{112,96},{1... | collective-permute-start | bytes 1179656 | tf_op jit(solution)/shard_map/ppermute | solution.py:266
  22.9 19.1 %collective-permute-start.8 = (bf16[256,768]{1,0:T(8,128)(2,1)}, bf16[256,768]{1,0:T(8,128)(2,1)S(1)}, u32[]{:S(2)}, u32[]{:S(2)}) collective-permute-start(bf16[256,768]{1,0:T(8,128)(2,1)} %own_ref.1), channel_id=1, source_target_pairs={{0,2},{2,0},{1,3},{3,1},{4,6},{6,4},{5,7},{7,5},{8,10},{10,8},{9,1... | collective-permute-start | bytes 1179656 | tf_op jit(solution)/shard_map/ppermute | solution.py:236
  39.8 8.5 %collective-permute-start.4 = (bf16[2,3,256,128]{3,2,1,0:T(8,128)(2,1)}, bf16[2,3,256,128]{3,2,1,0:T(8,128)(2,1)S(1)}, u32[]{:S(2)}, u32[]{:S(2)}) collective-permute-start(bf16[2,3,256,128]{3,2,1,0:T(8,128)(2,1)} %collective-permute-done.2.refs_3_), channel_id=1, source_target_pairs={{0,16},{16,32},{32,48},{48,64},{64,80},{80,96},{96,112},{112,0},{1... | collective-permute-start | bytes 1179656 | tf_op jit(solution)/shard_map/ppermute | solution.py:266
  40.4 9.5 %collective-permute-start.5 = (bf16[2,3,256,128]{3,2,1,0:T(8,128)(2,1)}, bf16[2,3,256,128]{3,2,1,0:T(8,128)(2,1)S(1)}, u32[]{:S(2)}, u32[]{:S(2)}) collective-permute-start(bf16[2,3,256,128]{3,2,1,0:T(8,128)(2,1)} %collective-permute-done.3.refs_4_), channel_id=1, source_target_pairs={{0,112},{16,0},{32,16},{48,32},{64,48},{80,64},{96,80},{112,96},{1... | collective-permute-start | bytes 1179656 | tf_op jit(solution)/shard_map/ppermute | solution.py:266
  42.0 13.9 %copy-start.5 = (bf16[256,768]{1,0:T(8,128)(2,1)}, bf16[256,768]{1,0:T(8,128)(2,1)S(1)}, u32[]{:S(2)}) copy-start(bf16[256,768]{1,0:T(8,128)(2,1)S(1)} %collective-permute-done.8.flip_ref) | copy-start | bytes 1179652
  43.2 10.2 %collective-permute-start.9 = (bf16[2,256,768]{2,1,0:T(8,128)(2,1)S(1)}, bf16[2,256,768]{2,1,0:T(8,128)(2,1)S(1)}, u32[]{:S(2)}, u32[]{:S(2)}) collective-permute-start(bf16[2,256,768]{2,1,0:T(8,128)(2,1)S(1)} %pad_maximum_fusion), channel_id=1, source_target_pairs={{0,1},{1,0},{2,3},{3,2},{4,5},{5,4},{6,7},{7,6},{8,9},{9,8},{10,11... | collective-permute-start | bytes 2359304 | tf_op jit(solution)/shard_map/ppermute | solution.py:237
  48.3 7.5 %copy-start.6 = (bf16[2,3,256,128]{3,2,1,0:T(8,128)(2,1)}, bf16[2,3,256,128]{3,2,1,0:T(8,128)(2,1)S(1)}, u32[]{:S(2)}) copy-start(bf16[2,3,256,128]{3,2,1,0:T(8,128)(2,1)S(1)} %collective-permute-done.4.refs_5_) | copy-start | bytes 1179652
  48.4 6.1 %collective-permute-start.6 = (bf16[3,256,128]{2,1,0:T(8,128)(2,1)S(1)}, bf16[3,256,128]{2,1,0:T(8,128)(2,1)S(1)}, u32[]{:S(2)}, u32[]{:S(2)}) collective-permute-start(bf16[3,256,128]{2,1,0:T(8,128)(2,1)S(1)} %slice_bitcast_fusion.1), channel_id=1, source_target_pairs={{0,16},{16,32},{32,48},{48,64},{64,80},{80,96},{96,112},{112,0},{1... | collective-permute-start | bytes 589832 | tf_op jit(solution)/shard_map/ppermute | solution.py:266
  49.9 21.4 %copy-start.7 = (bf16[2,3,256,128]{3,2,1,0:T(8,128)(2,1)}, bf16[2,3,256,128]{3,2,1,0:T(8,128)(2,1)S(1)}, u32[]{:S(2)}) copy-start(bf16[2,3,256,128]{3,2,1,0:T(8,128)(2,1)S(1)} %collective-permute-done.5.refs_6_) | copy-start | bytes 1179652
  49.9 5.9 %collective-permute-start.7 = (bf16[3,256,128]{2,1,0:T(8,128)(2,1)S(1)}, bf16[3,256,128]{2,1,0:T(8,128)(2,1)}, u32[]{:S(2)}, u32[]{:S(2)}) collective-permute-start(bf16[3,256,128]{2,1,0:T(8,128)(2,1)S(1)} %slice_bitcast_fusion), channel_id=1, source_target_pairs={{0,112},{16,0},{32,16},{48,32},{64,48},{80,64},{96,80},{112,96},{1... | collective-permute-start | bytes 589832 | tf_op jit(solution)/shard_map/ppermute | solution.py:266
  53.4 0.9 copy-start.8
  54.5 0.7 copy-start.11
  55.8 45.6 %all-to-all-start.2 = ((bf16[64,3,2,16,128]{4,3,2,1,0:T(8,128)(2,1)}), bf16[64,3,2,16,128]{4,3,2,1,0:T(8,128)(2,1)S(1)}, u32[]{:S(2)}, u32[]{:S(2)}) async-start(bf16[64,3,2,16,128]{4,3,2,1,0:T(8,128)(2,1)} %shard_map.85), calls=%async_computation.2 | async-start | bytes 3145728 | tf_op jit(solution)/shard_map/all_to_all | solution.py:325
  76.1 21.2 %collective-permute-start.10 = (bf16[8,3,2,16,128]{4,3,2,1,0:T(8,128)(2,1)}, bf16[8,3,2,16,128]{4,3,2,1,0:T(8,128)(2,1)S(1)}, u32[]{:S(2)}, u32[]{:S(2)}) collective-permute-start(bf16[8,3,2,16,128]{4,3,2,1,0:T(8,128)(2,1)} %get-tuple-element.78), channel_id=1, source_target_pairs={{0,4},{4,8},{8,12},{12,0},{128,132},{132,136},{136,140},{140,128},... | collective-permute-start | bytes 589832 | tf_op jit(solution)/shard_map/ppermute | solution.py:272
  77.6 23.8 %collective-permute-start.11 = (bf16[8,3,2,16,128]{4,3,2,1,0:T(8,128)(2,1)}, bf16[8,3,2,16,128]{4,3,2,1,0:T(8,128)(2,1)S(1)}, u32[]{:S(2)}, u32[]{:S(2)}) collective-permute-start(bf16[8,3,2,16,128]{4,3,2,1,0:T(8,128)(2,1)} %get-tuple-element.79), channel_id=1, source_target_pairs={{0,8},{4,12},{8,0},{12,4},{128,136},{132,140},{136,128},{140,132},... | collective-permute-start | bytes 589832 | tf_op jit(solution)/shard_map/ppermute | solution.py:272
  80.3 29.3 %collective-permute-start.12 = (bf16[8,3,2,16,128]{4,3,2,1,0:T(8,128)(2,1)}, bf16[8,3,2,16,128]{4,3,2,1,0:T(8,128)(2,1)S(1)}, u32[]{:S(2)}, u32[]{:S(2)}) collective-permute-start(bf16[8,3,2,16,128]{4,3,2,1,0:T(8,128)(2,1)} %get-tuple-element.80), channel_id=1, source_target_pairs={{0,12},{4,0},{8,4},{12,8},{128,140},{132,128},{136,132},{140,136},... | collective-permute-start | bytes 589832 | tf_op jit(solution)/shard_map/ppermute | solution.py:272
  81.8 27.9 %collective-permute-start.13 = (bf16[8,3,2,16,128]{4,3,2,1,0:T(8,128)(2,1)}, bf16[8,3,2,16,128]{4,3,2,1,0:T(8,128)(2,1)S(1)}, u32[]{:S(2)}, u32[]{:S(2)}) collective-permute-start(bf16[8,3,2,16,128]{4,3,2,1,0:T(8,128)(2,1)} %get-tuple-element.81), channel_id=1, source_target_pairs={{0,128},{4,132},{8,136},{12,140},{128,0},{132,4},{136,8},{140,12},... | collective-permute-start | bytes 589832 | tf_op jit(solution)/shard_map/ppermute | solution.py:272
  83.4 26.3 %collective-permute-start.14 = (bf16[8,3,2,16,128]{4,3,2,1,0:T(8,128)(2,1)}, bf16[8,3,2,16,128]{4,3,2,1,0:T(8,128)(2,1)S(1)}, u32[]{:S(2)}, u32[]{:S(2)}) collective-permute-start(bf16[8,3,2,16,128]{4,3,2,1,0:T(8,128)(2,1)} %get-tuple-element.82), channel_id=1, source_target_pairs={{0,132},{4,136},{8,140},{12,128},{128,4},{132,8},{136,12},{140,0},... | collective-permute-start | bytes 589832 | tf_op jit(solution)/shard_map/ppermute | solution.py:272
  97.3 12.4 %copy-start.12 = (bf16[8,3,2,16,128]{4,3,2,1,0:T(8,128)(2,1)}, bf16[8,3,2,16,128]{4,3,2,1,0:T(8,128)(2,1)S(1)}, u32[]{:S(2)}) copy-start(bf16[8,3,2,16,128]{4,3,2,1,0:T(8,128)(2,1)S(1)} %collective-permute-done.10.refs_1_) | copy-start | bytes 589828
  97.3 12.4 %collective-permute-start.15 = (bf16[8,3,2,16,128]{4,3,2,1,0:T(8,128)(2,1)}, bf16[8,3,2,16,128]{4,3,2,1,0:T(8,128)(2,1)S(1)}, u32[]{:S(2)}, u32[]{:S(2)}) collective-permute-start(bf16[8,3,2,16,128]{4,3,2,1,0:T(8,128)(2,1)} %get-tuple-element.83), channel_id=1, source_target_pairs={{0,136},{4,140},{8,128},{12,132},{128,8},{132,12},{136,0},{140,4},... | collective-permute-start | bytes 589832 | tf_op jit(solution)/shard_map/ppermute | solution.py:272
  101.4 8.3 %copy-start.13 = (bf16[8,3,2,16,128]{4,3,2,1,0:T(8,128)(2,1)}, bf16[8,3,2,16,128]{4,3,2,1,0:T(8,128)(2,1)S(1)}, u32[]{:S(2)}) copy-start(bf16[8,3,2,16,128]{4,3,2,1,0:T(8,128)(2,1)S(1)} %collective-permute-done.11.refs_2_) | copy-start | bytes 589828
  101.4 8.3 %collective-permute-start.16 = (bf16[8,3,2,16,128]{4,3,2,1,0:T(8,128)(2,1)}, bf16[8,3,2,16,128]{4,3,2,1,0:T(8,128)(2,1)S(1)}, u32[]{:S(2)}, u32[]{:S(2)}) collective-permute-start(bf16[8,3,2,16,128]{4,3,2,1,0:T(8,128)(2,1)} %get-tuple-element.84), channel_id=1, source_target_pairs={{0,140},{4,128},{8,132},{12,136},{128,12},{132,0},{136,4},{140,8},... | collective-permute-start | bytes 589832 | tf_op jit(solution)/shard_map/ppermute | solution.py:272
  101.4 1.2 copy-start.3
  109.6 0.7 copy-start.14
  109.6 0.7 copy-start.15
  109.7 0.8 copy-start.16
  109.7 0.8 copy-start.17
  109.7 0.9 copy-start.18
  117.4 73.3 %copy-start = (f32[2,6,256,128]{3,2,1,0:T(8,128)S(1)}, f32[2,6,256,128]{3,2,1,0:T(8,128)}, u32[]{:S(2)}) copy-start(f32[2,6,256,128]{3,2,1,0:T(8,128)} %get-tuple-element.91.own_ref) | copy-start | bytes 4718596

commit v6 on v5

--- a/solution.py
+++ b/solution.py
@@ -169,25 +169,25 @@
 
 
 def settle_kernel(asked_ref, own_ref, back_ref, dk_ref, dv_ref, *accs):
-    slots, heads = back_ref.shape[:2]
-    rows = own_ref.shape[2]
-    for h in range(heads):
+    slots = back_ref.shape[0]
+    block, rows, _ = dk_ref.shape
+    first = pl.program_id(0) * block
+    for h in range(block):
         for kind in range(2):
-            accs[h * 2 + kind][:rows] = own_ref[kind, h]
+            accs[h * 2 + kind][:rows] = own_ref[kind, first + h]
     for s in range(slots):
         asked = asked_ref[s]
         at = tile_rows(jnp.where(asked >= 0, asked, rows // KT))
-        for h in range(heads):
+        for h in range(block):
             for kind in range(2):
-                accs[h * 2 + kind][at] += back_ref[s, h, kind].astype(jnp.float32)
-    for h in range(heads):
+                accs[h * 2 + kind][at] += back_ref[s, first + h, kind].astype(jnp.float32)
+    for h in range(block):
         for kind, out in enumerate((dk_ref, dv_ref)):
             out[h] = accs[h * 2 + kind][:rows].astype(jnp.bfloat16)
 
 
 def settle(asked, own, back, block=2):
     _, heads, rows, _ = own.shape
-    slots = back.shape[0]
     out = pl.BlockSpec((block, rows, HD), lambda h, *_: (h, 0, 0))
     return pl.pallas_call(
         settle_kernel,
@@ -195,10 +195,7 @@
         grid_spec=pltpu.PrefetchScalarGridSpec(
             num_scalar_prefetch=1,
             grid=(heads // block,),
-            in_specs=[
-                pl.BlockSpec((2, block, rows, HD), lambda h, *_: (0, h, 0, 0)),
-                pl.BlockSpec((slots, block, 2, KT, HD), lambda h, *_: (0, h, 0, 0, 0)),
-            ],
+            in_specs=[pl.BlockSpec(memory_space=pltpu.VMEM)] * 2,
             out_specs=[out, out],
             scratch_shapes=[pltpu.VMEM((rows + KT, HD), jnp.float32)] * (2 * block),
         ),

time: 195 us -> 194 us (level)
  no operation moved by 1% of the time
where the time goes in v6:
time: 194 us
  blocking collectives  98.5 us (51%)
  starting transfers between devices  33.4 us (17%)
  Pallas kernels  29.2 us (15%)
  waiting for transfers between devices  19.5 us (10%)
  local copies, waits for them, and re-layouts  6.5 us (3%)
  other arithmetic  5.54 us (3%)
    all_to_all x1, blocking collectives, shards(): back = lax.all_to_all(out, TOK, 0, 0, tiled=True)  73.3 us
    all_to_all x1, blocking collectives, shards(): asked = lax.all_to_all(wanted.T, 'z', 0, 0, tiled=True)  13.9 us
    pallas_call x2, Pallas kernels, attend(): pl.pallas_call(functools.partial(attend_kernel, tiles, len(pieces)), out_...  13.8 us
    ppermute x7, waiting for transfers between devices, across_plane(): return lax.ppermute(value, PLANE, pairs)  13.5 us
    ppermute x7, starting transfers between devices, across_plane(): return lax.ppermute(value, PLANE, pairs)  11.8 us
    all_to_all x1, blocking collectives, shards(): lax.all_to_all(want.reshape(nx, nz, ny).transpose(0, 2, 1).reshape(nx * n...  11.4 us
    ppermute x8, starting transfers between devices, along_z(): lax.ppermute(value, 'z', [(i, (i + step) % count) for i in range(count)])  10.8 us
    all_to_all x1, starting transfers between devices, shards(): far = lax.all_to_all(served, TOK, 0, 0, tiled=True)  7.9 us
  transfers between devices with their start and end apart: 18, of which 5 were waited for; matrix products, arithmetic and copies ran while one was open for 4% of the time, Pallas kernels for 10%

profile of v6, /device:TPU:32, one launch (start us, length us, event | category | flops | bytes accessed | tf_op | source)
XLA Modules:
  0.0 193.6 jit_solution(10869312343454214283)
XLA Ops:
  0.6 0.0 copy-start.2
  0.6 0.0 copy-start.1
  0.7 1.1 slice_bitcast_fusion.2
  1.8 0.0 copy-start.4
  1.8 1.9 collective-permute-start.1
  3.8 0.2 collective-permute-start
  3.9 1.4 convert_reduce_fusion.1
  5.4 0.1 select_reduce_fusion.1
  5.5 0.1 reshape.264
  5.5 0.1 copy.26
  5.6 11.4 %all_to_all.31 = s32[8,1,8]{2,1,0:T(1,128)S(1)} all-to-all(s32[8,1,8]{2,1,0:T(1,128)S(1)} %bitcast.51), channel_id=1, replica_groups=mesh['x_lo'=2,'z'=8,'y'=4,'x_hi'=2,'core'=2] {'x_lo','y'}, dimensions={0} | all-to-all | bytes 512 | tf_op jit(solution)/shard_map/all_to_all | solution.py:290
  17.0 0.5 broadcast.109
  17.5 0.7 reduce.3
  18.2 0.6 reshape.265.wanted_ref
  18.8 2.0 %collective-permute-start.2 = (bf16[2,3,256,128]{3,2,1,0:T(8,128)(2,1)S(1)}, bf16[2,3,256,128]{3,2,1,0:T(8,128)(2,1)}, u32[]{:S(2)}, u32[]{:S(2)}) collective-permute-start(bf16[2,3,256,128]{3,2,1,0:T(8,128)(2,1)S(1)} %collective-permute-done.refs_1_), channel_id=1, source_target_pairs={{0,16},{16,32},{32,48},{48,64},{64,80},{80,96},{96,112},{112,0},{1... | collective-permute-start | bytes 1179656 | tf_op jit(solution)/shard_map/ppermute | solution.py:263
  20.8 2.1 %collective-permute-start.3 = (bf16[2,3,256,128]{3,2,1,0:T(8,128)(2,1)S(1)}, bf16[2,3,256,128]{3,2,1,0:T(8,128)(2,1)}, u32[]{:S(2)}, u32[]{:S(2)}) collective-permute-start(bf16[2,3,256,128]{3,2,1,0:T(8,128)(2,1)S(1)} %collective-permute-done.1.refs_2_), channel_id=1, source_target_pairs={{0,112},{16,0},{32,16},{48,32},{64,48},{80,64},{96,80},{112,96},{1... | collective-permute-start | bytes 1179656 | tf_op jit(solution)/shard_map/ppermute | solution.py:263
  22.9 2.7 %collective-permute-start.8 = (bf16[256,768]{1,0:T(8,128)(2,1)}, bf16[256,768]{1,0:T(8,128)(2,1)S(1)}, u32[]{:S(2)}, u32[]{:S(2)}) collective-permute-start(bf16[256,768]{1,0:T(8,128)(2,1)} %own_ref.1), channel_id=1, source_target_pairs={{0,2},{2,0},{1,3},{3,1},{4,6},{6,4},{5,7},{7,5},{8,10},{10,8},{9,1... | collective-permute-start | bytes 1179656 | tf_op jit(solution)/shard_map/ppermute | solution.py:233
  25.6 0.1 copy.29
  25.7 13.9 %all_to_all.32 = s32[8,1,8]{2,1,0:T(1,128)S(1)} all-to-all(s32[8,1,8]{2,1,0:T(1,128)S(1)} %copy.29), channel_id=1, replica_groups=mesh['x_lo'=2,'z'=8,'y'=4,'x_hi'=2,'core'=2] {'z'}, dimensions={0} | all-to-all | bytes 512 | tf_op jit(solution)/shard_map/all_to_all | solution.py:293
  39.6 0.1 copy.30
  39.6 0.1 copy.31
  39.7 0.1 reshape.267.asked_ref
  39.8 0.0 collective-permute-done.3.refs_4_
  39.8 0.5 collective-permute-start.4
  40.4 1.6 collective-permute-start.5
  42.0 1.2 pad_maximum_fusion
  43.2 0.1 collective-permute-start.9
  43.3 5.1 %collective-permute-done.4.refs_5_ = bf16[2,3,256,128]{3,2,1,0:T(8,128)(2,1)S(1)} collective-permute-done((bf16[2,3,256,128]{3,2,1,0:T(8,128)(2,1)}, bf16[2,3,256,128]{3,2,1,0:T(8,128)(2,1)S(1)}, u32[]{:S(2)}, u32[]{:S(2)}) %collective-permute-start.4) | collective-permute-done | bytes 393248 | tf_op jit(solution)/shard_map/ppermute | solution.py:263
  48.4 1.5 collective-permute-start.6
  49.8 0.1 collective-permute-done.5.refs_6_
  49.9 1.0 collective-permute-start.7
  51.0 2.4 %shard_map.85 = bf16[64,3,2,16,128]{4,3,2,1,0:T(8,128)(2,1)} custom-call(s32[64]{0:T(128)S(1)} %reshape.267.asked_ref, bf16[6,256,128]{2,1,0:T(8,128)(2,1)S(1)} %bitcast.39, bf16[6,256,128]{2,1,0:T(8,128)(2,1)S(1)} %bitcast.43), custom_call_target="tpu_custom_call" | custom-call | tf_op jit(solution)/shard_map/pallas_call | solution.py:42
  53.4 0.0 collective-permute-done.9.both_ref
  53.4 0.9 copy-done.8
  54.3 0.2 collective-permute-done.6.refs_7_
  54.5 0.7 copy-done.11
  55.2 0.6 collective-permute-done.7.refs_8_
  55.8 7.9 %all-to-all-start.2 = ((bf16[64,3,2,16,128]{4,3,2,1,0:T(8,128)(2,1)}), bf16[64,3,2,16,128]{4,3,2,1,0:T(8,128)(2,1)S(1)}, u32[]{:S(2)}, u32[]{:S(2)}) async-start(bf16[64,3,2,16,128]{4,3,2,1,0:T(8,128)(2,1)} %shard_map.85), calls=%async_computation.2 | async-start | bytes 3145728 | tf_op jit(solution)/shard_map/all_to_all | solution.py:322
  63.7 0.6 pad_add_fusion.1.pos_ref
  64.4 0.1 convert_reduce_fusion
  64.5 0.1 select_reduce_fusion
  64.6 1.2 add_add_fusion.1
  65.9 5.4 %shard_map.86.do_ref = bf16[256,768]{1,0:T(8,128)(2,1)} custom-call(s32[1]{0:T(128)} %bitcast.19.me_ref, bf16[256,768]{1,0:T(8,128)(2,1)} %own_ref.1, bf16[256,768]{1,0:T(8,128)(2,1)} %copy-done.5, bf16[2,256,768]{2,1,0:T(8,128)(2,1)} %copy-done.8, bf16[768,3072]{1,0:T(8,128)(2,1)} %w_ref.1), custom_call_target="tpu_custom_call" | custom-call | tf_op jit(solution)/shard_map/pallas_call | solution.py:242
  71.3 4.8 %shard_map.87 = (bf16[8,3,2,16,128]{4,3,2,1,0:T(8,128)(2,1)}, bf16[8,3,2,16,128]{4,3,2,1,0:T(8,128)(2,1)}, bf16[8,3,2,16,128]{4,3,2,1,0:T(8,128)(2,1)}, bf16[8,3...) custom-call(s32[64]{0:T(128)} %reshape.265.wanted_ref, ...), custom_call_target="tpu_custom_call" | custom-call | tf_op jit(solution)/shard_map/pallas_call | solution.py:75
  76.1 1.5 collective-permute-start.10
  77.6 2.7 %collective-permute-start.11 = (bf16[8,3,2,16,128]{4,3,2,1,0:T(8,128)(2,1)}, bf16[8,3,2,16,128]{4,3,2,1,0:T(8,128)(2,1)S(1)}, u32[]{:S(2)}, u32[]{:S(2)}) collective-permute-start(bf16[8,3,2,16,128]{4,3,2,1,0:T(8,128)(2,1)} %get-tuple-element.79), channel_id=1, source_target_pairs={{0,8},{4,12},{8,0},{12,4},{128,136},{132,140},{136,128},{140,132},... | collective-permute-start | bytes 589832 | tf_op jit(solution)/shard_map/ppermute | solution.py:269
  80.3 1.5 collective-permute-start.12
  81.8 1.6 collective-permute-start.13
  83.4 0.4 collective-permute-start.14
  83.8 13.5 %collective-permute-done.10.refs_1_ = bf16[8,3,2,16,128]{4,3,2,1,0:T(8,128)(2,1)S(1)} collective-permute-done((bf16[8,3,2,16,128]{4,3,2,1,0:T(8,128)(2,1)}, bf16[8,3,2,16,128]{4,3,2,1,0:T(8,128)(2,1)S(1)}, u32[]{:S(2)}, u32[]{:S(2)}) %collective-permute-start.10) | collective-permute-done | bytes 196640 | tf_op jit(solution)/shard_map/ppermute | solution.py:269
  97.3 4.1 %collective-permute-start.15 = (bf16[8,3,2,16,128]{4,3,2,1,0:T(8,128)(2,1)}, bf16[8,3,2,16,128]{4,3,2,1,0:T(8,128)(2,1)S(1)}, u32[]{:S(2)}, u32[]{:S(2)}) collective-permute-start(bf16[8,3,2,16,128]{4,3,2,1,0:T(8,128)(2,1)} %get-tuple-element.83), channel_id=1, source_target_pairs={{0,136},{4,140},{8,128},{12,132},{128,8},{132,12},{136,0},{140,4},... | collective-permute-start | bytes 589832 | tf_op jit(solution)/shard_map/ppermute | solution.py:269
  101.4 0.0 collective-permute-done.11.refs_2_
  101.4 0.0 collective-permute-start.16
  101.4 1.2 copy-done.3
  102.7 6.9 %shard_map.88 = (bf16[6,256,128]{2,1,0:T(8,128)(2,1)}, f32[2,6,256,128]{3,2,1,0:T(8,128)}, bf16[64,6,2,16,128]{4,3,2,1,0:T(8,128)(2,1)}) custom-call(s32[85]{0:T(128)} %get-tuple-element.85.list_ref, bf16[6,256,128]{2,1,0:T(8,128)(2,1)} %bitcast.44, bf16[256,768]{1,0:T(8,128)(2,1)} %shard_map.86.do_ref, bf16[6,256,128]{2,1,0:T(8,128)(2,1)} %bitcast.37, ...), custom_call_target="tpu_custom_call" | custom-call | tf_op jit(solution)/shard_map/pallas_call | solution.py:142
  109.6 0.0 collective-permute-done.12.refs_3_
  109.7 0.6 copy-done.14
  110.3 0.1 copy-done.15
  110.4 0.1 copy-done.16
  110.4 0.1 copy-done.17
  110.5 0.1 copy-done.18
  110.6 6.9 %shard_map.89 = (bf16[6,256,128]{2,1,0:T(8,128)(2,1)}, f32[2,6,256,128]{3,2,1,0:T(8,128)}, bf16[64,6,2,16,128]{4,3,2,1,0:T(8,128)(2,1)}) custom-call(s32[85]{0:T(128)} %get-tuple-element.65.list_ref, bf16[6,256,128]{2,1,0:T(8,128)(2,1)} %bitcast.45, ...), custom_call_target="tpu_custom_call", output_to_operand_aliasing={{0}: (13, {}), {1}: (14, {}), {2}: (15, {})} | custom-call | tf_op jit(solution)/shard_map/pallas_call | solution.py:142
  117.5 73.3 %all_to_all.33.back_ref = bf16[64,6,2,16,128]{4,3,2,1,0:T(8,128)(2,1)S(1)} all-to-all(bf16[64,6,2,16,128]{4,3,2,1,0:T(8,128)(2,1)} %get-tuple-element.92), channel_id=1, replica_groups=mesh['x_lo'=2,'z'=8,'y'=4,'x_hi'=2,'core'=2] {'x_lo','z','y'}, dimensions={0} | all-to-all | bytes 6291456 | tf_op jit(solution)/shard_map/all_to_all | solution.py:331
  190.8 2.8 %shard_map.90 = (bf16[6,256,128]{2,1,0:T(8,128)(2,1)}, bf16[6,256,128]{2,1,0:T(8,128)(2,1)}) custom-call(s32[64]{0:T(128)S(1)} %reshape.267.asked_ref, f32[2,6,256,128]{3,2,1,0:T(8,128)S(1)} %copy-done, bf16[64,6,2,16,128]{4,3,2,1,0:T(8,128)(2,1)S(1)} %all_to_all.33.back_ref), custom_call_target="tpu_custom_call" | custom-call | tf_op jit(solution)/shard_map/pallas_call | solution.py:192
  (42 shorter events, 0.2 us)
Async XLA Ops:
  0.6 50.4 %copy-start.2 = (bf16[256,6,128]{2,0,1:T(8,128)(2,1)S(1)}, bf16[256,6,128]{2,0,1:T(8,128)(2,1)}, u32[]{:S(2)}) copy-start(bf16[256,6,128]{2,0,1:T(8,128)(2,1)} %param.8) | copy-start | bytes 1179652
  0.6 50.4 %copy-start.1 = (bf16[256,6,128]{2,0,1:T(8,128)(2,1)S(1)}, bf16[256,6,128]{2,0,1:T(8,128)(2,1)}, u32[]{:S(2)}) copy-start(bf16[256,6,128]{2,0,1:T(8,128)(2,1)} %param.7) | copy-start | bytes 1179652
  1.8 54.0 %copy-start.4 = (bf16[2,3,256,128]{3,2,1,0:T(8,128)(2,1)}, bf16[2,3,256,128]{3,2,1,0:T(8,128)(2,1)S(1)}, u32[]{:S(2)}) copy-start(bf16[2,3,256,128]{3,2,1,0:T(8,128)(2,1)S(1)} %pad_maximum_fusion.1.refs_0_) | copy-start | bytes 1179652
  1.8 16.9 %collective-permute-start.1 = (bf16[2,3,256,128]{3,2,1,0:T(8,128)(2,1)S(1)}, bf16[2,3,256,128]{3,2,1,0:T(8,128)(2,1)S(1)}, u32[]{:S(2)}, u32[]{:S(2)}) collective-permute-start(bf16[2,3,256,128]{3,2,1,0:T(8,128)(2,1)S(1)} %pad_maximum_fusion.1.refs_0_), channel_id=1, source_target_pairs={{0,112},{16,0},{32,16},{48,32},{64,48},{80,64},{96,80},{112,96},{1... | collective-permute-start | bytes 1179656 | tf_op jit(solution)/shard_map/ppermute | solution.py:263
  3.8 15.0 %collective-permute-start = (bf16[2,3,256,128]{3,2,1,0:T(8,128)(2,1)S(1)}, bf16[2,3,256,128]{3,2,1,0:T(8,128)(2,1)S(1)}, u32[]{:S(2)}, u32[]{:S(2)}) collective-permute-start(bf16[2,3,256,128]{3,2,1,0:T(8,128)(2,1)S(1)} %pad_maximum_fusion.1.refs_0_), channel_id=1, source_target_pairs={{0,16},{16,32},{32,48},{48,64},{64,80},{80,96},{96,112},{112,0},{1... | collective-permute-start | bytes 1179656 | tf_op jit(solution)/shard_map/ppermute | solution.py:263
  18.8 37.0 %copy-start.9 = (bf16[2,3,256,128]{3,2,1,0:T(8,128)(2,1)}, bf16[2,3,256,128]{3,2,1,0:T(8,128)(2,1)S(1)}, u32[]{:S(2)}) copy-start(bf16[2,3,256,128]{3,2,1,0:T(8,128)(2,1)S(1)} %collective-permute-done.1.refs_2_) | copy-start | bytes 1179652
  18.8 23.2 %copy-start.10 = (bf16[2,3,256,128]{3,2,1,0:T(8,128)(2,1)}, bf16[2,3,256,128]{3,2,1,0:T(8,128)(2,1)S(1)}, u32[]{:S(2)}) copy-start(bf16[2,3,256,128]{3,2,1,0:T(8,128)(2,1)S(1)} %collective-permute-done.refs_1_) | copy-start | bytes 1179652
  18.8 21.0 %collective-permute-start.2 = (bf16[2,3,256,128]{3,2,1,0:T(8,128)(2,1)S(1)}, bf16[2,3,256,128]{3,2,1,0:T(8,128)(2,1)}, u32[]{:S(2)}, u32[]{:S(2)}) collective-permute-start(bf16[2,3,256,128]{3,2,1,0:T(8,128)(2,1)S(1)} %collective-permute-done.refs_1_), channel_id=1, source_target_pairs={{0,16},{16,32},{32,48},{48,64},{64,80},{80,96},{96,112},{112,0},{1... | collective-permute-start | bytes 1179656 | tf_op jit(solution)/shard_map/ppermute | solution.py:263
  20.8 19.1 %collective-permute-start.3 = (bf16[2,3,256,128]{3,2,1,0:T(8,128)(2,1)S(1)}, bf16[2,3,256,128]{3,2,1,0:T(8,128)(2,1)}, u32[]{:S(2)}, u32[]{:S(2)}) collective-permute-start(bf16[2,3,256,128]{3,2,1,0:T(8,128)(2,1)S(1)} %collective-permute-done.1.refs_2_), channel_id=1, source_target_pairs={{0,112},{16,0},{32,16},{48,32},{64,48},{80,64},{96,80},{112,96},{1... | collective-permute-start | bytes 1179656 | tf_op jit(solution)/shard_map/ppermute | solution.py:263
  22.9 19.1 %collective-permute-start.8 = (bf16[256,768]{1,0:T(8,128)(2,1)}, bf16[256,768]{1,0:T(8,128)(2,1)S(1)}, u32[]{:S(2)}, u32[]{:S(2)}) collective-permute-start(bf16[256,768]{1,0:T(8,128)(2,1)} %own_ref.1), channel_id=1, source_target_pairs={{0,2},{2,0},{1,3},{3,1},{4,6},{6,4},{5,7},{7,5},{8,10},{10,8},{9,1... | collective-permute-start | bytes 1179656 | tf_op jit(solution)/shard_map/ppermute | solution.py:233
  39.8 8.5 %collective-permute-start.4 = (bf16[2,3,256,128]{3,2,1,0:T(8,128)(2,1)}, bf16[2,3,256,128]{3,2,1,0:T(8,128)(2,1)S(1)}, u32[]{:S(2)}, u32[]{:S(2)}) collective-permute-start(bf16[2,3,256,128]{3,2,1,0:T(8,128)(2,1)} %collective-permute-done.2.refs_3_), channel_id=1, source_target_pairs={{0,16},{16,32},{32,48},{48,64},{64,80},{80,96},{96,112},{112,0},{1... | collective-permute-start | bytes 1179656 | tf_op jit(solution)/shard_map/ppermute | solution.py:263
  40.4 9.5 %collective-permute-start.5 = (bf16[2,3,256,128]{3,2,1,0:T(8,128)(2,1)}, bf16[2,3,256,128]{3,2,1,0:T(8,128)(2,1)S(1)}, u32[]{:S(2)}, u32[]{:S(2)}) collective-permute-start(bf16[2,3,256,128]{3,2,1,0:T(8,128)(2,1)} %collective-permute-done.3.refs_4_), channel_id=1, source_target_pairs={{0,112},{16,0},{32,16},{48,32},{64,48},{80,64},{96,80},{112,96},{1... | collective-permute-start | bytes 1179656 | tf_op jit(solution)/shard_map/ppermute | solution.py:263
  42.0 13.9 %copy-start.5 = (bf16[256,768]{1,0:T(8,128)(2,1)}, bf16[256,768]{1,0:T(8,128)(2,1)S(1)}, u32[]{:S(2)}) copy-start(bf16[256,768]{1,0:T(8,128)(2,1)S(1)} %collective-permute-done.8.flip_ref) | copy-start | bytes 1179652
  43.2 10.2 %collective-permute-start.9 = (bf16[2,256,768]{2,1,0:T(8,128)(2,1)S(1)}, bf16[2,256,768]{2,1,0:T(8,128)(2,1)S(1)}, u32[]{:S(2)}, u32[]{:S(2)}) collective-permute-start(bf16[2,256,768]{2,1,0:T(8,128)(2,1)S(1)} %pad_maximum_fusion), channel_id=1, source_target_pairs={{0,1},{1,0},{2,3},{3,2},{4,5},{5,4},{6,7},{7,6},{8,9},{9,8},{10,11... | collective-permute-start | bytes 2359304 | tf_op jit(solution)/shard_map/ppermute | solution.py:234
  48.3 7.5 %copy-start.6 = (bf16[2,3,256,128]{3,2,1,0:T(8,128)(2,1)}, bf16[2,3,256,128]{3,2,1,0:T(8,128)(2,1)S(1)}, u32[]{:S(2)}) copy-start(bf16[2,3,256,128]{3,2,1,0:T(8,128)(2,1)S(1)} %collective-permute-done.4.refs_5_) | copy-start | bytes 1179652
  48.4 6.1 %collective-permute-start.6 = (bf16[3,256,128]{2,1,0:T(8,128)(2,1)S(1)}, bf16[3,256,128]{2,1,0:T(8,128)(2,1)S(1)}, u32[]{:S(2)}, u32[]{:S(2)}) collective-permute-start(bf16[3,256,128]{2,1,0:T(8,128)(2,1)S(1)} %slice_bitcast_fusion.1), channel_id=1, source_target_pairs={{0,16},{16,32},{32,48},{48,64},{64,80},{80,96},{96,112},{112,0},{1... | collective-permute-start | bytes 589832 | tf_op jit(solution)/shard_map/ppermute | solution.py:263
  49.9 21.4 %copy-start.7 = (bf16[2,3,256,128]{3,2,1,0:T(8,128)(2,1)}, bf16[2,3,256,128]{3,2,1,0:T(8,128)(2,1)S(1)}, u32[]{:S(2)}) copy-start(bf16[2,3,256,128]{3,2,1,0:T(8,128)(2,1)S(1)} %collective-permute-done.5.refs_6_) | copy-start | bytes 1179652
  49.9 5.9 %collective-permute-start.7 = (bf16[3,256,128]{2,1,0:T(8,128)(2,1)S(1)}, bf16[3,256,128]{2,1,0:T(8,128)(2,1)}, u32[]{:S(2)}, u32[]{:S(2)}) collective-permute-start(bf16[3,256,128]{2,1,0:T(8,128)(2,1)S(1)} %slice_bitcast_fusion), channel_id=1, source_target_pairs={{0,112},{16,0},{32,16},{48,32},{64,48},{80,64},{96,80},{112,96},{1... | collective-permute-start | bytes 589832 | tf_op jit(solution)/shard_map/ppermute | solution.py:263
  53.4 0.9 copy-start.8
  54.5 0.7 copy-start.11
  55.8 45.6 %all-to-all-start.2 = ((bf16[64,3,2,16,128]{4,3,2,1,0:T(8,128)(2,1)}), bf16[64,3,2,16,128]{4,3,2,1,0:T(8,128)(2,1)S(1)}, u32[]{:S(2)}, u32[]{:S(2)}) async-start(bf16[64,3,2,16,128]{4,3,2,1,0:T(8,128)(2,1)} %shard_map.85), calls=%async_computation.2 | async-start | bytes 3145728 | tf_op jit(solution)/shard_map/all_to_all | solution.py:322
  76.1 21.2 %collective-permute-start.10 = (bf16[8,3,2,16,128]{4,3,2,1,0:T(8,128)(2,1)}, bf16[8,3,2,16,128]{4,3,2,1,0:T(8,128)(2,1)S(1)}, u32[]{:S(2)}, u32[]{:S(2)}) collective-permute-start(bf16[8,3,2,16,128]{4,3,2,1,0:T(8,128)(2,1)} %get-tuple-element.78), channel_id=1, source_target_pairs={{0,4},{4,8},{8,12},{12,0},{128,132},{132,136},{136,140},{140,128},... | collective-permute-start | bytes 589832 | tf_op jit(solution)/shard_map/ppermute | solution.py:269
  77.6 23.8 %collective-permute-start.11 = (bf16[8,3,2,16,128]{4,3,2,1,0:T(8,128)(2,1)}, bf16[8,3,2,16,128]{4,3,2,1,0:T(8,128)(2,1)S(1)}, u32[]{:S(2)}, u32[]{:S(2)}) collective-permute-start(bf16[8,3,2,16,128]{4,3,2,1,0:T(8,128)(2,1)} %get-tuple-element.79), channel_id=1, source_target_pairs={{0,8},{4,12},{8,0},{12,4},{128,136},{132,140},{136,128},{140,132},... | collective-permute-start | bytes 589832 | tf_op jit(solution)/shard_map/ppermute | solution.py:269
  80.3 29.3 %collective-permute-start.12 = (bf16[8,3,2,16,128]{4,3,2,1,0:T(8,128)(2,1)}, bf16[8,3,2,16,128]{4,3,2,1,0:T(8,128)(2,1)S(1)}, u32[]{:S(2)}, u32[]{:S(2)}) collective-permute-start(bf16[8,3,2,16,128]{4,3,2,1,0:T(8,128)(2,1)} %get-tuple-element.80), channel_id=1, source_target_pairs={{0,12},{4,0},{8,4},{12,8},{128,140},{132,128},{136,132},{140,136},... | collective-permute-start | bytes 589832 | tf_op jit(solution)/shard_map/ppermute | solution.py:269
  81.8 27.9 %collective-permute-start.13 = (bf16[8,3,2,16,128]{4,3,2,1,0:T(8,128)(2,1)}, bf16[8,3,2,16,128]{4,3,2,1,0:T(8,128)(2,1)S(1)}, u32[]{:S(2)}, u32[]{:S(2)}) collective-permute-start(bf16[8,3,2,16,128]{4,3,2,1,0:T(8,128)(2,1)} %get-tuple-element.81), channel_id=1, source_target_pairs={{0,128},{4,132},{8,136},{12,140},{128,0},{132,4},{136,8},{140,12},... | collective-permute-start | bytes 589832 | tf_op jit(solution)/shard_map/ppermute | solution.py:269
  83.4 26.3 %collective-permute-start.14 = (bf16[8,3,2,16,128]{4,3,2,1,0:T(8,128)(2,1)}, bf16[8,3,2,16,128]{4,3,2,1,0:T(8,128)(2,1)S(1)}, u32[]{:S(2)}, u32[]{:S(2)}) collective-permute-start(bf16[8,3,2,16,128]{4,3,2,1,0:T(8,128)(2,1)} %get-tuple-element.82), channel_id=1, source_target_pairs={{0,132},{4,136},{8,140},{12,128},{128,4},{132,8},{136,12},{140,0},... | collective-permute-start | bytes 589832 | tf_op jit(solution)/shard_map/ppermute | solution.py:269
  97.3 12.4 %copy-start.12 = (bf16[8,3,2,16,128]{4,3,2,1,0:T(8,128)(2,1)}, bf16[8,3,2,16,128]{4,3,2,1,0:T(8,128)(2,1)S(1)}, u32[]{:S(2)}) copy-start(bf16[8,3,2,16,128]{4,3,2,1,0:T(8,128)(2,1)S(1)} %collective-permute-done.10.refs_1_) | copy-start | bytes 589828
  97.3 12.4 %collective-permute-start.15 = (bf16[8,3,2,16,128]{4,3,2,1,0:T(8,128)(2,1)}, bf16[8,3,2,16,128]{4,3,2,1,0:T(8,128)(2,1)S(1)}, u32[]{:S(2)}, u32[]{:S(2)}) collective-permute-start(bf16[8,3,2,16,128]{4,3,2,1,0:T(8,128)(2,1)} %get-tuple-element.83), channel_id=1, source_target_pairs={{0,136},{4,140},{8,128},{12,132},{128,8},{132,12},{136,0},{140,4},... | collective-permute-start | bytes 589832 | tf_op jit(solution)/shard_map/ppermute | solution.py:269
  101.4 8.3 %copy-start.13 = (bf16[8,3,2,16,128]{4,3,2,1,0:T(8,128)(2,1)}, bf16[8,3,2,16,128]{4,3,2,1,0:T(8,128)(2,1)S(1)}, u32[]{:S(2)}) copy-start(bf16[8,3,2,16,128]{4,3,2,1,0:T(8,128)(2,1)S(1)} %collective-permute-done.11.refs_2_) | copy-start | bytes 589828
  101.4 8.3 %collective-permute-start.16 = (bf16[8,3,2,16,128]{4,3,2,1,0:T(8,128)(2,1)}, bf16[8,3,2,16,128]{4,3,2,1,0:T(8,128)(2,1)S(1)}, u32[]{:S(2)}, u32[]{:S(2)}) collective-permute-start(bf16[8,3,2,16,128]{4,3,2,1,0:T(8,128)(2,1)} %get-tuple-element.84), channel_id=1, source_target_pairs={{0,140},{4,128},{8,132},{12,136},{128,12},{132,0},{136,4},{140,8},... | collective-permute-start | bytes 589832 | tf_op jit(solution)/shard_map/ppermute | solution.py:269
  101.4 1.2 copy-start.3
  109.6 0.7 copy-start.14
  109.6 0.7 copy-start.15
  109.7 0.8 copy-start.16
  109.7 0.8 copy-start.17
  109.7 0.9 copy-start.18
  117.4 73.3 %copy-start = (f32[2,6,256,128]{3,2,1,0:T(8,128)S(1)}, f32[2,6,256,128]{3,2,1,0:T(8,128)}, u32[]{:S(2)}) copy-start(f32[2,6,256,128]{3,2,1,0:T(8,128)} %get-tuple-element.91.own_ref) | copy-start | bytes 4718596
